TPU v7x, 32 devices: a whole 2x2x4 slice. The times are simulated.
32 devices in a mesh: dp: 16 (over z, x, core), tensor: 2 (over y).
Axes of the slice: x: 2, y: 2, z: 4, core: 2. Of those that a mesh axis runs over, the one named last changes fastest.
Arguments:
- big_patches: bfloat16 [64, 1024, 768], P('dp'), may hold values from -6 to 6
- small_patches: bfloat16 [64, 256, 768], P('dp'), may hold values from -6 to 6
- big_visible: int32 [64, 256], P('dp'), may hold values from 0 to 1023, as said below
- small_visible: int32 [64, 64], P('dp'), may hold values from 0 to 255, as said below
- big_cot: bfloat16 [64, 256, 768], P('dp'), may hold values from -6 to 6
- small_cot: bfloat16 [64, 64, 768], P('dp'), may hold values from -6 to 6
- qkv_weight: float32 [768, 3, 768], P('dp', None, 'tensor'), may hold values from -0.21875 to 0.21875
- qkv_first: float32 [768, 3, 768], P('dp', None, 'tensor'), may hold values from -96 to 96
- qkv_second: float32 [768, 3, 768], P('dp', None, 'tensor'), may hold values from 4.096 to 163.84
- out_weight: float32 [768, 768], P('dp', 'tensor'), may hold values from -0.875 to 0.875
- out_first: float32 [768, 768], P('dp', 'tensor'), may hold values from -28 to 28
- out_second: float32 [768, 768], P('dp', 'tensor'), may hold values from 0.9216 to 14.7456
- up_weight: float32 [768, 3072], P('dp', 'tensor'), may hold values from -0.21875 to 0.21875
- up_first: float32 [768, 3072], P('dp', 'tensor'), may hold values from -24 to 24
- up_second: float32 [768, 3072], P('dp', 'tensor'), may hold values from 0.6144 to 10.24
- down_weight: float32 [768, 3072], P('dp', 'tensor'), may hold values from -0.109375 to 0.109375
- down_first: float32 [768, 3072], P('dp', 'tensor'), may hold values from -56 to 56
- down_second: float32 [768, 3072], P('dp', 'tensor'), may hold values from 3.6864 to 59.392
- up_bias: float32 [2, 1536], P('tensor', 'dp'), may hold values from -1.75 to 1.75
- up_bias_first: float32 [2, 1536], P('tensor', 'dp'), may hold values from -24 to 24
- up_bias_second: float32 [2, 1536], P('tensor', 'dp'), may hold values from 0.6144 to 10.24
- norm_vectors: float32 [6, 768], P(None, 'dp')
- norm_first: float32 [6, 768], P(None, 'dp'), may hold values from -64 to 64
- norm_second: float32 [6, 768], P(None, 'dp'), may hold values from 5.12 to 81.92
Outputs:
- big_out: bfloat16 [64, 256, 768], P('dp')
- small_out: bfloat16 [64, 64, 768], P('dp')
- big_grad: float32 [64, 1024, 768], P('dp')
- small_grad: float32 [64, 256, 768], P('dp')
- qkv_weight_new: float32 [768, 3, 768], P('dp', None, 'tensor')
- qkv_first_new: float32 [768, 3, 768], P('dp', None, 'tensor')
- qkv_second_new: float32 [768, 3, 768], P('dp', None, 'tensor')
- out_weight_new: float32 [768, 768], P('dp', 'tensor')
- out_first_new: float32 [768, 768], P('dp', 'tensor')
- out_second_new: float32 [768, 768], P('dp', 'tensor')
- up_weight_new: float32 [768, 3072], P('dp', 'tensor')
- up_first_new: float32 [768, 3072], P('dp', 'tensor')
- up_second_new: float32 [768, 3072], P('dp', 'tensor')
- down_weight_new: float32 [768, 3072], P('dp', 'tensor')
- down_first_new: float32 [768, 3072], P('dp', 'tensor')
- down_second_new: float32 [768, 3072], P('dp', 'tensor')
- up_bias_new: float32 [2, 1536], P('tensor', 'dp')
- up_bias_first_new: float32 [2, 1536], P('tensor', 'dp')
- up_bias_second_new: float32 [2, 1536], P('tensor', 'dp')
- norm_vectors_new: float32 [6, 768], P(None, 'dp')
- norm_first_new: float32 [6, 768], P(None, 'dp')
- norm_second_new: float32 [6, 768], P(None, 'dp')
Inputs may be any that keep to these rules, and one draw needn't show every extreme that they name: `big_visible`: each row lists 256 different patch positions of its chip, in no particular order. `small_visible`: each row lists 64 different patch positions of its chip, in no particular order.
All inputs are finite; a program needn't handle non-finite values.
Results may differ from a plain program's by a relative error of at most 0.015.
Values may be sent and summed in bfloat16 or wider, within the bound.
A program may use at most 192 MiB of HBM per device.

v0:
```python
import jax
import jax.numpy as jnp
from jax import lax
from jax.sharding import PartitionSpec as P

HD = 64
STEP_NUMBER = 10


LEARN_RATES = (0.03, 0.1, 0.03, 0.015, 0.2, 0.2)
DECAYS = (0.05, 0.05, 0.05, 0.05, 0.0, 0.0)


def layer_norm(row_data, norm_gain, norm_shift):
    centred = row_data - jnp.mean(row_data, axis=-1, keepdims=True)
    spread = jnp.mean(centred * centred, axis=-1, keepdims=True)
    return centred * lax.rsqrt(spread + 1e-05) * norm_gain + norm_shift


def gelu_exact(values):
    return jax.nn.gelu(values, approximate=False)


def pick_rows(row_data, places):
    return row_data[places]


def scatter_rows(places, row_values, length):

    def one_chip(index_row, value_rows):
        return jnp.zeros((length, value_rows.shape[-1]), jnp.float32).at[index_row].set(value_rows)

    return jax.vmap(one_chip)(places, row_values)


def attend(qkv_rows):
    chips, length, feature_width = (qkv_rows.shape[0], qkv_rows.shape[1], qkv_rows.shape[3])
    pieces = qkv_rows.reshape(chips, length, 3, feature_width // HD, HD)
    raw_scores = jnp.einsum(
        "bqhd,bkhd->bhqk", pieces[:, :, 0], pieces[:, :, 1], preferred_element_type=jnp.float32
    ) * HD ** (-0.5)
    attn_prob = jax.nn.softmax(raw_scores, axis=-1)
    prob_low = attn_prob.astype(jnp.bfloat16)
    mixture = jnp.einsum(
        "bhqk,bkhd->bqhd", prob_low, pieces[:, :, 2], preferred_element_type=jnp.float32
    )
    return (mixture.reshape(chips * length, feature_width), attn_prob, prob_low)


def attend_back(qkv_rows, attn_prob, prob_low, back_heads):
    chips, length, feature_width = (qkv_rows.shape[0], qkv_rows.shape[1], qkv_rows.shape[3])
    pieces = qkv_rows.reshape(chips, length, 3, feature_width // HD, HD)
    grad_rows = back_heads.reshape(chips, length, feature_width // HD, HD)
    back_prob = jnp.einsum(
        "bqhd,bkhd->bhqk", grad_rows, pieces[:, :, 2], preferred_element_type=jnp.float32
    )
    back_value = jnp.einsum(
        "bhqk,bqhd->bkhd", prob_low, grad_rows, preferred_element_type=jnp.float32
    )
    back_scores = attn_prob * (back_prob - jnp.sum(attn_prob * back_prob, axis=-1, keepdims=True))
    scores_low = back_scores.astype(jnp.bfloat16)
    back_query = jnp.einsum(
        "bhqk,bkhd->bqhd", scores_low, pieces[:, :, 1], preferred_element_type=jnp.float32
    ) * HD ** (-0.5)
    back_key = jnp.einsum(
        "bhqk,bqhd->bkhd", scores_low, pieces[:, :, 0], preferred_element_type=jnp.float32
    ) * HD ** (-0.5)
    stacked = jnp.stack([back_query, back_key, back_value], axis=2)
    return stacked.reshape(chips * length, 3, feature_width).astype(jnp.bfloat16)


def front_half(rows_in, gathered, big_count, big_len, small_count, small_len):
    vectors = gathered[5].astype(jnp.float32)
    normed_one = layer_norm(rows_in, vectors[0], vectors[1]).astype(jnp.bfloat16)
    feature_width = gathered[0].shape[2]
    qkv_rows = jnp.einsum(
        "td,dcj->tcj", normed_one, gathered[0], preferred_element_type=jnp.float32
    ).astype(jnp.bfloat16)
    cut_at = big_count * big_len
    heads_big, prob_big, low_big = attend(
        qkv_rows[:cut_at].reshape(big_count, big_len, 3, feature_width)
    )
    heads_small, prob_small, low_small = attend(
        qkv_rows[cut_at:].reshape(small_count, small_len, 3, feature_width)
    )
    heads_low = jnp.concatenate([heads_big, heads_small], axis=0).astype(jnp.bfloat16)
    return (normed_one, qkv_rows, (prob_big, low_big, prob_small, low_small), heads_low)


def mlp_front(normed_two, gathered):
    pre_act = jnp.dot(normed_two, gathered[2], preferred_element_type=jnp.float32) + gathered[
        4
    ].astype(jnp.float32).reshape(-1)
    activated = gelu_exact(pre_act).astype(jnp.bfloat16)
    return (pre_act, activated)


def back_half(middle, gathered):
    vectors = gathered[5].astype(jnp.float32)
    normed_two = layer_norm(middle, vectors[2], vectors[3]).astype(jnp.bfloat16)
    pre_act, activated = mlp_front(normed_two, gathered)
    return (normed_two, pre_act, activated)


def adam_step(weight, moment_one, moment_two, gradient, step_rate, decay_rate):
    moment_one = 0.9 * moment_one + 0.1 * gradient
    moment_two = 0.999 * moment_two + 0.001 * gradient * gradient
    fixed_one = moment_one / (1.0 - 0.9**STEP_NUMBER)
    fixed_two = moment_two / (1.0 - 0.999**STEP_NUMBER)
    update = fixed_one / (jnp.sqrt(fixed_two) + 1e-08) + decay_rate * weight
    return (weight - step_rate * update, moment_one, moment_two)


def on_device(
    big_patches,
    small_patches,
    big_visible,
    small_visible,
    big_cot,
    small_cot,
    qkv_weight,
    qkv_first,
    qkv_second,
    out_weight,
    out_first,
    out_second,
    up_weight,
    up_first,
    up_second,
    down_weight,
    down_first,
    down_second,
    up_bias,
    up_bias_first,
    up_bias_second,
    norm_vectors,
    norm_first,
    norm_second,
):
    gathered = (
        lax.all_gather(qkv_weight.astype(jnp.bfloat16), "dp", axis=0, tiled=True),
        lax.all_gather(out_weight.astype(jnp.bfloat16), "dp", axis=0, tiled=True),
        lax.all_gather(up_weight.astype(jnp.bfloat16), "dp", axis=0, tiled=True),
        lax.all_gather(down_weight.astype(jnp.bfloat16), "dp", axis=0, tiled=True),
        lax.all_gather(up_bias.astype(jnp.bfloat16), "dp", axis=1, tiled=True),
        lax.all_gather(norm_vectors.astype(jnp.bfloat16), "dp", axis=1, tiled=True),
    )
    big_count, big_len = big_visible.shape
    small_count, small_len = small_visible.shape
    cut_at = big_count * big_len
    big_taken = jax.vmap(pick_rows)(big_patches, big_visible)
    small_taken = jax.vmap(pick_rows)(small_patches, small_visible)
    rows_in = jnp.concatenate(
        [big_taken.reshape(cut_at, -1), small_taken.reshape(small_count * small_len, -1)], axis=0
    ).astype(jnp.float32)
    normed_one, qkv_rows, kept_prob, heads_low = front_half(
        rows_in, gathered, big_count, big_len, small_count, small_len
    )
    attn_part = jnp.einsum("ti,oi->to", heads_low, gathered[1], preferred_element_type=jnp.float32)
    vectors = gathered[5].astype(jnp.float32)
    attended = lax.psum(attn_part.astype(jnp.bfloat16), "tensor").astype(jnp.float32)
    middle = rows_in + attended + vectors[4]
    normed_two, pre_act, activated = back_half(middle, gathered)
    mlp_part = jnp.einsum("tf,of->to", activated, gathered[3], preferred_element_type=jnp.float32)
    mlp_out = lax.psum(mlp_part.astype(jnp.bfloat16), "tensor").astype(jnp.float32)
    output = (middle + mlp_out + vectors[5]).astype(jnp.bfloat16)
    gathered = (
        lax.all_gather(qkv_weight.astype(jnp.bfloat16), "dp", axis=0, tiled=True),
        lax.all_gather(out_weight.astype(jnp.bfloat16), "dp", axis=0, tiled=True),
        lax.all_gather(up_weight.astype(jnp.bfloat16), "dp", axis=0, tiled=True),
        lax.all_gather(down_weight.astype(jnp.bfloat16), "dp", axis=0, tiled=True),
        lax.all_gather(up_bias.astype(jnp.bfloat16), "dp", axis=1, tiled=True),
        lax.all_gather(norm_vectors.astype(jnp.bfloat16), "dp", axis=1, tiled=True),
    )
    vectors = gathered[5].astype(jnp.float32)
    normed_one, qkv_rows, kept_prob, heads_low = front_half(
        rows_in, gathered, big_count, big_len, small_count, small_len
    )
    middle = rows_in + attended + vectors[4]
    normed_two, pre_act, activated = back_half(middle, gathered)
    back_out = jnp.concatenate(
        [big_cot.reshape(cut_at, -1), small_cot.reshape(small_count * small_len, -1)], axis=0
    )
    back_float = back_out.astype(jnp.float32)
    grad_down = jnp.einsum("to,tf->of", back_out, activated, preferred_element_type=jnp.float32)
    back_act = jnp.dot(back_out, gathered[3], preferred_element_type=jnp.float32)
    gelu_values, gelu_pull = jax.vjp(gelu_exact, pre_act)
    back_pre = gelu_pull(back_act)[0].astype(jnp.bfloat16)
    grad_up = jnp.einsum("td,tf->df", normed_two, back_pre, preferred_element_type=jnp.float32)
    grad_up_bias = jnp.sum(back_pre.astype(jnp.float32), axis=0).reshape(1, -1)
    back_norm_part = jnp.einsum(
        "tf,df->td", back_pre, gathered[2], preferred_element_type=jnp.float32
    )
    back_norm = lax.psum(back_norm_part.astype(jnp.bfloat16), "tensor").astype(jnp.float32)
    norm_values, norm_pull = jax.vjp(layer_norm, middle, vectors[2], vectors[3])
    middle_part, grad_gain_two, grad_shift_two = norm_pull(back_norm)
    back_middle = back_float + middle_part
    norm_two_grads = jnp.stack(
        [grad_gain_two, grad_shift_two, jnp.sum(back_middle, axis=0)], axis=0
    )
    big_out = output[:cut_at].reshape(big_count, big_len, -1)
    small_out = output[cut_at:].reshape(small_count, small_len, -1)
    back_attn = back_middle.astype(jnp.bfloat16)
    grad_out = jnp.einsum("to,ti->oi", back_attn, heads_low, preferred_element_type=jnp.float32)
    back_heads = jnp.dot(back_attn, gathered[1], preferred_element_type=jnp.float32).astype(
        jnp.bfloat16
    )
    prob_big, low_big, prob_small, low_small = kept_prob
    feature_width = qkv_rows.shape[2]
    back_qkv = jnp.concatenate(
        [
            attend_back(
                qkv_rows[:cut_at].reshape(big_count, big_len, 3, feature_width),
                prob_big,
                low_big,
                back_heads[:cut_at],
            ),
            attend_back(
                qkv_rows[cut_at:].reshape(small_count, small_len, 3, feature_width),
                prob_small,
                low_small,
                back_heads[cut_at:],
            ),
        ],
        axis=0,
    )
    grad_qkv = jnp.einsum("td,tcj->dcj", normed_one, back_qkv, preferred_element_type=jnp.float32)
    back_first = lax.psum(
        jnp.einsum("tcj,dcj->td", back_qkv, gathered[0], preferred_element_type=jnp.float32).astype(
            jnp.bfloat16
        ),
        "tensor",
    ).astype(jnp.float32)
    first_values, first_pull = jax.vjp(layer_norm, rows_in, vectors[0], vectors[1])
    input_part, grad_gain_one, grad_shift_one = first_pull(back_first)
    back_in = back_middle + input_part
    grad_norm = jnp.stack(
        [
            grad_gain_one,
            grad_shift_one,
            norm_two_grads[0],
            norm_two_grads[1],
            norm_two_grads[2],
            jnp.sum(back_float, axis=0),
        ],
        axis=0,
    )
    qkv_share, out_share, up_share, down_share, bias_share, norm_share = (
        lax.psum_scatter(grad_qkv, "dp", scatter_dimension=0, tiled=True),
        lax.psum_scatter(grad_out, "dp", scatter_dimension=0, tiled=True),
        lax.psum_scatter(grad_up, "dp", scatter_dimension=0, tiled=True),
        lax.psum_scatter(grad_down, "dp", scatter_dimension=0, tiled=True),
        lax.psum_scatter(grad_up_bias, "dp", scatter_dimension=1, tiled=True),
        lax.psum_scatter(grad_norm, "dp", scatter_dimension=1, tiled=True),
    )
    big_grad = scatter_rows(
        big_visible, back_in[:cut_at].reshape(big_count, big_len, -1), big_patches.shape[1]
    )
    small_grad = scatter_rows(
        small_visible, back_in[cut_at:].reshape(small_count, small_len, -1), small_patches.shape[1]
    )
    qkv_new = adam_step(qkv_weight, qkv_first, qkv_second, qkv_share, LEARN_RATES[0], DECAYS[0])
    out_new = adam_step(out_weight, out_first, out_second, out_share, LEARN_RATES[1], DECAYS[1])
    up_new = adam_step(up_weight, up_first, up_second, up_share, LEARN_RATES[2], DECAYS[2])
    down_new = adam_step(
        down_weight, down_first, down_second, down_share, LEARN_RATES[3], DECAYS[3]
    )
    bias_new = adam_step(
        up_bias, up_bias_first, up_bias_second, bias_share, LEARN_RATES[4], DECAYS[4]
    )
    norm_new = adam_step(
        norm_vectors, norm_first, norm_second, norm_share, LEARN_RATES[5], DECAYS[5]
    )
    return (
        big_out,
        small_out,
        big_grad,
        small_grad,
        qkv_new[0],
        qkv_new[1],
        qkv_new[2],
        out_new[0],
        out_new[1],
        out_new[2],
        up_new[0],
        up_new[1],
        up_new[2],
        down_new[0],
        down_new[1],
        down_new[2],
        bias_new[0],
        bias_new[1],
        bias_new[2],
        norm_new[0],
        norm_new[1],
        norm_new[2],
    )


def solution(mesh):
    return jax.shard_map(
        on_device,
        mesh=mesh,
        in_specs=(
            P("dp", None, None),
            P("dp", None, None),
            P("dp", None),
            P("dp", None),
            P("dp", None, None),
            P("dp", None, None),
            P("dp", None, "tensor"),
            P("dp", None, "tensor"),
            P("dp", None, "tensor"),
            P("dp", "tensor"),
            P("dp", "tensor"),
            P("dp", "tensor"),
            P("dp", "tensor"),
            P("dp", "tensor"),
            P("dp", "tensor"),
            P("dp", "tensor"),
            P("dp", "tensor"),
            P("dp", "tensor"),
            P("tensor", "dp"),
            P("tensor", "dp"),
            P("tensor", "dp"),
            P(None, "dp"),
            P(None, "dp"),
            P(None, "dp"),
        ),
        out_specs=(
            P("dp", None, None),
            P("dp", None, None),
            P("dp", None, None),
            P("dp", None, None),
            P("dp", None, "tensor"),
            P("dp", None, "tensor"),
            P("dp", None, "tensor"),
            P("dp", "tensor"),
            P("dp", "tensor"),
            P("dp", "tensor"),
            P("dp", "tensor"),
            P("dp", "tensor"),
            P("dp", "tensor"),
            P("dp", "tensor"),
            P("dp", "tensor"),
            P("dp", "tensor"),
            P("tensor", "dp"),
            P("tensor", "dp"),
            P("tensor", "dp"),
            P(None, "dp"),
            P(None, "dp"),
            P(None, "dp"),
        ),
        check_vma=False,
    )
```

profile of v0, /device:TPU:0, one launch (start us, length us, event | category | flops | bytes accessed | tf_op | source)
XLA Modules:
  0.0 985.0 jit_solution(4858458133170610957)
XLA Ops:
  11.8 23.3 %all-gather = bf16[16,48,6]{1,2,0:T(8,128)(2,1)S(1)} all-gather(bf16[1,48,6]{1,2,0:T(8,128)(2,1)S(1)} %convert_bitcast_fusion), channel_id=1, replica_groups=mesh['dp'=16,'tensor'=2] {'dp'}, dimensions={0}, use_global_device_ids=true | all-gather | bytes 9792 | tf_op jit(solution)/shard_map/all_gather | solution.py:146
  38.5 15.0 %gather_fusion = bf16[1024,768]{1,0:T(8,128)(2,1)S(1)} fusion(bf16[4,1024,768]{2,1,0:T(8,128)(2,1)} %param.24, s32[1024]{0:T(1024)S(1)} %bitcast.163), kind=kCustom, calls=%fused_computation | custom fusion | bytes 3153920 | tf_op jit(solution)/shard_map/vmap()/gather | solution.py:25
  55.3 20.6 %all_gather.26 = bf16[768,384]{1,0:T(8,128)(2,1)} all-gather(bf16[48,384]{1,0:T(8,128)(2,1)S(1)} %convert_element_type.121), channel_id=1, replica_groups=mesh['dp'=16,'tensor'=2] {'dp'}, dimensions={0}, use_global_device_ids=true | all-gather | bytes 626688 | tf_op jit(solution)/shard_map/all_gather | solution.py:142
  117.7 31.6 %all-reduce = bf16[1536]{0:T(1024)(128)(2,1)S(1)} all-reduce(bf16[1536]{0:T(1024)(128)(2,1)S(1)} %dynamic-update-slice), channel_id=1, replica_groups=mesh['dp'=16,'tensor'=2] {'dp'}, use_global_device_ids=true, to_apply=%add | all-reduce | flops 1536 | bytes 6144
  149.9 23.5 %all-reduce.6.cloned.1.call-done = bf16[1280,768]{1,0:T(8,128)(2,1)} async-done(((bf16[1280,768]{1,0:T(8,128)(2,1)}), bf16[1280,768]{1,0:T(8,128)(2,1)}) %all-reduce.6.cloned.1.call-update) | async-done | bytes 1966096 | tf_op jit(solution)/shard_map/psum | solution.py:161
  179.1 39.7 %all-gather.7.cloned.1.call-done = bf16[768,1536]{1,0:T(8,128)(2,1)} async-done(((bf16[48,1536]{1,0:T(8,128)(2,1)}), bf16[768,1536]{1,0:T(8,128)(2,1)}) %all-gather.7.cloned.1.call-update) | async-done | bytes 2359312 | tf_op jit(solution)/shard_map/all_gather | solution.py:143
  218.9 25.3 %multiply_convert_fusion = (bf16[1280,1536]{1,0:T(8,128)(2,1)S(1)}, f32[1280,1536]{1,0:T(8,128)}, f32[1280,1536]{1,0:T(8,128)}) fusion(f32[1536]{0:T(1024)} %add.274, bf16[768,1536]{1,0:T(8,128)(2,1)} %all-gather.7.cloned.1.call-done, f32[768]{0:T(1024)} %get-tuple-element.31, f32[768]{0:T(1024)S(1)} %get-tuple-element.32, f32[1280]{0:T(1024)} %fusion.83, ...), kind=kOutput, calls=%fused_computation.11 | convolution fusion | flops 3161456640 | bytes 25977856 | tf_op jit(solution)/shard_map/dot_general | solution.py:91
  251.0 74.5 %reduce-scatter.17.cloned.1.call-done = f32[48,1536]{1,0:T(8,128)} async-done(((f32[768,1536]{1,0:T(8,128)}), f32[48,1536]{1,0:T(8,128)}) %reduce-scatter.17.cloned.1.call-update) | async-done | bytes 294928 | tf_op jit(solution)/shard_map/reduce_scatter | solution.py:252
  328.1 41.5 %all-gather.9.cloned.1.call-done = bf16[768,1536]{1,0:T(8,128)(2,1)} async-done(((bf16[48,1536]{1,0:T(8,128)(2,1)}), bf16[768,1536]{1,0:T(8,128)(2,1)}) %all-gather.9.cloned.1.call-update) | async-done | bytes 2359312 | tf_op jit(solution)/shard_map/all_gather | solution.py:144
  369.6 10.7 %convert_reduce_fusion = (f32[1536]{0:T(1024)}, bf16[1280,1536]{1,0:T(8,128)(2,1)S(1)}) fusion(f32[1280,1536]{1,0:T(8,128)} %get-tuple-element.59, f32[1280,1536]{1,0:T(8,128)} %get-tuple-element.76, bf16[768,1536]{1,0:T(8,128)(2,1)} %all-gather.9.cloned.1.call-done, bf16[256,768]{1,0:T(8,128)(2,1)} %bitcast.174, bf16[1024,768]{1,0:T(8,128)(2,1)} %bitcast.171), kind=kOutput, calls=%fused_computation.9 | convolution fusion | flops 3055286784 | bytes 23992320 | tf_op jit(solution)/shard_map/dot_general | solution.py:186
  387.0 7.4 convolution_convert_fusion.2
  394.4 51.2 %all-reduce.8.cloned.1.call-done = bf16[1280,768]{1,0:T(8,128)(2,1)} async-done(((bf16[1280,768]{1,0:T(8,128)(2,1)}), bf16[1280,768]{1,0:T(8,128)(2,1)}) %all-reduce.8.cloned.1.call-update) | async-done | bytes 1966096 | tf_op jit(solution)/shard_map/psum | solution.py:194
  469.1 7.3 multiply_reduce_fusion
  476.4 6.2 multiply_convert_fusion.1
  536.0 6.5 bitcast_convert_fusion
  553.5 92.2 %all-reduce.10.cloned.1.call-done = (bf16[1280,768]{1,0:T(8,128)(2,1)}, bf16[1280,768]{1,0:T(8,128)(2,1)}) async-done(((bf16[1280,768]{1,0:T(8,128)(2,1)}, bf16[1280,768]{1,0:T(8,128)(2,1)}), (bf16[1280,768]{1,0:T(8,128)(2,1)}, bf16[1280,768]{1,0:T(8,128)(2,1)})) %all-reduce.10.cloned.1.call-update) | async-done | bytes 3932176 | tf_op jit(solution)/shard_map/psum | solution.py:165
  658.3 8.1 fusion.122
  667.1 6.8 fusion.68
  677.4 28.4 %reduce-scatter.19.cloned.1.call-done = f32[96,1]{1,0:T(8,128)} async-done(((f32[1536,1]{1,0:T(8,128)}), f32[96,1]{1,0:T(8,128)}) %reduce-scatter.19.cloned.1.call-update) | async-done | bytes 400
  708.4 59.1 %reduce-scatter.13.cloned.1.call-done = f32[48,384]{1,0:T(8,128)} async-done(((f32[768,384]{1,0:T(8,128)}), f32[48,384]{1,0:T(8,128)}) %reduce-scatter.13.cloned.1.call-update) | async-done | bytes 73744 | tf_op jit(solution)/shard_map/reduce_scatter | solution.py:250
  778.2 11.4 %scatter_custom_fusion.1 = f32[4096,768]{1,0:T(8,128)} fusion(s32[1024]{0:T(1024)} %bitcast.181, f32[]{:T(128)} %constant.53.clone.1, f32[1280,768]{1,0:T(8,128)} %copy-done.10), kind=kCustom, calls=%fused_computation.25 | custom fusion | bytes 15729152
  791.6 34.2 %scatter_fusion = f32[4,256,768]{2,1,0:T(8,128)} fusion(f32[4,256,768]{2,1,0:T(8,128)} %broadcast_in_dim.23, s32[256]{0:T(256)S(1)} %reshape.215, f32[256,768]{1,0:T(8,128)S(1)} %slice.128), kind=kCustom, calls=%fused_computation.2 | custom fusion | bytes 2361344 | tf_op jit(solution)/shard_map/vmap()/scatter | solution.py:31
  827.3 77.0 %reduce-scatter.15.cloned.1.call-done = f32[48,1536]{1,0:T(8,128)} async-done(((f32[768,1536]{1,0:T(8,128)}), f32[48,1536]{1,0:T(8,128)}) %reduce-scatter.15.cloned.1.call-update) | async-done | bytes 294928 | tf_op jit(solution)/shard_map/reduce_scatter | solution.py:251
  906.3 69.3 %reduce-scatter.11.cloned.1.call-done = f32[48,3,384]{2,0,1:T(8,128)} async-done(((f32[768,3,384]{2,0,1:T(8,128)}), f32[48,3,384]{2,0,1:T(8,128)}) %reduce-scatter.11.cloned.1.call-update) | async-done | bytes 221200 | tf_op jit(solution)/shard_map/reduce_scatter | solution.py:249
  (278 shorter events, 198.4 us)
Async XLA Ops:
  7.2 68.6 %all-gather.5.cloned.1.call-start = ((), (), s32[]{:S(2)}) async-start(), calls=%async_computation.6 | async-start | bytes 1880064 | tf_op jit(solution)/shard_map/all_gather | solution.py:141
  9.0 164.4 %all-reduce.6.cloned.1.call-start = ((), (), s32[]{:S(2)}) async-start(), calls=%async_computation.7 | async-start | bytes 3932160 | tf_op jit(solution)/shard_map/psum | solution.py:161
  38.5 37.4 %copy-start.4 = (bf16[256,768]{1,0:T(8,128)(2,1)}, bf16[256,768]{1,0:T(8,128)(2,1)S(1)}, u32[]{:S(2)}) copy-start(bf16[256,768]{1,0:T(8,128)(2,1)S(1)} %gather_fusion.1) | copy-start | bytes 1179652
  54.5 400.1 %copy-start.48 = (f32[768]{0:T(1024)}, f32[768]{0:T(1024)S(1)}, u32[]{:S(2)}) copy-start(f32[768]{0:T(1024)S(1)} %get-tuple-element.32) | copy-start | bytes 9220
  111.9 38.0 %copy-start.16 = (bf16[1280,384]{0,1:T(8,128)(2,1)}, bf16[1280,384]{0,1:T(8,128)(2,1)S(1)}, u32[]{:S(2)}) copy-start(bf16[1280,384]{0,1:T(8,128)(2,1)S(1)} %constant_dynamic-update-slice_fusion) | copy-start | bytes 2949124
  114.4 104.4 %all-gather.7.cloned.1.call-start = ((), (), s32[]{:S(2)}) async-start(), calls=%async_computation.8 | async-start | bytes 2506752 | tf_op jit(solution)/shard_map/all_gather | solution.py:143
  116.2 209.3 %reduce-scatter.17.cloned.1.call-start = ((), (), s32[]{:S(2)}) async-start(), calls=%async_computation.14 | async-start | bytes 5013504 | tf_op jit(solution)/shard_map/reduce_scatter | solution.py:252
  175.8 278.8 %copy-start.37 = (f32[1280]{0:T(1024)}, f32[1280]{0:T(1024)S(1)}, u32[]{:S(2)}) copy-start(f32[1280]{0:T(1024)S(1)} %broadcast_multiply_fusion) | copy-start | bytes 15364
  251.0 118.6 %all-gather.9.cloned.1.call-start = ((), (), s32[]{:S(2)}) async-start(), calls=%async_computation.9 | async-start | bytes 2506752 | tf_op jit(solution)/shard_map/all_gather | solution.py:144
  328.1 117.6 %all-reduce.8.cloned.1.call-start = ((), (), s32[]{:S(2)}) async-start(), calls=%async_computation.10 | async-start | bytes 3932160 | tf_op jit(solution)/shard_map/psum | solution.py:194
  386.6 259.2 %all-reduce.10.cloned.1.call-start = ((), (), s32[]{:S(2)}) async-start(), calls=%async_computation.17 | async-start | bytes 7864320 | tf_op jit(solution)/shard_map/psum | solution.py:165
  542.5 163.3 %reduce-scatter.19.cloned.1.call-start = ((), (), s32[]{:S(2)}) async-start(), calls=%async_computation.15 | async-start | bytes 835584
  544.4 101.4 %copy-start.36 = (f32[1280]{0:T(1024)S(1)}, f32[1280]{0:T(1024)}, u32[]{:S(2)}) copy-start(f32[1280]{0:T(1024)} %copy-done.35) | copy-start | bytes 15364
  544.4 223.1 %reduce-scatter.13.cloned.1.call-start = ((), (), s32[]{:S(2)}) async-start(), calls=%async_computation.12 | async-start | bytes 1253376 | tf_op jit(solution)/shard_map/reduce_scatter | solution.py:250
  549.1 276.7 %reduce-scatter.21.cloned.1.call-start = ((), (), s32[]{:S(2)}) async-start(), calls=%async_computation.16 | async-start | bytes 417792
  658.2 246.1 %reduce-scatter.15.cloned.1.call-start = ((), (), s32[]{:S(2)}) async-start(), calls=%async_computation.13 | async-start | bytes 5013504 | tf_op jit(solution)/shard_map/reduce_scatter | solution.py:251
  666.4 309.2 %reduce-scatter.11.cloned.1.call-start = ((), (), s32[]{:S(2)}) async-start(), calls=%async_computation.11 | async-start | bytes 3760128 | tf_op jit(solution)/shard_map/reduce_scatter | solution.py:249
  791.6 35.1 %copy-start.56 = (f32[6,48]{1,0:T(8,128)S(1)}, f32[6,48]{1,0:T(8,128)}, u32[]{:S(2)}) copy-start(f32[6,48]{1,0:T(8,128)} %param.46) | copy-start | bytes 3460
  791.6 35.1 %copy-start.57 = (f32[6,48]{1,0:T(8,128)S(1)}, f32[6,48]{1,0:T(8,128)}, u32[]{:S(2)}) copy-start(f32[6,48]{1,0:T(8,128)} %param.47) | copy-start | bytes 3460
  791.6 112.8 %copy-start.25 = (f32[48,1536]{1,0:T(8,128)S(1)}, f32[48,1536]{1,0:T(8,128)}, u32[]{:S(2)}) copy-start(f32[48,1536]{1,0:T(8,128)} %param.36) | copy-start | bytes 884740
  791.6 112.8 %copy-start.33 = (f32[48,1536]{1,0:T(8,128)S(1)}, f32[48,1536]{1,0:T(8,128)}, u32[]{:S(2)}) copy-start(f32[48,1536]{1,0:T(8,128)} %param.37) | copy-start | bytes 884740
  791.6 112.8 %copy-start.34 = (f32[48,1536]{1,0:T(8,128)S(1)}, f32[48,1536]{1,0:T(8,128)}, u32[]{:S(2)}) copy-start(f32[48,1536]{1,0:T(8,128)} %param.38) | copy-start | bytes 884740
  791.6 184.1 %copy-start.26 = (f32[48,3,384]{2,0,1:T(8,128)S(1)}, f32[48,3,384]{2,0,1:T(8,128)}, u32[]{:S(2)}) copy-start(f32[48,3,384]{2,0,1:T(8,128)} %param.30) | copy-start | bytes 663556
  791.6 186.1 %copy-start.1 = (bf16[4,256,768]{2,1,0:T(8,128)(2,1)S(1)}, bf16[4,256,768]{2,1,0:T(8,128)(2,1)}, u32[]{:S(2)}) copy-start(bf16[4,256,768]{2,1,0:T(8,128)(2,1)} %param.25) | copy-start | bytes 4718596
  (54 other events, 425.1 us)
Sparse Core Ops, SparseCore 0:
  10.9 43.1 all-gather.4
  114.6 58.7 all-reduce.5
  176.5 42.3 all-gather.6
  251.1 74.3 reduce-scatter.16
  328.2 41.3 all-gather.8
  386.7 58.8 all-reduce.7
  542.6 103.0 all-reduce.9
  649.3 56.4 reduce-scatter.18
  710.5 57.0 reduce-scatter.12
  771.3 54.5 reduce-scatter.20
  829.7 74.5 reduce-scatter.14
  908.5 67.0 reduce-scatter.10
where the time goes:
time: 993 us; the launch traced here: 985 us
  waiting for transfers between devices  557 us (56%)
  local copies, waits for them, and re-layouts  159 us (16%)
  matrix products  111 us (11%)
  blocking collectives  75.4 us (8%)
  other arithmetic  65.7 us (7%)
  between operations  16 us (2%)
    psum x1, waiting for transfers between devices, on_device(): lax.psum(mlp_part.astype(jnp.bfloat16), 'tensor').astype(jnp.float32)  92.2 us
    reduce_scatter x1, waiting for transfers between devices, on_device(): lax.psum_scatter(grad_up, 'dp', scatter_dimension=0, tiled=True)  77 us
    reduce_scatter x1, waiting for transfers between devices, on_device(): lax.psum_scatter(grad_down, 'dp', scatter_dimension=0, tiled=True)  74.5 us
    reduce_scatter x1, waiting for transfers between devices, on_device(): lax.psum_scatter(grad_qkv, 'dp', scatter_dimension=0, tiled=True)  69.3 us
    reduce_scatter x1, waiting for transfers between devices, on_device(): lax.psum_scatter(grad_out, 'dp', scatter_dimension=0, tiled=True)  59.1 us
    psum x1, waiting for transfers between devices, on_device(): lax.psum(back_norm_part.astype(jnp.bfloat16), 'tensor').astype(jnp.float32)  51.2 us
    all_gather x1, waiting for transfers between devices, on_device(): lax.all_gather(down_weight.astype(jnp.bfloat16), 'dp', axis=0, tiled=True)  41.5 us
    all_gather x1, waiting for transfers between devices, on_device(): lax.all_gather(up_weight.astype(jnp.bfloat16), 'dp', axis=0, tiled=True)  39.7 us
  transfers between devices with their start and end apart: 12, of which 11 were waited for; matrix products, arithmetic and copies ran while one was open for 15% of the time, Pallas kernels for 0%

commit v1 on v0

v1 whole, which is shorter than its diff:
```python
import functools

import jax
import jax.numpy as jnp
from jax import lax
from jax.experimental import pallas as pl
from jax.experimental.pallas import tpu as pltpu
from jax.sharding import PartitionSpec as P

HD = 64
STEP_NUMBER = 10
BF, F32 = jnp.bfloat16, jnp.float32
MESH = pl.DeviceIdType.MESH
MIB = 2**20

LEARN_RATES = (0.03, 0.1, 0.03, 0.015, 0.2, 0.2)
DECAYS = (0.05, 0.05, 0.05, 0.05, 0.0, 0.0)

Z1, Z2, X, Y = 1, 2, 4, 8
DIMS = (Z1, Z2, X, Y)
ORDERS = ((Z1, Z2, X, Y), (Z1, Z2, Y, X))


def place(code, other_core=False):
    d, t = lax.axis_index("dp"), lax.axis_index("tensor")
    z, x, c = d // 4, (d // 2) % 2, d % 2
    if code & Z1:
        z = z + 1 - 2 * (z % 2)
    if code & Z2:
        z = z + 2 - 4 * (z // 2)
    if code & X:
        x = 1 - x
    if code & Y:
        t = 1 - t
    if other_core:
        c = 1 - c
    return z * 4 + x * 2 + c, t


def greet():
    barrier = pltpu.get_barrier_semaphore()
    for dim in DIMS:
        pl.semaphore_signal(barrier, inc=1, device_id=place(dim), device_id_type=MESH)
    pl.semaphore_signal(barrier, inc=1, device_id=place(0, True), device_id_type=MESH)
    pl.semaphore_wait(barrier, 5)


def bits(code):
    return bin(code).count("1")


def top_of(order, code):
    return max([order.index(k) for k in DIMS if code & k], default=-1)


def halves(cols):
    half = cols // 256 * 128
    return (pl.ds(0, half), pl.ds(half, cols - half))


def gather_kernel(p_ref, w_ref, send, recv, csend, crecv, own):
    groups, _, cols = p_ref.shape
    parts = tuple(zip(ORDERS, halves(cols)))
    greet()
    d, t = place(0)
    started = []

    def put(g, part, code, dim):
        pd, pt = place(code)
        span = parts[part][1]
        source = p_ref.at[g, :, span] if code == 0 else w_ref.at[g, pt, pd, :, span]
        move = pltpu.make_async_remote_copy(
            source,
            w_ref.at[g, pt, pd, :, span],
            send.at[g, part, DIMS.index(dim), code],
            recv.at[g, part, code ^ dim],
            device_id=place(dim),
            device_id_type=MESH,
        )
        move.start()
        started.append(move)

    def core_move(g, part, code, mine):
        pd, pt = place(code, not mine)
        span = parts[part][1]
        target = w_ref.at[g, pt, pd, :, span]
        source = p_ref.at[g, :, span] if code == 0 and mine else target
        return pltpu.make_async_remote_copy(
            source,
            target,
            csend.at[g, part, code],
            crecv.at[g, part, code],
            device_id=place(0, True),
            device_id_type=MESH,
        )

    def forward(g, part, code):
        order = parts[part][0]
        for dim in order[top_of(order, code) + 1 :]:
            put(g, part, code, dim)
        move = core_move(g, part, code, True)
        move.start()
        started.append(move)

    local = pltpu.make_async_copy(p_ref, w_ref.at[:, t, d], own)
    local.start()
    for g in range(groups):
        for part in range(2):
            forward(g, part, 0)
        for code in sorted(range(1, 16), key=bits):
            for part in range(2):
                order, span = parts[part]
                dim = order[top_of(order, code)]
                pd, pt = place(code)
                ref = w_ref.at[g, pt, pd, :, span]
                pltpu.make_async_remote_copy(
                    ref,
                    ref,
                    send.at[g, part, DIMS.index(dim), code ^ dim],
                    recv.at[g, part, code],
                    device_id=place(dim),
                    device_id_type=MESH,
                ).wait_recv()
                forward(g, part, code)
    local.wait()
    for g in range(groups):
        for part in range(2):
            for code in range(16):
                core_move(g, part, code, False).wait_recv()
    for move in started:
        move.wait_send()


def gather_weights(piece):
    groups, rows, cols = piece.shape
    return pl.pallas_call(
        gather_kernel,
        out_shape=jax.ShapeDtypeStruct((groups, 2, 16, rows, cols), piece.dtype),
        in_specs=[pl.BlockSpec(memory_space=pl.ANY)],
        out_specs=pl.BlockSpec(memory_space=pl.ANY),
        scratch_shapes=[
            pltpu.SemaphoreType.DMA((groups, 2, 4, 16)),
            pltpu.SemaphoreType.DMA((groups, 2, 16)),
            pltpu.SemaphoreType.DMA((groups, 2, 16)),
            pltpu.SemaphoreType.DMA((groups, 2, 16)),
            pltpu.SemaphoreType.DMA,
        ],
        compiler_params=pltpu.CompilerParams(collective_id=0, has_side_effects=True),
        name="gather_weights",
    )(piece)


def reduce_kernel(
    g_ref, rows_ref, out_ref, both_ref, total, from_core, from_chip, load, csend, crecv, send, recv, rsend, rrecv, own
):
    groups, _, _, rows, cols = g_ref.shape
    parts = tuple(zip(ORDERS, halves(cols)))
    slots = []
    for order in ORDERS:
        names = {}
        for at, dim in enumerate(order):
            for code in range(16):
                if top_of(order, code) < at:
                    names[code, dim] = len(names)
        slots.append(names)
    loads = [pltpu.make_async_copy(g_ref.at[g], total.at[g], load.at[g]) for g in range(groups)]
    for copy in loads:
        copy.start()
    greet()
    t = lax.axis_index("tensor")
    started = []
    swap = pltpu.make_async_remote_copy(
        rows_ref, both_ref.at[t], rsend, rrecv, device_id=place(Y), device_id_type=MESH
    )
    swap.start()
    local = pltpu.make_async_copy(rows_ref, both_ref.at[t], own)
    local.start()

    def core_move(g, code):
        pd, pt = place(code, True)
        return pltpu.make_async_remote_copy(
            total.at[g, pt, pd],
            from_core.at[g, code],
            csend.at[g, code],
            crecv.at[g, code],
            device_id=place(0, True),
            device_id_type=MESH,
        )

    def chip_move(g, part, code, dim, sending):
        pd, pt = place(code)
        span = parts[part][1]
        there = code ^ dim if sending else code
        slot = slots[part][there, dim]
        return pltpu.make_async_remote_copy(
            total.at[g, pt, pd, :, span],
            from_chip.at[g, slot, :, span],
            send.at[g, part, slot],
            recv.at[g, part, slot],
            device_id=place(dim),
            device_id_type=MESH,
        )

    codes = sorted(range(16), key=lambda code: -bits(code))
    for g in range(groups):
        loads[g].wait()
        for code in codes:
            move = core_move(g, code)
            move.start()
            started.append(move)
    for g in range(groups):
        for code in codes:
            pd, pt = place(code)
            core_move(g, code).wait_recv()
            for part in range(2):
                order, span = parts[part]
                value = total[g, pt, pd, :, span].astype(F32) + from_core[g, code, :, span].astype(F32)
                at = top_of(order, code)
                for dim in reversed(order[at + 1 :]):
                    chip_move(g, part, code, dim, False).wait_recv()
                    value = value + from_chip[g, slots[part][code, dim], :, span].astype(F32)
                if code == 0:
                    out_ref[g, :, span] = value
                else:
                    total[g, pt, pd, :, span] = value.astype(BF)
                    move = chip_move(g, part, code, order[at], True)
                    move.start()
                    started.append(move)
    local.wait()
    swap.wait_recv()
    swap.wait_send()
    for move in started:
        move.wait_send()


def reduce_grads(grads, rows_pair):
    groups, _, _, rows, cols = grads.shape
    return pl.pallas_call(
        reduce_kernel,
        out_shape=(
            jax.ShapeDtypeStruct((groups, rows, cols), F32),
            jax.ShapeDtypeStruct((2,) + rows_pair.shape, BF),
        ),
        in_specs=[pl.BlockSpec(memory_space=pl.ANY)] * 2,
        out_specs=(pl.BlockSpec(memory_space=pltpu.VMEM), pl.BlockSpec(memory_space=pl.ANY)),
        scratch_shapes=[
            pltpu.VMEM(grads.shape, BF),
            pltpu.VMEM((groups, 16, rows, cols), BF),
            pltpu.VMEM((groups, 15, rows, cols), BF),
            pltpu.SemaphoreType.DMA((groups,)),
            pltpu.SemaphoreType.DMA((groups, 16)),
            pltpu.SemaphoreType.DMA((groups, 16)),
            pltpu.SemaphoreType.DMA((groups, 2, 15)),
            pltpu.SemaphoreType.DMA((groups, 2, 15)),
            pltpu.SemaphoreType.DMA,
            pltpu.SemaphoreType.DMA,
            pltpu.SemaphoreType.DMA,
        ],
        compiler_params=pltpu.CompilerParams(
            collective_id=1, has_side_effects=True, vmem_limit_bytes=56 * MIB
        ),
        name="reduce_grads",
    )(grads, rows_pair)


def dot(a, b):
    return jnp.dot(a, b, preferred_element_type=F32)


def dot_nt(a, b):
    return lax.dot_general(a, b, (((1,), (1,)), ((), ())), preferred_element_type=F32)


def normed(v):
    centred = v - jnp.mean(v, axis=-1, keepdims=True)
    r = lax.rsqrt(jnp.mean(centred * centred, axis=-1, keepdims=True) + 1e-05)
    return centred * r, r


def norm_back(e, xhat, r, gain):
    eg = e * gain
    return r * (eg - jnp.mean(eg, axis=-1, keepdims=True) - xhat * jnp.mean(eg * xhat, axis=-1, keepdims=True))


def column_of(row):
    wide = jnp.broadcast_to(row.astype(F32), (128, row.shape[1]))
    return jnp.transpose(wide).astype(jnp.int32)


def layer_kernel(
    shape,
    big_ref, small_ref, bvis_ref, svis_ref, bcot_ref, scot_ref, w_ref, vec_ref, bias_ref,
    out_ref, back_ref, g_ref, vgrad_ref, bgrad_ref,
    w, patch, patch_small, x, n1, n1t, qkv, prob, prob_small, heads, mid, n2, n2t, act, slope, cot, cott, dqkv, acc,
    w_sem, p_sem, c_sem, g_sem,
):
    nb, bl, ns, sl, wide = shape
    cut = nb * bl
    tokens = cut + ns * sl
    half = 768 // 2
    pairs = half // 128
    t = lax.axis_index("tensor")
    block = 128
    steps = tokens // block

    loads = [[pltpu.make_async_copy(w_ref.at[g, k], w.at[g, k], w_sem.at[g, k]) for k in range(2)] for g in range(3)]
    ploads = [pltpu.make_async_copy(big_ref.at[t * nb + i], patch.at[i], p_sem.at[i]) for i in range(nb)]
    ploads += [pltpu.make_async_copy(small_ref.at[t * ns + i], patch_small.at[i], p_sem.at[nb + i]) for i in range(ns)]
    cloads = [
        pltpu.make_async_copy(bcot_ref.at[t * nb + i], cot.at[pl.ds(i * bl, bl)], c_sem.at[i]) for i in range(nb)
    ]
    cloads += [
        pltpu.make_async_copy(scot_ref.at[t * ns + i], cot.at[pl.ds(cut + i * sl, sl)], c_sem.at[nb + i])
        for i in range(ns)
    ]
    for copy in ploads + loads[0] + cloads + loads[1] + loads[2]:
        copy.start()

    def pick(vis_ref, row, source, length):
        column = column_of(vis_ref[row])
        lane = lax.broadcasted_iota(jnp.int32, column.shape, 1)
        hot = jnp.concatenate([(column == lane + k * 128).astype(BF) for k in range(length // 128)], axis=1)
        return dot(hot, source).astype(BF)

    for i in range(nb):
        ploads[i].wait()
        x[pl.ds(i * bl, bl), :] = pick(bvis_ref, t * nb + i, patch[i], patch.shape[1])
    for i in range(ns):
        ploads[nb + i].wait()
        x[pl.ds(cut + i * sl, sl), :] = pick(svis_ref, t * ns + i, patch_small[i], patch_small.shape[1])

    def vec(i):
        return vec_ref[i : i + 1, :]

    def rows_of(i):
        return pl.ds(pl.multiple_of(i * block, block), block)

    @pl.loop(0, steps)
    def _(i):
        xhat, r = normed(x[rows_of(i), :].astype(F32))
        value = xhat * vec(0) + vec(1)
        n1[rows_of(i), :] = value.astype(BF)
        n1t[:, rows_of(i)] = jnp.transpose(value).astype(BF)

    for copy in loads[0]:
        copy.wait()

    @pl.loop(0, 6)
    def _(i):
        k, c = i // 3, i % 3
        span = pl.ds(pl.multiple_of(c * half, half), half)
        qkv[k, :, span] = dot(n1[...], w[0, k, :, span]).astype(BF)

    lane = lax.broadcasted_iota(jnp.int32, (1, 128), 1)
    first = lane < HD

    def softmax(scores):
        e = jnp.exp(scores - jnp.max(scores, axis=-1, keepdims=True))
        return e / jnp.sum(e, axis=-1, keepdims=True)

    small_rows = ns * sl
    same = (
        lax.broadcasted_iota(jnp.int32, (small_rows, small_rows), 0) // sl
        == lax.broadcasted_iota(jnp.int32, (small_rows, small_rows), 1) // sl
    )
    spans = [(i, pl.ds(i * bl, bl)) for i in range(nb)] + [(nb, pl.ds(cut, small_rows))]

    def pair_spans(pair):
        k, j = pair // pairs, pair % pairs
        return k, [pl.ds(pl.multiple_of(c * half + j * 128, 128), 128) for c in range(3)]

    zero = jnp.zeros((), BF)

    @pl.loop(0, 2 * pairs)
    def _(pair):
        k, lanes = pair_spans(pair)
        for i, rows in spans:
            q, key, value = (qkv[k, rows, lanes[c]] for c in range(3))
            mixed = []
            for h in range(2):
                q_head = jnp.where(first if h == 0 else ~first, q, zero)
                scores = dot_nt(q_head, key) * HD ** (-0.5)
                if i == nb:
                    scores = jnp.where(same, scores, -jnp.inf)
                p = softmax(scores).astype(BF)
                if i == nb:
                    prob_small[pair, h] = p
                else:
                    prob[pair, i, h] = p
                mixed.append(dot(p, value))
            heads[rows, pl.ds(pl.multiple_of(pair * 128, 128), 128)] = jnp.where(first, mixed[0], mixed[1]).astype(BF)

    @pl.loop(0, 3)
    def _(i):
        span = pl.ds(pl.multiple_of(i * 256, 256), 256)
        mid[:, span] = dot_nt(heads[:, :half], w[0, 0, span, pl.ds(1152, half)]) + dot_nt(
            heads[:, half:], w[0, 1, span, pl.ds(1152, half)]
        )

    @pl.loop(0, steps)
    def _(i):
        middle = x[rows_of(i), :].astype(F32) + mid[rows_of(i), :] + vec(4)
        mid[rows_of(i), :] = middle
        xhat, r = normed(middle)
        value = xhat * vec(2) + vec(3)
        n2[rows_of(i), :] = value.astype(BF)
        n2t[:, rows_of(i)] = jnp.transpose(value).astype(BF)
        acc[rows_of(i), :] = middle + vec(5)

    for copy in loads[1]:
        copy.wait()
    tiles = 2 * (wide // 256)

    def tile_of(i):
        return i // (tiles // 2), pl.ds(pl.multiple_of((i % (tiles // 2)) * 256, 256), 256)

    @pl.loop(0, tiles)
    def _(i):
        k, span = tile_of(i)
        acc_pre = dot(n2[...], w[1, k, :, span]) + bias_ref[i]
        cdf = 0.5 * (1.0 + lax.erf(acc_pre * 0.7071067811865476))
        act[i] = (acc_pre * cdf).astype(BF)
        slope[i] = (cdf + acc_pre * jnp.exp(-0.5 * acc_pre * acc_pre) * 0.3989422804014327).astype(BF)

    for copy in loads[2]:
        copy.wait()

    @pl.loop(0, tiles)
    def _(i):
        k, span = tile_of(i)
        acc[...] += dot_nt(act[i], w[2, k, :, span])

    out_ref[...] = acc[...].astype(BF)

    for copy in cloads:
        copy.wait()

    @pl.loop(0, steps)
    def _(i):
        value = cot[rows_of(i), :].astype(F32)
        cott[:, rows_of(i)] = jnp.transpose(value).astype(BF)

    acc[...] = jnp.zeros_like(acc)

    @pl.loop(0, tiles)
    def _(i):
        k, span = tile_of(i)
        back = (slope[i].astype(F32) * dot(cot[...], w[2, k, :, span])).astype(BF)
        bgrad_ref[i] = jnp.sum(back.astype(F32), axis=0, keepdims=True)
        w[2, k, :, span] = dot(cott[...], act[i]).astype(BF)
        acc[...] += dot_nt(back, w[1, k, :, span])
        w[1, k, :, span] = dot(n2t[...], back).astype(BF)

    saves = [
        [pltpu.make_async_copy(w.at[g, k], g_ref.at[g, k], g_sem.at[g, k]) for k in range(2)] for g in range(3)
    ]
    for copy in saves[1] + saves[2]:
        copy.start()

    back_attn, back_attn_t, back_heads = n2, n2t, x
    vgrad_ref[...] = jnp.zeros_like(vgrad_ref)

    @pl.loop(0, steps)
    def _(i):
        e = acc[rows_of(i), :]
        xhat, r = normed(mid[rows_of(i), :])
        back_out = cot[rows_of(i), :].astype(F32)
        back_middle = back_out + norm_back(e, xhat, r, vec(2))
        acc[rows_of(i), :] = back_middle
        back_attn[rows_of(i), :] = back_middle.astype(BF)
        back_attn_t[:, rows_of(i)] = jnp.transpose(back_middle).astype(BF)
        vgrad_ref[2:3, :] += jnp.sum(e * xhat, axis=0, keepdims=True)
        vgrad_ref[3:4, :] += jnp.sum(e, axis=0, keepdims=True)
        vgrad_ref[4:5, :] += jnp.sum(back_middle, axis=0, keepdims=True)
        vgrad_ref[5:6, :] += jnp.sum(back_out, axis=0, keepdims=True)

    dheads = cot
    for k in range(2):
        span = pl.ds(1152, half)
        dheads[:, pl.ds(k * half, half)] = dot(back_attn[...], w[0, k, :, span]).astype(BF)
        w[0, k, :, span] = dot(back_attn_t[...], heads[:, pl.ds(k * half, half)]).astype(BF)

    @pl.loop(0, 2 * pairs)
    def _(pair):
        k, lanes = pair_spans(pair)
        for i, rows in spans:
            q, key, value = (qkv[k, rows, lanes[c]] for c in range(3))
            dh = dheads[rows, pl.ds(pl.multiple_of(pair * 128, 128), 128)]
            dh_t = jnp.transpose(dh.astype(F32)).astype(BF)
            q_t = jnp.transpose(q.astype(F32)).astype(BF)
            dq, dk_t, dv_t = [], [], []
            for h in range(2):
                p = prob_small[pair, h] if i == nb else prob[pair, i, h]
                dh_head = jnp.where(first if h == 0 else ~first, dh, zero)
                dp = dot_nt(dh_head, value)
                pf = p.astype(F32)
                ds = (pf * (dp - jnp.sum(pf * dp, axis=-1, keepdims=True))).astype(BF)
                dq.append(dot(ds, key))
                dk_t.append(dot(q_t[h * HD : (h + 1) * HD], ds))
                dv_t.append(dot(dh_t[h * HD : (h + 1) * HD], p))
            scale = HD ** (-0.5)
            dqkv[k, rows, lanes[0]] = (jnp.where(first, dq[0], dq[1]) * scale).astype(BF)
            dqkv[k, rows, lanes[1]] = jnp.transpose(jnp.concatenate(dk_t, axis=0) * scale).astype(BF)
            dqkv[k, rows, lanes[2]] = jnp.transpose(jnp.concatenate(dv_t, axis=0)).astype(BF)

    @pl.loop(0, 3)
    def _(i):
        span = pl.ds(pl.multiple_of(i * 256, 256), 256)
        mid[:, span] = dot_nt(dqkv[0], w[0, 0, span, pl.ds(0, 1152)]) + dot_nt(
            dqkv[1], w[0, 1, span, pl.ds(0, 1152)]
        )

    @pl.loop(0, 6)
    def _(i):
        k, c = i // 3, i % 3
        span = pl.ds(pl.multiple_of(c * half, half), half)
        w[0, k, :, span] = dot(n1t[...], dqkv[k, :, span]).astype(BF)

    for copy in saves[0]:
        copy.start()

    @pl.loop(0, steps)
    def _(i):
        e = mid[rows_of(i), :]
        xhat, r = normed(x[rows_of(i), :].astype(F32))
        back_in = acc[rows_of(i), :] + norm_back(e, xhat, r, vec(0))
        back_ref[rows_of(i), :] = back_in.astype(BF)
        vgrad_ref[0:1, :] += jnp.sum(e * xhat, axis=0, keepdims=True)
        vgrad_ref[1:2, :] += jnp.sum(e, axis=0, keepdims=True)

    for copy in saves[0] + saves[1] + saves[2]:
        copy.wait()


def run_layer(big, small, bvis, svis, bcot, scot, w, vectors, bias, parts):
    nb, bl = bvis.shape[0] // parts, bvis.shape[2]
    ns, sl = svis.shape[0] // parts, svis.shape[2]
    tokens = nb * bl + ns * sl
    feat = big.shape[2]
    wide = w.shape[3]
    tiles = 2 * (wide // 256)
    pairs = feat // 128
    vm, hbm = pl.BlockSpec(memory_space=pltpu.VMEM), pl.BlockSpec(memory_space=pl.ANY)
    return pl.pallas_call(
        functools.partial(layer_kernel, (nb, bl, ns, sl, wide)),
        out_shape=(
            jax.ShapeDtypeStruct((tokens, feat), BF),
            jax.ShapeDtypeStruct((tokens, feat), BF),
            jax.ShapeDtypeStruct(w.shape, BF),
            jax.ShapeDtypeStruct((8, feat), F32),
            jax.ShapeDtypeStruct((tiles, 1, 256), F32),
        ),
        in_specs=[hbm, hbm, vm, vm, hbm, hbm, hbm, vm, vm],
        out_specs=(vm, vm, hbm, vm, vm),
        scratch_shapes=[
            pltpu.VMEM(w.shape, BF),
            pltpu.VMEM((nb,) + big.shape[1:], BF),
            pltpu.VMEM((ns,) + small.shape[1:], BF),
            pltpu.VMEM((tokens, feat), BF),
            pltpu.VMEM((tokens, feat), BF),
            pltpu.VMEM((feat, tokens), BF),
            pltpu.VMEM((2, tokens, 3 * feat // 2), BF),
            pltpu.VMEM((pairs, nb, 2, bl, bl), BF),
            pltpu.VMEM((pairs, 2, ns * sl, ns * sl), BF),
            pltpu.VMEM((tokens, feat), BF),
            pltpu.VMEM((tokens, feat), F32),
            pltpu.VMEM((tokens, feat), BF),
            pltpu.VMEM((feat, tokens), BF),
            pltpu.VMEM((tiles, tokens, 256), BF),
            pltpu.VMEM((tiles, tokens, 256), BF),
            pltpu.VMEM((tokens, feat), BF),
            pltpu.VMEM((feat, tokens), BF),
            pltpu.VMEM((2, tokens, 3 * feat // 2), BF),
            pltpu.VMEM((tokens, feat), F32),
            pltpu.SemaphoreType.DMA((3, 2)),
            pltpu.SemaphoreType.DMA((nb + ns,)),
            pltpu.SemaphoreType.DMA((nb + ns,)),
            pltpu.SemaphoreType.DMA((3, 2)),
        ],
        compiler_params=pltpu.CompilerParams(vmem_limit_bytes=60 * MIB),
        name="layer",
    )(big, small, bvis, svis, bcot, scot, w, vectors, bias)


def scatter_kernel(bvis_ref, svis_ref, brow_ref, srow_ref, big_ref, small_ref):
    def spread(vis, rows, length):
        hot = lax.broadcasted_iota(jnp.int32, (length, vis.shape[1]), 0) == vis
        return dot(hot.astype(BF), rows)

    big_ref[...] = spread(bvis_ref[...], brow_ref[...], big_ref.shape[0])
    small_ref[...] = spread(svis_ref[...], srow_ref[...], small_ref.shape[0])


def scatter_rows(bvis, svis, rows, big_len, small_len):
    parts = rows.shape[0]
    nb, _, bl = bvis.shape
    ns, _, sl = svis.shape
    feat = rows.shape[2]
    share = nb // parts
    first_small = share * bl // sl
    return pl.pallas_call(
        scatter_kernel,
        grid=(nb,),
        out_shape=(
            jax.ShapeDtypeStruct((nb, big_len, feat), F32),
            jax.ShapeDtypeStruct((ns, small_len, feat), F32),
        ),
        in_specs=[
            pl.BlockSpec((None, 1, bl), lambda i: (i, 0, 0)),
            pl.BlockSpec((None, 1, sl), lambda i: (i, 0, 0)),
            pl.BlockSpec((None, bl, feat), lambda i: (i // share, i % share, 0)),
            pl.BlockSpec((None, sl, feat), lambda i: (i // share, first_small + i % share, 0)),
        ],
        out_specs=(
            pl.BlockSpec((None, big_len, feat), lambda i: (i, 0, 0)),
            pl.BlockSpec((None, small_len, feat), lambda i: (i, 0, 0)),
        ),
        compiler_params=pltpu.CompilerParams(vmem_limit_bytes=40 * MIB),
        name="scatter_rows",
    )(bvis, svis, rows, rows)


def adam_step(weight, moment_one, moment_two, gradient, step_rate, decay_rate):
    moment_one = 0.9 * moment_one + 0.1 * gradient
    moment_two = 0.999 * moment_two + 0.001 * gradient * gradient
    fixed_one = moment_one / (1.0 - 0.9**STEP_NUMBER)
    fixed_two = moment_two / (1.0 - 0.999**STEP_NUMBER)
    update = fixed_one / (jnp.sqrt(fixed_two) + 1e-08) + decay_rate * weight
    return (weight - step_rate * update, moment_one, moment_two)


def on_device(
    special,
    big_patches, small_patches, big_visible, small_visible, big_cot, small_cot,
    qkv_weight, qkv_first, qkv_second, out_weight, out_first, out_second,
    up_weight, up_first, up_second, down_weight, down_first, down_second,
    up_bias, up_bias_first, up_bias_second, norm_vectors, norm_first, norm_second,
):
    rows, half = out_weight.shape
    wide = up_weight.shape[1]
    feat = big_patches.shape[2]
    parts = feat // half
    piece = jnp.stack(
        [
            jnp.concatenate([qkv_weight.reshape(rows, 3 * half), out_weight], axis=1).astype(BF),
            up_weight.astype(BF),
            down_weight.astype(BF),
        ]
    )
    if special:
        w = gather_weights(piece).reshape(3, parts, feat, wide)
    else:
        w = lax.all_gather(lax.all_gather(piece, "dp", axis=1, tiled=True), "tensor", axis=1)
    vectors = lax.all_gather(norm_vectors.astype(BF), "dp", axis=1, tiled=True).astype(F32)
    vectors = jnp.concatenate([vectors, jnp.zeros((2, feat), F32)], axis=0)
    bias = lax.all_gather(up_bias.astype(BF), "dp", axis=1, tiled=True)
    bias = lax.all_gather(bias, "tensor", axis=0, tiled=True).astype(F32)
    bias = bias.reshape(2 * (wide // 256), 1, 256)

    bvis, svis = big_visible[:, None, :], small_visible[:, None, :]
    out_rows, back_rows, grads, vgrad, bgrad = run_layer(
        big_patches, small_patches, bvis, svis, big_cot, small_cot, w, vectors, bias, parts
    )
    pair = jnp.stack([out_rows, back_rows])
    if special:
        share, both = reduce_grads(grads.reshape(3, parts, -1, rows, wide), pair)
    else:
        share = lax.psum_scatter(grads, "tensor", scatter_dimension=1)
        share = lax.psum_scatter(share, "dp", scatter_dimension=1, tiled=True).astype(F32)
        both = lax.all_gather(pair, "tensor", axis=0)
    vgrad = lax.psum(vgrad[:6], "tensor")
    norm_share = lax.psum_scatter(vgrad, "dp", scatter_dimension=1, tiled=True)
    bias_share = lax.psum_scatter(bgrad.reshape(parts, wide), "tensor", scatter_dimension=0, tiled=True)
    bias_share = lax.psum_scatter(bias_share, "dp", scatter_dimension=1, tiled=True)
    big_count, big_len = big_visible.shape
    small_count, small_len = small_visible.shape
    cut = big_count // parts * big_len
    big_out = both[:, 0, :cut].reshape(big_count, big_len, feat)
    small_out = both[:, 0, cut:].reshape(small_count, small_len, feat)
    big_grad, small_grad = scatter_rows(bvis, svis, both[:, 1], big_patches.shape[1], small_patches.shape[1])

    qkv_share = share[0, :, : 3 * half].reshape(rows, 3, half)
    new = []
    for at, (weight, one, two, gradient) in enumerate(
        (
            (qkv_weight, qkv_first, qkv_second, qkv_share),
            (out_weight, out_first, out_second, share[0, :, 3 * half :]),
            (up_weight, up_first, up_second, share[1]),
            (down_weight, down_first, down_second, share[2]),
            (up_bias, up_bias_first, up_bias_second, bias_share),
            (norm_vectors, norm_first, norm_second, norm_share),
        )
    ):
        new.extend(adam_step(weight, one, two, gradient, LEARN_RATES[at], DECAYS[at]))
    return (big_out, small_out, big_grad, small_grad, *new)


def solution(mesh):
    special = mesh.shape["dp"] == 16 and mesh.shape["tensor"] == 2
    chips = P("dp", None, None)
    matrix, qkv = P("dp", "tensor"), P("dp", None, "tensor")
    states = (qkv,) * 3 + (matrix,) * 9 + (P("tensor", "dp"),) * 3 + (P(None, "dp"),) * 3
    return jax.shard_map(
        functools.partial(on_device, special),
        mesh=mesh,
        in_specs=(chips, chips, P("dp", None), P("dp", None), chips, chips) + states,
        out_specs=(chips,) * 4 + states,
        check_vma=False,
    )
```

time: 993 us -> 454 us (0.46)
  waiting for transfers between devices: 557 us -> 53.9 us
  Pallas kernels: 0 us -> 295 us
  local copies, waits for them, and re-layouts: 159 us -> 12.4 us
  matrix products: 111 us -> 0 us
  other arithmetic: 65.7 us -> 15.7 us
  blocking collectives: 75.4 us -> 60.8 us
    pallas_call x0 -> x4, Pallas kernels: none -> 295 us  [the longest x1 122 us: reduce_grads(): pl.pallas_call(reduce_kernel, out_shape=(jax.ShapeDtypeStruct((groups, ro...]
    reduce_scatter x4 -> x0, waiting for transfers between devices: 280 us -> none  [the longest x1 77 us: on_device(): lax.psum_scatter(grad_up, 'dp', scatter_dimension=0, tiled=True)]
    psum x3 -> x0, waiting for transfers between devices: 167 us -> none  [the longest x1 92.2 us: on_device(): lax.psum(mlp_part.astype(jnp.bfloat16), 'tensor').astype(jnp.float32)]
    dot_general x23 -> x0, matrix products: 110 us -> none  [the longest x1 25.3 us: mlp_front(): jnp.dot(normed_two, gathered[2], preferred_element_type=jnp.float32)]
    all_gather x3 -> x0, waiting for transfers between devices: 81.2 us -> none  [the longest x1 41.5 us: on_device(): lax.all_gather(down_weight.astype(jnp.bfloat16), 'dp', axis=0, tiled=True)]
    another operation x17 -> x2, local copies, waits for them, and re-layouts: 37 us -> 0.15 us  [the longest x1 0.09 us: on_device(): qkv_share = share[0, :, :3 * half].reshape(rows, 3, half)]
    scatter x1 -> x0, local copies, waits for them, and re-layouts: 34.2 us -> none  [one_chip(): jnp.zeros((length, value_rows.shape[-1]), jnp.float32).at[index_row]]
    reduce_sum x9 -> x0, other arithmetic: 27 us -> none  [the longest x4 17.1 us: layer_norm(): return centred * lax.rsqrt(spread + 1e-05) * norm_gain + norm_shift]
  transfers between devices with their start and end apart: 12 -> 2, of which waited for: 11 -> 1; matrix products, arithmetic and copies ran while one was open for 15% -> 3% of each run, Pallas kernels for 0% -> 28%
where the time goes in v1:
time: 454 us; the launch traced here: 453 us
  Pallas kernels  295 us (65%)
  blocking collectives  60.8 us (13%)
  waiting for transfers between devices  53.9 us (12%)
  other arithmetic  15.7 us (3%)
  between operations  15 us (3%)
  local copies, waits for them, and re-layouts  12.4 us (3%)
    pallas_call x1, Pallas kernels, reduce_grads(): pl.pallas_call(reduce_kernel, out_shape=(jax.ShapeDtypeStruct((groups, ro...  122 us
    pallas_call x1, Pallas kernels, gather_weights(): pl.pallas_call(gather_kernel, out_shape=jax.ShapeDtypeStruct((groups, 2,...  84.4 us
    pallas_call x1, Pallas kernels, run_layer(): pl.pallas_call(functools.partial(layer_kernel, (nb, bl, ns, sl, wide)), o...  82.1 us
    unnamed x4, waiting for transfers between devices  53.9 us
    unnamed x2, blocking collectives  36.6 us
    all_gather x1, blocking collectives, on_device(): lax.all_gather(norm_vectors.astype(BF), 'dp', axis=1, tiled=True)  19.6 us
  transfers between devices with their start and end apart: 2, of which 1 were waited for; matrix products, arithmetic and copies ran while one was open for 3% of the time, Pallas kernels for 28%

profile of v1, /device:TPU:0, one launch (start us, length us, event | category | flops | bytes accessed | tf_op | source)
XLA Modules:
  0.0 452.9 jit_solution(3305062481453343220)
XLA Ops:
  7.2 1.0 convert.11
  8.4 0.9 convert_bitcast_fusion.2
  9.3 1.1 convert_bitcast_fusion
  10.3 0.8 pad_maximum_fusion.1.p_ref
  11.2 84.4 %gather_weights.1 = bf16[3,2,16,48,1536]{4,3,2,1,0:T(8,128)(2,1)} custom-call(bf16[3,48,1536]{2,1,0:T(8,128)(2,1)} %pad_maximum_fusion.1.p_ref), custom_call_target="tpu_custom_call" | custom-call | tf_op jit(solution)/shard_map/gather_weights/pallas_call | solution.py:136
  96.2 19.6 %all-gather = bf16[16,48,6]{1,2,0:T(8,128)(2,1)S(1)} all-gather(bf16[1,48,6]{1,2,0:T(8,128)(2,1)S(1)} %convert_bitcast_fusion.3), channel_id=1, replica_groups=mesh['dp'=16,'tensor'=2] {'dp'}, dimensions={0}, use_global_device_ids=true | all-gather | bytes 9792 | tf_op jit(solution)/shard_map/all_gather | solution.py:654
  118.0 29.8 %all-reduce.1 = bf16[1536]{0:T(1024)(128)(2,1)S(1)} all-reduce(bf16[1536]{0:T(1024)(128)(2,1)S(1)} %dynamic-update-slice), channel_id=1, replica_groups=mesh['dp'=16,'tensor'=2] {'dp'}, use_global_device_ids=true, to_apply=%add.1 | all-reduce | flops 1536 | bytes 6144
  147.9 4.6 %all-gather.1 = bf16[2,1,1536]{2,1,0:T(2,128)(2,1)S(1)} all-gather(bf16[1,1,1536]{2,1,0:T(2,128)(2,1)S(1)} %reshape.103), channel_id=1, replica_groups=mesh['dp'=16,'tensor'=2] {'tensor'}, dimensions={0}, use_global_device_ids=true | all-gather | bytes 9216 | tf_op jit(solution)/shard_map/all_gather | solution.py:657
  153.1 82.1 %layer.1 = (bf16[640,768]{1,0:T(8,128)(2,1)}, bf16[640,768]{1,0:T(8,128)(2,1)}, bf16[3,2,768,1536]{3,2,1,0:T(8,128)(2,1)}, f32[8,768]{1,0:T(8,128)}, f32[12,1,256]{2,1,0:T(1,128)}) custom-call(bf16[4,1024,768]{2,1,0:T(8,128)(2,1)} %big_ref.1, bf16[4,256,768]{2,1,0:T(8,128)(2,1)} %small_ref.1, s32[4,1,256]{2,1,0:T(1,128)} %broadcast_in_dim.7.bvis_ref, ...), custom_call_target="tpu_custom_call" | custom-call | tf_op jit(solution)/shard_map/layer/pallas_call | solution.py:544
  235.2 1.7 copy.80
  237.2 3.0 pad_maximum_fusion.rows_ref
  240.1 121.9 %reduce_grads.1 = (f32[3,48,1536]{2,1,0:T(8,128)}, bf16[2,2,640,768]{3,2,1,0:T(8,128)(2,1)}) custom-call(bf16[3,2,16,48,1536]{4,3,2,1,0:T(8,128)(2,1)} %bitcast.57, bf16[2,640,768]{2,1,0:T(8,128)(2,1)} %pad_maximum_fusion.rows_ref), custom_call_target="tpu_custom_call" | custom-call | tf_op jit(solution)/shard_map/reduce_grads/pallas_call | solution.py:238
  362.0 1.7 slice_bitcast_fusion.brow_ref.srow_ref
  363.8 1.0 slice.27
  364.9 2.1 multiply_subtract_fusion.2
  367.0 2.9 multiply_subtract_fusion
  370.0 1.6 multiply_subtract_fusion.3
  371.6 1.2 slice.24
  373.6 6.4 %scatter_rows.1 = (f32[4,1024,768]{2,1,0:T(8,128)}, f32[4,256,768]{2,1,0:T(8,128)}) custom-call(s32[4,1,256]{2,1,0:T(1,128)S(1)} %copy-done, s32[4,1,64]{2,1,0:T(1,128)S(1)} %bitcast.55, bf16[2,640,768]{2,1,0:T(8,128)(2,1)S(1)} %slice_bitcast_fusion.brow_ref.srow_ref, bf16[2,640,768]{2,1,0:T(8,128)(2,1)S(1)} %slice_bitcast_fusion.brow_ref.srow_ref), custom_call_target="tpu_custom_call" | custom-call | tf_op jit(solution)/shard_map/scatter_rows/pallas_call | solution.py:601
  380.7 0.8 copy.81
  381.5 6.7 %all-reduce.3 = (f32[2,1536]{1,0:T(2,128)S(1)}, f32[6,48]{1,0:T(8,128)S(1)}) all-reduce(f32[2,1536]{1,0:T(2,128)S(1)} %reshape.95, f32[6,48]{1,0:T(8,128)S(1)} %copy.81), channel_id=2, replica_groups=mesh['dp'=16,'tensor'=2] {'tensor'}, use_global_device_ids=true, to_apply=%region_0.0.clone | all-reduce | flops 3360 | bytes 26880
  388.9 1.2 copy.78
  390.7 53.9 %reduce-scatter.7.cloned.1.call-done = f32[96,1]{1,0:T(8,128)} async-done(((f32[1536,1]{1,0:T(8,128)}), f32[96,1]{1,0:T(8,128)}) %reduce-scatter.7.cloned.1.call-update) | async-done | bytes 400
  444.6 0.9 copy.79
  (64 shorter events, 6.7 us)
Async XLA Ops:
  7.2 373.5 %reduce-scatter.9.cloned.1.call-start = ((), (), s32[]{:S(2)}) async-start(), calls=%async_computation.3 | async-start | bytes 417792
  11.1 84.4 %copy-start.13 = (s32[4,256]{1,0:T(4,128)S(1)}, s32[4,256]{1,0:T(4,128)}, u32[]{:S(2)}) copy-start(s32[4,256]{1,0:T(4,128)} %param.26) | copy-start | bytes 12292
  11.1 85.0 %copy-start.9 = (f32[6,48]{1,0:T(8,128)S(1)}, f32[6,48]{1,0:T(8,128)}, u32[]{:S(2)}) copy-start(f32[6,48]{1,0:T(8,128)} %param.45) | copy-start | bytes 3460
  11.1 105.4 %copy-start.14 = (f32[1,96]{1,0:T(1,128)S(1)}, f32[1,96]{1,0:T(1,128)}, u32[]{:S(2)}) copy-start(f32[1,96]{1,0:T(1,128)} %param.42) | copy-start | bytes 1156
  11.1 105.4 %copy-start.18 = (u32[32]{0:T(128)S(1)}, u32[32]{0:T(128)}, u32[]{:S(2)}) copy-start(u32[32]{0:T(128)} %constant.39) | copy-start | bytes 388
  236.9 207.7 %reduce-scatter.7.cloned.1.call-start = ((), (), s32[]{:S(2)}) async-start(), calls=%async_computation.2 | async-start | bytes 835584
  362.0 2.9 copy-start.5
  362.0 5.0 %copy-start.3 = (f32[48,1536]{1,0:T(8,128)S(1)}, f32[48,1536]{1,0:T(8,128)}, u32[]{:S(2)}) copy-start(f32[48,1536]{1,0:T(8,128)} %param.39) | copy-start | bytes 884740
  362.0 5.0 %copy-start.4 = (f32[48,1536]{1,0:T(8,128)S(1)}, f32[48,1536]{1,0:T(8,128)}, u32[]{:S(2)}) copy-start(f32[48,1536]{1,0:T(8,128)} %param.36) | copy-start | bytes 884740
  364.7 5.2 %copy-start.6 = (f32[48,384]{1,0:T(8,128)S(1)}, f32[48,384]{1,0:T(8,128)}, u32[]{:S(2)}) copy-start(f32[48,384]{1,0:T(8,128)} %param.33) | copy-start | bytes 221188
  364.8 5.2 %copy-start.7 = (f32[48,384]{1,0:T(8,128)S(1)}, f32[48,384]{1,0:T(8,128)}, u32[]{:S(2)}) copy-start(f32[48,384]{1,0:T(8,128)} %param.34) | copy-start | bytes 221188
  364.8 5.2 %copy-start.8 = (f32[48,384]{1,0:T(8,128)S(1)}, f32[48,384]{1,0:T(8,128)}, u32[]{:S(2)}) copy-start(f32[48,384]{1,0:T(8,128)} %param.35) | copy-start | bytes 221188
  364.9 6.7 %copy-start.2 = (bf16[2,2,640,768]{3,2,1,0:T(8,128)(2,1)S(1)}, bf16[2,2,640,768]{3,2,1,0:T(8,128)(2,1)}, u32[]{:S(2)}) copy-start(bf16[2,2,640,768]{3,2,1,0:T(8,128)(2,1)} %get-tuple-element.34) | copy-start | bytes 11796484
  369.9 3.7 copy-start
  369.9 3.7 copy-start.1
  372.8 7.2 %copy-start.10 = (f32[12,1,256]{2,1,0:T(1,128)S(1)}, f32[12,1,256]{2,1,0:T(1,128)}, u32[]{:S(2)}) copy-start(f32[12,1,256]{2,1,0:T(1,128)} %get-tuple-element.38) | copy-start | bytes 36868
  372.8 7.3 %copy-start.17 = (u32[32]{0:T(128)S(1)}, u32[32]{0:T(128)}, u32[]{:S(2)}) copy-start(u32[32]{0:T(128)} %constant.45) | copy-start | bytes 388
  372.8 17.3 %copy-start.11 = (f32[6,48]{1,0:T(8,128)S(1)}, f32[6,48]{1,0:T(8,128)}, u32[]{:S(2)}) copy-start(f32[6,48]{1,0:T(8,128)} %param.46) | copy-start | bytes 3460
  372.8 17.3 %copy-start.12 = (f32[6,48]{1,0:T(8,128)S(1)}, f32[6,48]{1,0:T(8,128)}, u32[]{:S(2)}) copy-start(f32[6,48]{1,0:T(8,128)} %param.47) | copy-start | bytes 3460
  372.8 72.7 %copy-start.15 = (f32[1,96]{1,0:T(1,128)S(1)}, f32[1,96]{1,0:T(1,128)}, u32[]{:S(2)}) copy-start(f32[1,96]{1,0:T(1,128)} %param.43) | copy-start | bytes 1156
  372.8 72.7 %copy-start.16 = (f32[1,96]{1,0:T(1,128)S(1)}, f32[1,96]{1,0:T(1,128)}, u32[]{:S(2)}) copy-start(f32[1,96]{1,0:T(1,128)} %param.44) | copy-start | bytes 1156
Sparse Core Ops, SparseCore 0:
  237.0 54.0 reduce-scatter.8
  390.2 54.3 reduce-scatter.6

commit v2 on v1

v2 whole, which is shorter than its diff:
```python
import functools

import jax
import jax.numpy as jnp
from jax import lax
from jax.experimental import pallas as pl
from jax.experimental.pallas import tpu as pltpu
from jax.sharding import PartitionSpec as P

HD = 64
STEP_NUMBER = 10
BF, F32 = jnp.bfloat16, jnp.float32
MESH = pl.DeviceIdType.MESH
MIB = 2**20

LEARN_RATES = (0.03, 0.1, 0.03, 0.015, 0.2, 0.2)
DECAYS = (0.05, 0.05, 0.05, 0.05, 0.0, 0.0)

Z1, Z2, X, Y = 1, 2, 4, 8
DIMS = (Z1, Z2, X, Y)
ORDERS = ((Z1, Z2, X, Y), (Z1, Z2, Y, X))


def place(code, other_core=False):
    d, t = lax.axis_index("dp"), lax.axis_index("tensor")
    z, x, c = d // 4, (d // 2) % 2, d % 2
    if code & Z1:
        z = z + 1 - 2 * (z % 2)
    if code & Z2:
        z = z + 2 - 4 * (z // 2)
    if code & X:
        x = 1 - x
    if code & Y:
        t = 1 - t
    if other_core:
        c = 1 - c
    return z * 4 + x * 2 + c, t


def greet():
    barrier = pltpu.get_barrier_semaphore()
    for dim in DIMS:
        pl.semaphore_signal(barrier, inc=1, device_id=place(dim), device_id_type=MESH)
    pl.semaphore_signal(barrier, inc=1, device_id=place(0, True), device_id_type=MESH)
    pl.semaphore_wait(barrier, 5)


def bits(code):
    return bin(code).count("1")


def top_of(order, code):
    return max([order.index(k) for k in DIMS if code & k], default=-1)


def dot(a, b):
    return jnp.dot(a, b, preferred_element_type=F32)


def dot_nt(a, b):
    return lax.dot_general(a, b, (((1,), (1,)), ((), ())), preferred_element_type=F32)


def normed(v):
    centred = v - jnp.mean(v, axis=-1, keepdims=True)
    r = lax.rsqrt(jnp.mean(centred * centred, axis=-1, keepdims=True) + 1e-05)
    return centred * r, r


def norm_back(e, xhat, r, gain):
    eg = e * gain
    return r * (eg - jnp.mean(eg, axis=-1, keepdims=True) - xhat * jnp.mean(eg * xhat, axis=-1, keepdims=True))


def column_of(row):
    wide = jnp.broadcast_to(row.astype(F32), (128, row.shape[1]))
    return jnp.transpose(wide).astype(jnp.int32)


GATHER_ORDERS = ((ORDERS[0], ORDERS[1]),) * 3
REDUCE_ORDERS = ((ORDERS[0], ORDERS[1]),) * 3
SLOTS = {}
for _order in ORDERS:
    SLOTS[_order] = {}
    for _at, _dim in enumerate(_order):
        for _code in range(16):
            if top_of(_order, _code) < _at:
                SLOTS[_order][_code, _dim] = len(SLOTS[_order])
RISING = sorted(range(1, 16), key=bits)
FALLING = sorted(range(16), key=lambda code: -bits(code))


def cut_columns(orders, cols):
    width = cols // len(orders)
    return [(order, pl.ds(at * width, width)) for at, order in enumerate(orders)]


class Links:
    def __init__(self, piece, w, gd, from_core, from_chip, share, sems):
        self.piece, self.w, self.gd = piece, w, gd
        self.from_core, self.from_chip, self.share = from_core, from_chip, share
        (
            self.asend, self.arecv, self.acsend, self.acrecv,
            self.rsend, self.rrecv, self.rcsend, self.rcrecv, self.own,
        ) = sems
        _, self.rows, self.cols = piece.shape
        self.groups = piece.shape[0]

    def rows_at(self, d):
        return pl.ds(pl.multiple_of(d * self.rows, self.rows), self.rows)

    def own_copy(self):
        d, t = place(0)
        return [
            pltpu.make_async_copy(self.piece.at[g], self.w.at[g, t, self.rows_at(d)], self.own.at[g])
            for g in range(self.groups)
        ]

    def weight_move(self, g, part, code, dim):
        pd, pt = place(code)
        span = cut_columns(GATHER_ORDERS[g], self.cols)[part][1]
        target = self.w.at[g, pt, self.rows_at(pd), span]
        return pltpu.make_async_remote_copy(
            self.piece.at[g, :, span] if code == 0 else target,
            target,
            self.asend.at[g, part, code ^ dim],
            self.arecv.at[g, part, code ^ dim],
            device_id=place(dim),
            device_id_type=MESH,
        )

    def weight_core_move(self, g, code, mine=True):
        pd, pt = place(code, not mine)
        target = self.w.at[g, pt, self.rows_at(pd)]
        return pltpu.make_async_remote_copy(
            self.piece.at[g] if code == 0 and mine else target,
            target,
            self.acsend.at[g, code],
            self.acrecv.at[g, code],
            device_id=place(0, True),
            device_id_type=MESH,
        )

    def weight_forward(self, g, code):
        for part, order in enumerate(GATHER_ORDERS[g]):
            at = top_of(order, code)
            if code:
                self.weight_arrival(g, part, code, order[at]).wait_recv()
            for dim in order[at + 1 :]:
                self.weight_move(g, part, code, dim).start()
        self.weight_core_move(g, code).start()

    def weight_arrival(self, g, part, code, dim):
        pd, pt = place(code)
        span = cut_columns(GATHER_ORDERS[g], self.cols)[part][1]
        target = self.w.at[g, pt, self.rows_at(pd), span]
        return pltpu.make_async_remote_copy(
            target, target, self.asend.at[g, part, code], self.arecv.at[g, part, code],
            device_id=place(dim), device_id_type=MESH,
        )

    def weights_complete(self, g):
        for code in range(16):
            self.weight_core_move(g, code, False).wait_recv()

    def weights_sent(self, g):
        for part, order in enumerate(GATHER_ORDERS[g]):
            for code in range(16):
                for dim in order[top_of(order, code) + 1 :]:
                    self.weight_move(g, part, code, dim).wait_send()
        for code in range(16):
            self.weight_core_move(g, code).wait_send()

    def grad(self, g, code, core=False, span=None):
        pd, pt = place(code, core)
        where = (pt, self.rows_at(pd)) if span is None else (pt, self.rows_at(pd), span)
        return (self.gd, where) if g == 2 else (self.w, (g,) + where)

    def grad_core_move(self, g, code):
        ref, where = self.grad(g, code, True)
        return pltpu.make_async_remote_copy(
            ref.at[where],
            self.from_core.at[g, code],
            self.rcsend.at[g, code],
            self.rcrecv.at[g, code],
            device_id=place(0, True),
            device_id_type=MESH,
        )

    def grad_move(self, g, part, code, dim, sending):
        order, span = cut_columns(REDUCE_ORDERS[g], self.cols)[part]
        ref, where = self.grad(g, code, span=span)
        slot = SLOTS[order][code ^ dim if sending else code, dim]
        return pltpu.make_async_remote_copy(
            ref.at[where],
            self.from_chip.at[g, slot, :, span],
            self.rsend.at[g, part, slot],
            self.rrecv.at[g, part, slot],
            device_id=place(dim),
            device_id_type=MESH,
        )

    def grads_to_core(self, g):
        for code in FALLING:
            self.grad_core_move(g, code).start()

    def grad_step(self, g, code):
        self.grad_core_move(g, code).wait_recv()
        for part, (order, span) in enumerate(cut_columns(REDUCE_ORDERS[g], self.cols)):
            at = top_of(order, code)
            ref, where = self.grad(g, code, span=span)
            value = ref[where].astype(F32) + self.from_core[g, code, :, span].astype(F32)
            for dim in reversed(order[at + 1 :]):
                self.grad_move(g, part, code, dim, False).wait_recv()
                value = value + self.from_chip[g, SLOTS[order][code, dim], :, span].astype(F32)
            if code == 0:
                self.share[g, :, span] = value
            else:
                ref[where] = value.astype(BF)
                self.grad_move(g, part, code, order[at], True).start()

    def grads_sent(self, g):
        for code in range(16):
            self.grad_core_move(g, code).wait_send()
            for part, order in enumerate(REDUCE_ORDERS[g]):
                if code:
                    self.grad_move(g, part, code, order[top_of(order, code)], True).wait_send()


def small_place(code):
    return place(code >> 1, bool(code & 1))


def looped(count, body, events=()):
    events = list(events)

    @pl.loop(0, count)
    def _(i):
        body(i)
        for at in range(count):
            mine = events[len(events) * at // count : len(events) * (at + 1) // count]
            if mine:

                @pl.when(i == at)
                def _():
                    for event in mine:
                        event()


def layer_kernel(
    shape,
    linked,
    big_ref, small_ref, bvis_ref, svis_ref, bcot_ref, scot_ref, w_ref, vec_ref, bias_ref,
    out_ref, back_ref, share, vshare,
    w, gd, from_core, from_chip, x, na, n1t, n2t, qkv, prob, prob_small, heads, mid, acc, act, slope, cot, cott,
    vecs, bias, vgrad, bgrad, small, small_abs, small_sum, small_in,
    asend, arecv, acsend, acrecv, rsend, rrecv, rcsend, rcrecv, own, p_sem, c_sem, o_sem, s_sem,
):
    nb, bl, ns, sl = shape
    feat, wide = w.shape[2:]
    cut = nb * bl
    tokens = cut + ns * sl
    half = feat // 2
    pairs = half // 128
    d, t = lax.axis_index("dp"), lax.axis_index("tensor")
    block = 128
    steps = tokens // block
    tiles = 2 * (wide // 256)
    per = tiles // 2
    small_rows = ns * sl
    spans = [(i, i * bl, bl) for i in range(nb)] + [(nb, cut, small_rows)]
    chunk = 512
    strips = feat // 256

    cloads = [
        pltpu.make_async_copy(bcot_ref.at[t * nb + i], cot.at[pl.ds(i * bl, bl)], c_sem.at[i]) for i in range(nb)
    ]
    cloads += [
        pltpu.make_async_copy(scot_ref.at[t * ns + i], cot.at[pl.ds(cut + i * sl, sl)], c_sem.at[nb + i])
        for i in range(ns)
    ]
    big_len, small_len = big_ref.shape[1], small_ref.shape[1]
    ploads = []
    for i in range(nb):
        for at in range(big_len // chunk):
            source = big_ref.at[t * nb + i, pl.ds(at * chunk, chunk)]
            ploads.append((i, at, source, chunk, (bvis_ref, t * nb + i, i * bl, bl)))
    for i in range(ns):
        ploads.append((nb + i, 0, small_ref.at[t * ns + i], small_len, (svis_ref, t * ns + i, cut + i * sl, sl)))

    def pload(at):
        _, _, source, length, _ = ploads[at]
        return [
            pltpu.make_async_copy(
                source.at[:, pl.ds(c * 256, 256)], act.at[at % 2 * strips + c, pl.ds(0, length)], p_sem.at[at, c]
            )
            for c in range(strips)
        ]

    for copy in pload(0):
        copy.start()
    for copy in cloads:
        copy.start()

    if linked:
        link = Links(
            w_ref, w, gd, from_core, from_chip, share, (asend, arecv, acsend, acrecv, rsend, rrecv, rcsend, rcrecv, own)
        )
        owns = link.own_copy()
        for copy in owns:
            copy.start()
        small[0] = vec_ref[...]
        greet()
    else:
        wloads = [
            [pltpu.make_async_copy(w_ref.at[g, k], w.at[g, k], acsend.at[g, k]) for k in range(2)] for g in range(3)
        ]
        for copy in sum(wloads, []):
            copy.start()

    def small_move(k):
        return pltpu.make_async_remote_copy(
            small.at[pl.ds(0, 2**k)],
            small.at[pl.ds(2**k, 2**k)],
            s_sem.at[0, k],
            s_sem.at[1, k],
            device_id=small_place(2**k),
            device_id_type=MESH,
        )

    def small_step(k):
        def go():
            if k:
                small_move(k - 1).wait()
            if k < 5:
                small_move(k).start()

        return go

    def set_vectors():
        for code in range(32):
            pd, pt = small_place(code)
            small_abs[pt, pd] = small[code]
        vec_sum, bias_sum = 0.0, [0.0, 0.0]
        parts = feat // 48 if linked else 0
        for at in range(parts):
            for k in range(2):
                value = small_abs[k, at].astype(F32)
                if k == 0:
                    padded = jnp.concatenate([value, jnp.zeros((16, feat - 128), F32)], axis=1)
                    vec_sum = vec_sum + (pltpu.roll(padded, at * 48, 1) if at else padded)
                padded = jnp.concatenate([value[:8], jnp.zeros((8, wide - 128), F32)], axis=1)
                bias_sum[k] = bias_sum[k] + (pltpu.roll(padded, at * 96, 1) if at else padded)
        vecs[...] = vec_sum[:8]
        for k in range(2):
            bias[k] = bias_sum[k]

    def vec(i):
        return vecs[i : i + 1, :]

    def rows_of(i):
        return pl.ds(pl.multiple_of(i * block, block), block)

    def pick(at):
        def go():
            chip, part, _, length, (vis_ref, row, first_row, count) = ploads[at]
            for copy in pload(at):
                copy.wait()
            if at + 1 < len(ploads):
                for copy in pload(at + 1):
                    copy.start()
            column = column_of(vis_ref[row]) - part * length
            lane = lax.broadcasted_iota(jnp.int32, column.shape, 1)
            hot = jnp.concatenate([(column == lane + k * 128).astype(BF) for k in range(length // 128)], axis=1)
            rows = pl.ds(first_row, count)
            for c in range(strips):
                picked = dot(hot, act[at % 2 * strips + c, :length])
                span = pl.ds(c * 256, 256)
                if part:
                    picked = picked + x[rows, span].astype(F32)
                x[rows, span] = picked.astype(BF)

        return go

    picks = [pick(at) for at in range(len(ploads))]

    def weight_event(g, code):
        return lambda: link.weight_forward(g, code)

    if linked:
        order = sorted(
            [(bits(code) + AHEAD * g, g, n, code) for g in range(3) for n, code in enumerate([0] + RISING)]
        )
        sequence = [(g, weight_event(g, code)) for _, g, _, code in order]
        last = [max(i for i, (g, _) in enumerate(sequence) if g == k) for k in range(3)]
        weight_events = [[e for _, e in sequence[lo : hi + 1]] for lo, hi in zip([0] + [i + 1 for i in last], last)]
        mixed = [e for e in weight_events[0][:1]]
        queue = weight_events[0][1:]
        smalls = [small_step(k) for k in range(6)]
        mixed += smalls[:1]
        smalls = smalls[1:]
        work = list(picks)
        while queue or smalls or work:
            if smalls:
                mixed.append(smalls.pop(0))
            if queue:
                mixed.append(queue.pop(0))
            if work:
                mixed.append(work.pop(0))
        for event in mixed:
            event()
        set_vectors()
    else:
        weight_events = [[], [], []]
        for event in picks:
            event()
        vecs[...] = vec_ref[...]
        bias[...] = bias_ref[...]

    def weights_ready(g):
        if linked:
            owns[g].wait()
            link.weights_complete(g)
        else:
            for copy in wloads[g]:
                copy.wait()

    def norm_one(i):
        xhat, r = normed(x[rows_of(i), :].astype(F32))
        value = xhat * vec(0) + vec(1)
        na[rows_of(i), :] = value.astype(BF)
        n1t[:, rows_of(i)] = jnp.transpose(value).astype(BF)

    looped(steps, norm_one)
    weights_ready(0)
    events = weight_events[1]
    lot = len(events) // 3

    def make_qkv(i):
        k, c = i // 3, i % 3
        span = pl.ds(pl.multiple_of(c * half, half), half)
        qkv[k, :, span] = dot(na[...], w[0, k, :, span]).astype(BF)

    looped(6, make_qkv, events[:lot])

    lane = lax.broadcasted_iota(jnp.int32, (1, 128), 1)
    first = lane < HD
    zero = jnp.zeros((), BF)

    def softmax(scores):
        e = jnp.exp(scores - jnp.max(scores, axis=-1, keepdims=True))
        return e / jnp.sum(e, axis=-1, keepdims=True)

    same = (
        lax.broadcasted_iota(jnp.int32, (small_rows, small_rows), 0) // sl
        == lax.broadcasted_iota(jnp.int32, (small_rows, small_rows), 1) // sl
    )

    def pair_spans(pair):
        k, j = pair // pairs, pair % pairs
        return k, [pl.ds(pl.multiple_of(c * half + j * 128, 128), 128) for c in range(3)]

    def attention(pair):
        k, lanes = pair_spans(pair)
        for i, start, count in spans:
            rows = pl.ds(start, count)
            q, key, value = (qkv[k, rows, lanes[c]] for c in range(3))
            mixed = []
            for h in range(2):
                q_head = jnp.where(first if h == 0 else ~first, q, zero)
                scores = dot_nt(q_head, key) * HD ** (-0.5)
                if i == nb:
                    scores = jnp.where(same, scores, -jnp.inf)
                p = softmax(scores).astype(BF)
                if i == nb:
                    prob_small[pair, h] = p
                else:
                    prob[pair, i, h] = p
                mixed.append(dot(p, value))
            heads[rows, pl.ds(pl.multiple_of(pair * 128, 128), 128)] = jnp.where(first, mixed[0], mixed[1]).astype(BF)

    looped(2 * pairs, attention, events[lot:])

    out_span = pl.ds(3 * half, half)

    def project(i):
        span = pl.ds(pl.multiple_of(i * 256, 256), 256)
        mid[:, span] = dot_nt(heads[:, :half], w[0, 0, span, out_span]) + dot_nt(heads[:, half:], w[0, 1, span, out_span])

    looped(feat // 256, project)

    def norm_two(i):
        middle = x[rows_of(i), :].astype(F32) + mid[rows_of(i), :] + vec(4)
        mid[rows_of(i), :] = middle
        xhat, r = normed(middle)
        value = xhat * vec(2) + vec(3)
        na[rows_of(i), :] = value.astype(BF)
        n2t[:, rows_of(i)] = jnp.transpose(value).astype(BF)
        acc[rows_of(i), :] = middle + vec(5)

    looped(steps, norm_two)
    for copy in cloads:
        copy.wait()

    def turn_cot(i):
        cott[:, rows_of(i)] = jnp.transpose(cot[rows_of(i), :].astype(F32)).astype(BF)

    looped(steps, turn_cot)
    weights_ready(1)
    events = weight_events[2]
    lot = len(events) * 2 // 3

    def tile_of(i):
        return i // per, pl.ds(pl.multiple_of((i % per) * 256, 256), 256)

    def up(i):
        k, span = tile_of(i)
        pre = dot(na[...], w[1, k, :, span]) + bias[k, 6:7, span]
        cdf = 0.5 * (1.0 + lax.erf(pre * 0.7071067811865476))
        act[i] = (pre * cdf).astype(BF)
        slope[i] = (cdf + pre * jnp.exp(-0.5 * pre * pre) * 0.3989422804014327).astype(BF)

    looped(tiles, up, events[:lot])

    def grad_down(i):
        k, span = tile_of(i)
        gd[k, :, span] = dot(cott[...], act[i]).astype(BF)

    looped(tiles, grad_down, events[lot:])
    if linked:
        link.grads_to_core(2)
    weights_ready(2)

    def down(i):
        k, span = tile_of(i)
        acc[...] += dot_nt(act[i], w[2, k, :, span])

    looped(tiles, down)
    na[...] = acc[...].astype(BF)

    def row_moves(kind, start, count, n):
        target = (out_ref if kind == 0 else back_ref).at[t, pl.ds(start, count)] if linked else (
            out_ref if kind == 0 else back_ref
        ).at[pl.ds(start, count)]
        source = (na if kind == 0 else cot).at[pl.ds(start, count)]
        near = pltpu.make_async_copy(source, target, o_sem.at[0, kind, n])
        if not linked:
            return [near], None
        far = pltpu.make_async_remote_copy(
            source, target, o_sem.at[1, kind, n], o_sem.at[2, kind, n], device_id=place(Y), device_id_type=MESH
        )
        return [near, far], far

    for move in row_moves(0, 0, tokens, 0)[0]:
        move.start()

    acc[...] = jnp.zeros_like(acc)
    if linked:
        for g in range(3):
            link.weights_sent(g)

    def grad_events(g, codes):
        if not linked:
            return []
        return [functools.partial(link.grad_step, g, code) for code in codes]

    def back_up(i):
        k, span = tile_of(i)
        back = (slope[i].astype(F32) * dot(cot[...], w[2, k, :, span])).astype(BF)
        bgrad[k, 6:7, span] = jnp.sum(back.astype(F32), axis=0, keepdims=True)
        acc[...] += dot_nt(back, w[1, k, :, span])
        w[1, k, :, span] = dot(n2t[...], back).astype(BF)

    bgrad[...] = jnp.zeros_like(bgrad)
    looped(tiles, back_up, grad_events(2, FALLING[:8]))
    if linked:
        link.grads_to_core(1)

    vgrad[...] = jnp.zeros_like(vgrad)

    def norm_two_back(i):
        e = acc[rows_of(i), :]
        xhat, r = normed(mid[rows_of(i), :])
        back_out = cot[rows_of(i), :].astype(F32)
        back_middle = back_out + norm_back(e, xhat, r, vec(2))
        acc[rows_of(i), :] = back_middle
        cot[rows_of(i), :] = back_middle.astype(BF)
        n2t[:, rows_of(i)] = jnp.transpose(back_middle).astype(BF)
        vgrad[2:3, :] += jnp.sum(e * xhat, axis=0, keepdims=True)
        vgrad[3:4, :] += jnp.sum(e, axis=0, keepdims=True)
        vgrad[4:5, :] += jnp.sum(back_middle, axis=0, keepdims=True)
        vgrad[5:6, :] += jnp.sum(back_out, axis=0, keepdims=True)

    looped(steps, norm_two_back, grad_events(2, FALLING[8:12]))

    dheads = heads
    for k in range(2):
        here = pl.ds(k * half, half)
        grad = dot(n2t[...], heads[:, here]).astype(BF)
        dheads[:, here] = dot(cot[...], w[0, k, :, out_span]).astype(BF)
        w[0, k, :, out_span] = grad

    def attention_back(i, rows, pair):
        k, lanes = pair_spans(pair)
        q, key, value = (qkv[k, rows, lanes[c]] for c in range(3))
        dh = dheads[rows, pl.ds(pl.multiple_of(pair * 128, 128), 128)]
        dh_t = jnp.transpose(dh.astype(F32)).astype(BF)
        q_t = jnp.transpose(q.astype(F32)).astype(BF)
        dq, dk_t, dv_t = [], [], []
        for h in range(2):
            p = prob_small[pair, h] if i == nb else prob[pair, i, h]
            dh_head = jnp.where(first if h == 0 else ~first, dh, zero)
            dp = dot_nt(dh_head, value)
            pf = p.astype(F32)
            ds = (pf * (dp - jnp.sum(pf * dp, axis=-1, keepdims=True))).astype(BF)
            dq.append(dot(ds, key))
            dk_t.append(dot(q_t[h * HD : (h + 1) * HD], ds))
            dv_t.append(dot(dh_t[h * HD : (h + 1) * HD], p))
        scale = HD ** (-0.5)
        qkv[k, rows, lanes[0]] = (jnp.where(first, dq[0], dq[1]) * scale).astype(BF)
        qkv[k, rows, lanes[1]] = jnp.transpose(jnp.concatenate(dk_t, axis=0) * scale).astype(BF)
        qkv[k, rows, lanes[2]] = jnp.transpose(jnp.concatenate(dv_t, axis=0)).astype(BF)

    during = [
        grad_events(2, FALLING[12:]) + grad_events(1, FALLING[:2]),
        grad_events(1, FALLING[2:8]),
        grad_events(1, FALLING[8:11]),
    ]
    for at, (i, start, count) in enumerate(spans):
        rows = pl.ds(start, count)
        looped(2 * pairs, lambda pair: attention_back(i, rows, pair), during[min(at, 2)] if at < 3 else [])

        def back_first(n):
            span = pl.ds(pl.multiple_of(n * 256, 256), 256)
            both = pl.ds(0, 3 * half)
            mid[rows, span] = dot_nt(qkv[0, rows, both], w[0, 0, span, both]) + dot_nt(
                qkv[1, rows, both], w[0, 1, span, both]
            )

        looped(feat // 256, back_first)

        def norm_one_back(n):
            here = pl.ds(pl.multiple_of(start + n * block, block), block)
            e = mid[here, :]
            xhat, r = normed(x[here, :].astype(F32))
            back_in = acc[here, :] + norm_back(e, xhat, r, vec(0))
            cot[here, :] = back_in.astype(BF)
            vgrad[0:1, :] += jnp.sum(e * xhat, axis=0, keepdims=True)
            vgrad[1:2, :] += jnp.sum(e, axis=0, keepdims=True)

        looped(count // block, norm_one_back)
        for move in row_moves(1, start, count, at)[0]:
            move.start()

    def grad_qkv(i):
        k, c = i // 3, i % 3
        span = pl.ds(pl.multiple_of(c * half, half), half)
        w[0, k, :, span] = dot(n1t[...], qkv[k, :, span]).astype(BF)

    looped(6, grad_qkv, grad_events(1, FALLING[11:]))

    def cut_small():
        low = lax.broadcasted_iota(jnp.int32, (8, 128), 1)
        row = lax.broadcasted_iota(jnp.int32, (8, 128), 0)
        for at in range(feat // 48):
            value = vgrad[...]
            if at:
                value = pltpu.roll(value, feat - at * 48, 1)
            value = jnp.where((low < 48) & (row < 6), value[:, :128], 0.0)
            for k in range(2):
                more = bgrad[k]
                if at:
                    more = pltpu.roll(more, wide - at * 96, 1)
                small_abs_sum[k, at] = value + jnp.where((low < 96) & (row == 6), more[:, :128], 0.0)
        for code in range(32):
            pd, pt = small_place(code)
            small_sum[code] = small_abs_sum[pt, pd]

    small_abs_sum = small_in[1]
    small_got = small_in[0]

    def sum_move(k):
        return pltpu.make_async_remote_copy(
            small_sum.at[pl.ds(2**k, 2**k)],
            small_got.at[pl.ds(2**k, 2**k)],
            s_sem.at[2, k],
            s_sem.at[3, k],
            device_id=small_place(2**k),
            device_id_type=MESH,
        )

    def sum_step(k):
        def go():
            if k < 4:
                sum_move(k + 1).wait()
                here = pl.ds(0, 2 ** (k + 1))
                small_sum[here] = small_sum[here] + small_got[pl.ds(2 ** (k + 1), 2 ** (k + 1))]
            if k >= 0:
                sum_move(k).start()

        return go

    if linked:
        link.grads_to_core(0)
        cut_small()
        last_events = grad_events(0, FALLING)
        sums = [sum_step(k) for k in range(4, -2, -1)]
        while last_events or sums:
            if sums:
                sums.pop(0)()
            for event in last_events[:2]:
                event()
            last_events = last_events[2:]
        vshare[...] = small_sum[0]
        for g in range(3):
            link.grads_sent(g)
    else:
        saves = []
        for g in range(3):
            for k in range(2):
                source = gd.at[k] if g == 2 else w.at[g, k]
                saves.append(pltpu.make_async_copy(source, share.at[g, k], acsend.at[g, k]))
        for copy in saves:
            copy.start()
        for copy in saves:
            copy.wait()
        vshare[pl.ds(0, 8), pl.ds(0, feat)] = vgrad[...]
        for k in range(2):
            vshare[pl.ds(8 + 8 * k, 8), :] = bgrad[k]
    for move in row_moves(0, 0, tokens, 0)[0]:
        move.wait()
    for at, (i, start, count) in enumerate(spans):
        near, far = row_moves(1, start, count, at)[0][0], row_moves(1, start, count, at)[1]
        near.wait()
        if linked:
            far.wait()


AHEAD = 3
VLIM = 60


def run_layer(linked, big, small, bvis, svis, bcot, scot, w, vectors, bias, parts, wide):
    nb, bl = bvis.shape[0] // parts, bvis.shape[2]
    ns, sl = svis.shape[0] // parts, svis.shape[2]
    tokens = nb * bl + ns * sl
    feat = big.shape[2]
    tiles = 2 * (wide // 256)
    pairs = feat // 128
    rows = w.shape[1] if linked else 48
    vm, hbm = pl.BlockSpec(memory_space=pltpu.VMEM), pl.BlockSpec(memory_space=pl.ANY)
    pair = (2, tokens, feat) if linked else (tokens, feat)
    dma = pltpu.SemaphoreType.DMA
    link = (lambda *shape: pltpu.VMEM(shape, BF)) if linked else (lambda *shape: pltpu.VMEM((16, 128), BF))
    loads = nb * (big.shape[1] // 512) + ns
    return pl.pallas_call(
        functools.partial(layer_kernel, (nb, bl, ns, sl), linked),
        out_shape=(
            jax.ShapeDtypeStruct(pair, BF),
            jax.ShapeDtypeStruct(pair, BF),
            jax.ShapeDtypeStruct((3, rows, wide) if linked else w.shape, F32 if linked else BF),
            jax.ShapeDtypeStruct((8, 128) if linked else (24, wide), F32),
        ),
        in_specs=[hbm, hbm, vm, vm, hbm, hbm, hbm, vm, vm],
        out_specs=(hbm, hbm, vm if linked else hbm, vm),
        scratch_shapes=[
            pltpu.VMEM((3, 2, feat, wide), BF),
            pltpu.VMEM((2, feat, wide), BF),
            link(3, 16, rows, wide),
            link(3, 15, rows, wide),
            pltpu.VMEM((tokens, feat), BF),
            pltpu.VMEM((tokens, feat), BF),
            pltpu.VMEM((feat, tokens), BF),
            pltpu.VMEM((feat, tokens), BF),
            pltpu.VMEM((2, tokens, 3 * feat // 2), BF),
            pltpu.VMEM((pairs, nb, 2, bl, bl), BF),
            pltpu.VMEM((pairs, 2, ns * sl, ns * sl), BF),
            pltpu.VMEM((tokens, feat), BF),
            pltpu.VMEM((tokens, feat), F32),
            pltpu.VMEM((tokens, feat), F32),
            pltpu.VMEM((tiles, tokens, 256), BF),
            pltpu.VMEM((tiles, tokens, 256), BF),
            pltpu.VMEM((tokens, feat), BF),
            pltpu.VMEM((feat, tokens), BF),
            pltpu.VMEM((8, feat), F32),
            pltpu.VMEM((2, 8, wide), F32),
            pltpu.VMEM((8, feat), F32),
            pltpu.VMEM((2, 8, wide), F32),
            pltpu.VMEM((32, 16, 128), BF),
            pltpu.VMEM((2, 16, 16, 128), BF),
            pltpu.VMEM((32, 8, 128), F32),
            [pltpu.VMEM((32, 8, 128), F32), pltpu.VMEM((2, 16, 8, 128), F32)],
            dma((3, 2, 16)),
            dma((3, 2, 16)),
            dma((3, 16)),
            dma((3, 16)),
            dma((3, 2, 15)),
            dma((3, 2, 15)),
            dma((3, 16)),
            dma((3, 16)),
            dma((3,)),
            dma((loads, feat // 256)),
            dma((nb + ns,)),
            dma((3, 2, nb + 1)),
            dma((4, 5)),
        ],
        compiler_params=pltpu.CompilerParams(
            collective_id=0 if linked else None, has_side_effects=linked, vmem_limit_bytes=VLIM * MIB
        ),
        name="layer",
    )(big, small, bvis, svis, bcot, scot, w, vectors, bias)


def scatter_kernel(bvis_ref, svis_ref, brow_ref, srow_ref, big_ref, small_ref):
    def spread(vis, rows, length):
        hot = lax.broadcasted_iota(jnp.int32, (length, vis.shape[1]), 0) == vis
        return dot(hot.astype(BF), rows)

    big_ref[...] = spread(bvis_ref[...], brow_ref[...], big_ref.shape[0])
    small_ref[...] = spread(svis_ref[...], srow_ref[...], small_ref.shape[0])


def scatter_rows(bvis, svis, rows, big_len, small_len):
    parts = rows.shape[0]
    nb, _, bl = bvis.shape
    ns, _, sl = svis.shape
    feat = rows.shape[2]
    share = nb // parts
    first_small = share * bl // sl
    return pl.pallas_call(
        scatter_kernel,
        grid=(nb,),
        out_shape=(
            jax.ShapeDtypeStruct((nb, big_len, feat), F32),
            jax.ShapeDtypeStruct((ns, small_len, feat), F32),
        ),
        in_specs=[
            pl.BlockSpec((None, 1, bl), lambda i: (i, 0, 0)),
            pl.BlockSpec((None, 1, sl), lambda i: (i, 0, 0)),
            pl.BlockSpec((None, bl, feat), lambda i: (i // share, i % share, 0)),
            pl.BlockSpec((None, sl, feat), lambda i: (i // share, first_small + i % share, 0)),
        ],
        out_specs=(
            pl.BlockSpec((None, big_len, feat), lambda i: (i, 0, 0)),
            pl.BlockSpec((None, small_len, feat), lambda i: (i, 0, 0)),
        ),
        compiler_params=pltpu.CompilerParams(vmem_limit_bytes=40 * MIB),
        name="scatter_rows",
    )(bvis, svis, rows, rows)


def adam_step(weight, moment_one, moment_two, gradient, step_rate, decay_rate):
    moment_one = 0.9 * moment_one + 0.1 * gradient
    moment_two = 0.999 * moment_two + 0.001 * gradient * gradient
    fixed_one = moment_one / (1.0 - 0.9**STEP_NUMBER)
    fixed_two = moment_two / (1.0 - 0.999**STEP_NUMBER)
    update = fixed_one / (jnp.sqrt(fixed_two) + 1e-08) + decay_rate * weight
    return (weight - step_rate * update, moment_one, moment_two)


def on_device(
    special,
    big_patches, small_patches, big_visible, small_visible, big_cot, small_cot,
    qkv_weight, qkv_first, qkv_second, out_weight, out_first, out_second,
    up_weight, up_first, up_second, down_weight, down_first, down_second,
    up_bias, up_bias_first, up_bias_second, norm_vectors, norm_first, norm_second,
):
    rows, half = out_weight.shape
    wide = up_weight.shape[1]
    feat = big_patches.shape[2]
    parts = feat // half
    piece = jnp.stack(
        [
            jnp.concatenate([qkv_weight.reshape(rows, 3 * half), out_weight], axis=1).astype(BF),
            up_weight.astype(BF),
            down_weight.astype(BF),
        ]
    )
    bvis, svis = big_visible[:, None, :], small_visible[:, None, :]
    chips = (big_patches, small_patches, bvis, svis, big_cot, small_cot)
    if special:
        few = jnp.concatenate(
            [
                jnp.pad(norm_vectors, ((0, 0), (0, 128 - norm_vectors.shape[1]))),
                jnp.pad(up_bias, ((0, 9), (0, 128 - up_bias.shape[1]))),
            ]
        ).astype(BF)
        out_both, back_both, share, vshare = run_layer(True, *chips, piece, few, few, parts, wide)
        norm_share = vshare[:6, : norm_vectors.shape[1]]
        bias_share = vshare[6:7, : up_bias.shape[1]]
    else:
        w = lax.all_gather(lax.all_gather(piece, "dp", axis=1, tiled=True), "tensor", axis=1)
        vectors = lax.all_gather(norm_vectors.astype(BF), "dp", axis=1, tiled=True).astype(F32)
        bias = lax.all_gather(up_bias.astype(BF), "dp", axis=1, tiled=True)
        bias = lax.all_gather(bias, "tensor", axis=0).astype(F32)
        out_rows, back_rows, grads, few = run_layer(
            False, *chips, w, jnp.pad(vectors, ((0, 2), (0, 0))), jnp.pad(bias, ((0, 0), (6, 1), (0, 0))), parts, wide
        )
        share = lax.psum_scatter(grads, "tensor", scatter_dimension=1)
        share = lax.psum_scatter(share, "dp", scatter_dimension=1, tiled=True).astype(F32)
        both = lax.all_gather(jnp.stack([out_rows, back_rows]), "tensor", axis=1)
        out_both, back_both = both[0], both[1]
        norm_share = lax.psum_scatter(lax.psum(few[:6, :feat], "tensor"), "dp", scatter_dimension=1, tiled=True)
        bias_share = lax.psum_scatter(few[14::8], "tensor", scatter_dimension=0, tiled=True)
        bias_share = lax.psum_scatter(bias_share, "dp", scatter_dimension=1, tiled=True)
    big_count, big_len = big_visible.shape
    small_count, small_len = small_visible.shape
    cut = big_count // parts * big_len
    big_out = out_both[:, :cut].reshape(big_count, big_len, feat)
    small_out = out_both[:, cut:].reshape(small_count, small_len, feat)
    big_grad, small_grad = scatter_rows(bvis, svis, back_both, big_patches.shape[1], small_patches.shape[1])

    qkv_share = share[0, :, : 3 * half].reshape(rows, 3, half)
    new = []
    for at, (weight, one, two, gradient) in enumerate(
        (
            (qkv_weight, qkv_first, qkv_second, qkv_share),
            (out_weight, out_first, out_second, share[0, :, 3 * half :]),
            (up_weight, up_first, up_second, share[1]),
            (down_weight, down_first, down_second, share[2]),
            (up_bias, up_bias_first, up_bias_second, bias_share),
            (norm_vectors, norm_first, norm_second, norm_share),
        )
    ):
        new.extend(adam_step(weight, one, two, gradient, LEARN_RATES[at], DECAYS[at]))
    return (big_out, small_out, big_grad, small_grad, *new)


def solution(mesh):
    special = mesh.shape["dp"] == 16 and mesh.shape["tensor"] == 2
    chips = P("dp", None, None)
    matrix, qkv = P("dp", "tensor"), P("dp", None, "tensor")
    states = (qkv,) * 3 + (matrix,) * 9 + (P("tensor", "dp"),) * 3 + (P(None, "dp"),) * 3
    return jax.shard_map(
        functools.partial(on_device, special),
        mesh=mesh,
        in_specs=(chips, chips, P("dp", None), P("dp", None), chips, chips) + states,
        out_specs=(chips,) * 4 + states,
        check_vma=False,
    )
```

time: 454 us -> 250 us (0.55)
  Pallas kernels: 295 us -> 232 us
  blocking collectives: 60.8 us -> 0 us
  waiting for transfers between devices: 53.9 us -> 0 us
  between operations: 15 us -> 0.91 us
  local copies, waits for them, and re-layouts: 12.4 us -> 6.22 us
  other arithmetic: 15.7 us -> 10.7 us
    pallas_call x3 -> x1, Pallas kernels: 288 us -> 226 us  [run_layer(): pl.pallas_call(functools.partial(layer_kernel, (nb, bl, ns, sl), linked),...]
    unnamed x4 -> x0, waiting for transfers between devices: 53.9 us -> none
    unnamed x2 -> x0, blocking collectives: 36.6 us -> none
    all_gather x2 -> x0, blocking collectives: 24.2 us -> none  [the longest x1 19.6 us: on_device(): lax.all_gather(norm_vectors.astype(BF), 'dp', axis=1, tiled=True)]
    unnamed x49 -> x40, local copies, waits for them, and re-layouts: 6.82 us -> 0.11 us
  transfers between devices with their start and end apart: 2 -> 0, of which waited for: 1 -> 0; matrix products, arithmetic and copies ran while one was open for 3% -> 0% of each run, Pallas kernels for 28% -> 0%
where the time goes in v2:
time: 250 us
  Pallas kernels  232 us (93%)
  other arithmetic  10.7 us (4%)
  local copies, waits for them, and re-layouts  6.22 us (2%)
    pallas_call x1, Pallas kernels, run_layer(): pl.pallas_call(functools.partial(layer_kernel, (nb, bl, ns, sl), linked),...  226 us
    pallas_call x1, Pallas kernels, scatter_rows(): pl.pallas_call(scatter_kernel, grid=(nb,), out_shape=(jax.ShapeDtypeStruc...  6.45 us
    sub x5, other arithmetic, adam_step(): return (weight - step_rate * update, moment_one, moment_two)  6.33 us

profile of v2, /device:TPU:0, one launch (start us, length us, event | category | flops | bytes accessed | tf_op | source)
XLA Modules:
  0.0 249.9 jit_solution(5193482146737776105)
XLA Ops:
  0.7 1.3 broadcast_in_dim.6.bvis_ref
  2.0 1.1 convert_bitcast_fusion
  3.1 0.9 convert_bitcast_fusion.2
  4.0 0.9 convert.18
  4.9 0.1 copy.58
  5.0 0.1 concatenate.19
  5.1 0.8 pad_maximum_fusion.w_ref
  5.9 0.6 fusion.10.vec_ref.bias_ref
  6.5 225.6 %layer.1 = (bf16[2,640,768]{2,1,0:T(8,128)(2,1)}, bf16[2,640,768]{2,1,0:T(8,128)(2,1)}, f32[3,48,1536]{2,1,0:T(8,128)}, f32[8,128]{1,0:T(8,128)}) custom-call(bf16[4,1024,768]{2,1,0:T(8,128)(2,1)} %big_ref.1, bf16[4,256,768]{2,1,0:T(8,128)(2,1)} %small_ref.1, s32[4,1,256]{2,1,0:T(1,128)} %broadcast_in_dim.6.bvis_ref, s32[4,1,64]{2,1,0:T(1,128)} %bitcast.30, ...), custom_call_target="tpu_custom_call" | custom-call | tf_op jit(solution)/shard_map/layer/pallas_call | solution.py:756
  232.2 0.0 copy-start.1
  232.2 2.8 %slice.24 = bf16[2,512,768]{2,1,0:T(8,128)(2,1)} slice(bf16[2,640,768]{2,1,0:T(8,128)(2,1)} %get-tuple-element.28), slice={[0:2], [0:512], [0:768]} | slice | bytes 3145728 | tf_op jit(solution)/shard_map/slice | solution.py:909
  235.0 1.8 slice.25
  236.8 0.0 copy-start.5
  236.8 6.4 %scatter_rows.1 = (f32[4,1024,768]{2,1,0:T(8,128)}, f32[4,256,768]{2,1,0:T(8,128)}) custom-call(s32[4,1,256]{2,1,0:T(1,128)S(1)} %copy-done.1, s32[4,1,64]{2,1,0:T(1,128)S(1)} %bitcast.31, bf16[2,640,768]{2,1,0:T(8,128)(2,1)S(1)} %copy-done, bf16[2,640,768]{2,1,0:T(8,128)(2,1)S(1)} %copy-done), custom_call_target="tpu_custom_call" | custom-call | tf_op jit(solution)/shard_map/scatter_rows/pallas_call | solution.py:830
  243.2 0.0 copy-start.7
  243.3 0.0 copy-start.10
  243.3 0.1 reshape_squeeze.3
  243.4 2.1 multiply_subtract_fusion.2
  245.5 1.6 multiply_subtract_fusion.3
  247.2 0.0 copy-start.15
  247.2 0.0 copy-start.16
  247.2 1.5 multiply_subtract_fusion
  248.7 0.5 multiply_subtract_fusion.5
  249.3 0.6 multiply_subtract_fusion.4
  (37 shorter events, 0.1 us)
Async XLA Ops:
  0.7 5.2 %copy-start.17 = (f32[1,96]{1,0:T(1,128)S(1)}, f32[1,96]{1,0:T(1,128)}, u32[]{:S(2)}) copy-start(f32[1,96]{1,0:T(1,128)} %param.42) | copy-start | bytes 1156
  0.7 5.2 %copy-start.13 = (f32[6,48]{1,0:T(8,128)S(1)}, f32[6,48]{1,0:T(8,128)}, u32[]{:S(2)}) copy-start(f32[6,48]{1,0:T(8,128)} %param.45) | copy-start | bytes 3460
  232.1 4.6 %copy-start = (bf16[2,640,768]{2,1,0:T(8,128)(2,1)S(1)}, bf16[2,640,768]{2,1,0:T(8,128)(2,1)}, u32[]{:S(2)}) copy-start(bf16[2,640,768]{2,1,0:T(8,128)(2,1)} %get-tuple-element.29.brow_ref.srow_ref) | copy-start | bytes 5898244
  232.2 4.6 %copy-start.1 = (s32[4,1,256]{2,1,0:T(1,128)S(1)}, s32[4,1,256]{2,1,0:T(1,128)}, u32[]{:S(2)}) copy-start(s32[4,1,256]{2,1,0:T(1,128)} %broadcast_in_dim.6.bvis_ref) | copy-start | bytes 12292
  232.2 4.6 %copy-start.2 = (s32[4,64]{1,0:T(4,128)S(1)}, s32[4,64]{1,0:T(4,128)}, u32[]{:S(2)}) copy-start(s32[4,64]{1,0:T(4,128)} %param.27) | copy-start | bytes 3076
  236.7 6.5 %copy-start.6 = (f32[3,48,1536]{2,1,0:T(8,128)S(1)}, f32[3,48,1536]{2,1,0:T(8,128)}, u32[]{:S(2)}) copy-start(f32[3,48,1536]{2,1,0:T(8,128)} %get-tuple-element.32) | copy-start | bytes 2654212
  236.8 6.7 %copy-start.5 = (f32[48,3,384]{2,0,1:T(8,128)S(1)}, f32[48,3,384]{2,0,1:T(8,128)}, u32[]{:S(2)}) copy-start(f32[48,3,384]{2,0,1:T(8,128)} %param.30) | copy-start | bytes 663556
  243.2 2.3 copy-start.11
  243.2 2.3 copy-start.12
  243.2 3.9 %copy-start.3 = (f32[48,1536]{1,0:T(8,128)S(1)}, f32[48,1536]{1,0:T(8,128)}, u32[]{:S(2)}) copy-start(f32[48,1536]{1,0:T(8,128)} %param.39) | copy-start | bytes 884740
  243.2 3.9 %copy-start.4 = (f32[48,1536]{1,0:T(8,128)S(1)}, f32[48,1536]{1,0:T(8,128)}, u32[]{:S(2)}) copy-start(f32[48,1536]{1,0:T(8,128)} %param.36) | copy-start | bytes 884740
  243.2 3.9 %copy-start.7 = (f32[48,1536]{1,0:T(8,128)S(1)}, f32[48,1536]{1,0:T(8,128)}, u32[]{:S(2)}) copy-start(f32[48,1536]{1,0:T(8,128)} %param.40) | copy-start | bytes 884740
  243.2 3.9 %copy-start.8 = (f32[48,1536]{1,0:T(8,128)S(1)}, f32[48,1536]{1,0:T(8,128)}, u32[]{:S(2)}) copy-start(f32[48,1536]{1,0:T(8,128)} %param.41) | copy-start | bytes 884740
  243.3 3.9 %copy-start.9 = (f32[48,1536]{1,0:T(8,128)S(1)}, f32[48,1536]{1,0:T(8,128)}, u32[]{:S(2)}) copy-start(f32[48,1536]{1,0:T(8,128)} %param.38) | copy-start | bytes 884740
  243.3 3.9 %copy-start.10 = (f32[48,1536]{1,0:T(8,128)S(1)}, f32[48,1536]{1,0:T(8,128)}, u32[]{:S(2)}) copy-start(f32[48,1536]{1,0:T(8,128)} %param.37) | copy-start | bytes 884740
  247.2 1.5 copy-start.14
  247.2 1.5 copy-start.18
  247.2 1.5 copy-start.19
  247.2 2.1 copy-start.15
  247.2 2.1 copy-start.16

commit v3 on v2

--- a/solution.py
+++ b/solution.py
@@ -18,16 +18,13 @@
 
 Z1, Z2, X, Y = 1, 2, 4, 8
 DIMS = (Z1, Z2, X, Y)
-ORDERS = ((Z1, Z2, X, Y), (Z1, Z2, Y, X))
-
-
 def place(code, other_core=False):
     d, t = lax.axis_index("dp"), lax.axis_index("tensor")
-    z, x, c = d // 4, (d // 2) % 2, d % 2
+    z, x, c = lax.div(d, 4), lax.rem(lax.div(d, 2), 2), lax.rem(d, 2)
     if code & Z1:
-        z = z + 1 - 2 * (z % 2)
+        z = z + 1 - 2 * lax.rem(z, 2)
     if code & Z2:
-        z = z + 2 - 4 * (z // 2)
+        z = z + 2 - 4 * lax.div(z, 2)
     if code & X:
         x = 1 - x
     if code & Y:
@@ -37,7 +34,7 @@
     return z * 4 + x * 2 + c, t
 
 
-def greet():
+def greet(place):
     barrier = pltpu.get_barrier_semaphore()
     for dim in DIMS:
         pl.semaphore_signal(barrier, inc=1, device_id=place(dim), device_id_type=MESH)
@@ -61,6 +58,10 @@
     return lax.dot_general(a, b, (((1,), (1,)), ((), ())), preferred_element_type=F32)
 
 
+def dot_tn(a, b):
+    return lax.dot_general(a, b, (((0,), (0,)), ((), ())), preferred_element_type=F32)
+
+
 def normed(v):
     centred = v - jnp.mean(v, axis=-1, keepdims=True)
     r = lax.rsqrt(jnp.mean(centred * centred, axis=-1, keepdims=True) + 1e-05)
@@ -77,10 +78,18 @@
     return jnp.transpose(wide).astype(jnp.int32)
 
 
-GATHER_ORDERS = ((ORDERS[0], ORDERS[1]),) * 3
-REDUCE_ORDERS = ((ORDERS[0], ORDERS[1]),) * 3
+T, PP, Q, R = (Z2, Z1, X, Y), (Z2, Z1, Y, X), (Z2, Y, X, Z1), (Y, Z2, X, Z1)
+GATHER_ORDERS = ((T, PP), (T, PP), (T, PP))
+AHEAD = 3
+DOWN, UP, OUT, QKV = range(4)
+SUMS = (
+    (2, ((PP, 0, 768), (R, 768, 768))),
+    (1, ((PP, 0, 768), (R, 768, 768))),
+    (0, ((PP, 1152, 256), (R, 1408, 128))),
+    (0, ((PP, 0, 512), (R, 512, 640))),
+)
 SLOTS = {}
-for _order in ORDERS:
+for _order in (T, PP, Q, R):
     SLOTS[_order] = {}
     for _at, _dim in enumerate(_order):
         for _code in range(16):
@@ -106,38 +115,41 @@
         _, self.rows, self.cols = piece.shape
         self.groups = piece.shape[0]
 
-    def rows_at(self, d):
-        return pl.ds(pl.multiple_of(d * self.rows, self.rows), self.rows)
+        self.places = {(code, core): place(code, core) for code in range(16) for core in (False, True)}
+        self.spans = {at: pl.ds(pl.multiple_of(d * self.rows, self.rows), self.rows) for at, (d, _) in self.places.items()}
+
+    def place(self, code, core=False):
+        return self.places[code, core]
+
+    def at(self, code, core=False):
+        return self.places[code, core][1], self.spans[code, core]
 
     def own_copy(self):
-        d, t = place(0)
         return [
-            pltpu.make_async_copy(self.piece.at[g], self.w.at[g, t, self.rows_at(d)], self.own.at[g])
+            pltpu.make_async_copy(self.piece.at[g], self.w.at[(g,) + self.at(0)], self.own.at[g])
             for g in range(self.groups)
         ]
 
     def weight_move(self, g, part, code, dim):
-        pd, pt = place(code)
         span = cut_columns(GATHER_ORDERS[g], self.cols)[part][1]
-        target = self.w.at[g, pt, self.rows_at(pd), span]
+        target = self.w.at[(g,) + self.at(code) + (span,)]
         return pltpu.make_async_remote_copy(
             self.piece.at[g, :, span] if code == 0 else target,
             target,
             self.asend.at[g, part, code ^ dim],
             self.arecv.at[g, part, code ^ dim],
-            device_id=place(dim),
+            device_id=self.place(dim),
             device_id_type=MESH,
         )
 
     def weight_core_move(self, g, code, mine=True):
-        pd, pt = place(code, not mine)
-        target = self.w.at[g, pt, self.rows_at(pd)]
+        target = self.w.at[(g,) + self.at(code, not mine)]
         return pltpu.make_async_remote_copy(
             self.piece.at[g] if code == 0 and mine else target,
             target,
             self.acsend.at[g, code],
             self.acrecv.at[g, code],
-            device_id=place(0, True),
+            device_id=self.place(0, True),
             device_id_type=MESH,
         )
 
@@ -151,12 +163,11 @@
         self.weight_core_move(g, code).start()
 
     def weight_arrival(self, g, part, code, dim):
-        pd, pt = place(code)
         span = cut_columns(GATHER_ORDERS[g], self.cols)[part][1]
-        target = self.w.at[g, pt, self.rows_at(pd), span]
+        target = self.w.at[(g,) + self.at(code) + (span,)]
         return pltpu.make_async_remote_copy(
             target, target, self.asend.at[g, part, code], self.arecv.at[g, part, code],
-            device_id=place(dim), device_id_type=MESH,
+            device_id=self.place(dim), device_id_type=MESH,
         )
 
     def weights_complete(self, g):
@@ -171,64 +182,65 @@
         for code in range(16):
             self.weight_core_move(g, code).wait_send()
 
-    def grad(self, g, code, core=False, span=None):
-        pd, pt = place(code, core)
-        where = (pt, self.rows_at(pd)) if span is None else (pt, self.rows_at(pd), span)
+    def grad(self, n, code, core, start, width):
+        g = SUMS[n][0]
+        where = self.at(code, core) + (pl.ds(start, width),)
         return (self.gd, where) if g == 2 else (self.w, (g,) + where)
 
-    def grad_core_move(self, g, code):
-        ref, where = self.grad(g, code, True)
+    def grad_core_move(self, n, code):
+        g, parts = SUMS[n]
+        start, width = parts[0][1], sum(part[2] for part in parts)
+        ref, where = self.grad(n, code, True, start, width)
         return pltpu.make_async_remote_copy(
             ref.at[where],
-            self.from_core.at[g, code],
-            self.rcsend.at[g, code],
-            self.rcrecv.at[g, code],
-            device_id=place(0, True),
+            self.from_core.at[g, code, :, pl.ds(start, width)],
+            self.rcsend.at[n, code],
+            self.rcrecv.at[n, code],
+            device_id=self.place(0, True),
             device_id_type=MESH,
         )
 
-    def grad_move(self, g, part, code, dim, sending):
-        order, span = cut_columns(REDUCE_ORDERS[g], self.cols)[part]
-        ref, where = self.grad(g, code, span=span)
+    def grad_move(self, n, part, code, dim, sending):
+        g, parts = SUMS[n]
+        order, start, width = parts[part]
+        ref, where = self.grad(n, code, False, start, width)
         slot = SLOTS[order][code ^ dim if sending else code, dim]
         return pltpu.make_async_remote_copy(
             ref.at[where],
-            self.from_chip.at[g, slot, :, span],
-            self.rsend.at[g, part, slot],
-            self.rrecv.at[g, part, slot],
-            device_id=place(dim),
+            self.from_chip.at[g, slot, :, pl.ds(start, width)],
+            self.rsend.at[n, part, slot],
+            self.rrecv.at[n, part, slot],
+            device_id=self.place(dim),
             device_id_type=MESH,
         )
 
-    def grads_to_core(self, g):
+    def grads_to_core(self, n):
         for code in FALLING:
-            self.grad_core_move(g, code).start()
-
-    def grad_step(self, g, code):
-        self.grad_core_move(g, code).wait_recv()
-        for part, (order, span) in enumerate(cut_columns(REDUCE_ORDERS[g], self.cols)):
+            self.grad_core_move(n, code).start()
+
+    def grad_step(self, n, code):
+        g, parts = SUMS[n]
+        self.grad_core_move(n, code).wait_recv()
+        for part, (order, start, width) in enumerate(parts):
             at = top_of(order, code)
-            ref, where = self.grad(g, code, span=span)
+            span = pl.ds(start, width)
+            ref, where = self.grad(n, code, False, start, width)
             value = ref[where].astype(F32) + self.from_core[g, code, :, span].astype(F32)
             for dim in reversed(order[at + 1 :]):
-                self.grad_move(g, part, code, dim, False).wait_recv()
+                self.grad_move(n, part, code, dim, False).wait_recv()
                 value = value + self.from_chip[g, SLOTS[order][code, dim], :, span].astype(F32)
             if code == 0:
                 self.share[g, :, span] = value
             else:
                 ref[where] = value.astype(BF)
-                self.grad_move(g, part, code, order[at], True).start()
-
-    def grads_sent(self, g):
+                self.grad_move(n, part, code, order[at], True).start()
+
+    def grads_sent(self, n):
         for code in range(16):
-            self.grad_core_move(g, code).wait_send()
-            for part, order in enumerate(REDUCE_ORDERS[g]):
+            self.grad_core_move(n, code).wait_send()
+            for part, (order, _, _) in enumerate(SUMS[n][1]):
                 if code:
-                    self.grad_move(g, part, code, order[top_of(order, code)], True).wait_send()
-
-
-def small_place(code):
-    return place(code >> 1, bool(code & 1))
+                    self.grad_move(n, part, code, order[top_of(order, code)], True).wait_send()
 
 
 def looped(count, body, events=()):
@@ -252,7 +264,7 @@
     linked,
     big_ref, small_ref, bvis_ref, svis_ref, bcot_ref, scot_ref, w_ref, vec_ref, bias_ref,
     out_ref, back_ref, share, vshare,
-    w, gd, from_core, from_chip, x, na, n1t, n2t, qkv, prob, prob_small, heads, mid, acc, act, slope, cot, cott,
+    w, gd, from_core, from_chip, x, n1, n2, qkv, prob, prob_small, heads, mid, acc, act, slope, cot, out_rows,
     vecs, bias, vgrad, bgrad, small, small_abs, small_sum, small_in,
     asend, arecv, acsend, acrecv, rsend, rrecv, rcsend, rcrecv, own, p_sem, c_sem, o_sem, s_sem,
 ):
@@ -265,12 +277,13 @@
     d, t = lax.axis_index("dp"), lax.axis_index("tensor")
     block = 128
     steps = tokens // block
-    tiles = 2 * (wide // 256)
+    tile = act.shape[2]
+    tiles = act.shape[0]
     per = tiles // 2
     small_rows = ns * sl
     spans = [(i, i * bl, bl) for i in range(nb)] + [(nb, cut, small_rows)]
     chunk = 512
-    strips = feat // 256
+    strips = [(at, min(tile, feat - at)) for at in range(0, feat, tile)]
 
     cloads = [
         pltpu.make_async_copy(bcot_ref.at[t * nb + i], cot.at[pl.ds(i * bl, bl)], c_sem.at[i]) for i in range(nb)
@@ -292,9 +305,11 @@
         _, _, source, length, _ = ploads[at]
         return [
             pltpu.make_async_copy(
-                source.at[:, pl.ds(c * 256, 256)], act.at[at % 2 * strips + c, pl.ds(0, length)], p_sem.at[at, c]
+                source.at[:, pl.ds(start, width)],
+                act.at[at % 2 * len(strips) + c, pl.ds(0, length), pl.ds(0, width)],
+                p_sem.at[at, c],
             )
-            for c in range(strips)
+            for c, (start, width) in enumerate(strips)
         ]
 
     for copy in pload(0):
@@ -309,8 +324,12 @@
         owns = link.own_copy()
         for copy in owns:
             copy.start()
+
+        def small_place(code):
+            return link.place(code >> 1, bool(code & 1))
+
         small[0] = vec_ref[...]
-        greet()
+        greet(link.place)
     else:
         wloads = [
             [pltpu.make_async_copy(w_ref.at[g, k], w.at[g, k], acsend.at[g, k]) for k in range(2)] for g in range(3)
@@ -373,9 +392,9 @@
             lane = lax.broadcasted_iota(jnp.int32, column.shape, 1)
             hot = jnp.concatenate([(column == lane + k * 128).astype(BF) for k in range(length // 128)], axis=1)
             rows = pl.ds(first_row, count)
-            for c in range(strips):
-                picked = dot(hot, act[at % 2 * strips + c, :length])
-                span = pl.ds(c * 256, 256)
+            for c, (start, width) in enumerate(strips):
+                picked = dot(hot, act[at % 2 * len(strips) + c, :length, :width])
+                span = pl.ds(start, width)
                 if part:
                     picked = picked + x[rows, span].astype(F32)
                 x[rows, span] = picked.astype(BF)
@@ -394,19 +413,11 @@
         sequence = [(g, weight_event(g, code)) for _, g, _, code in order]
         last = [max(i for i, (g, _) in enumerate(sequence) if g == k) for k in range(3)]
         weight_events = [[e for _, e in sequence[lo : hi + 1]] for lo, hi in zip([0] + [i + 1 for i in last], last)]
-        mixed = [e for e in weight_events[0][:1]]
-        queue = weight_events[0][1:]
         smalls = [small_step(k) for k in range(6)]
-        mixed += smalls[:1]
-        smalls = smalls[1:]
-        work = list(picks)
-        while queue or smalls or work:
-            if smalls:
-                mixed.append(smalls.pop(0))
-            if queue:
-                mixed.append(queue.pop(0))
-            if work:
-                mixed.append(work.pop(0))
+        mixed = [weight_events[0][0], smalls[0], picks[0], picks[1]] + weight_events[0][1:3] + [smalls[1], picks[2]]
+        mixed += weight_events[0][3:5] + [picks[3], smalls[2]] + weight_events[0][5:8] + [picks[4], smalls[3]]
+        mixed += weight_events[0][8:11] + picks[5:] + [smalls[4]] + weight_events[0][11:14] + [smalls[5]]
+        mixed += weight_events[0][14:]
         for event in mixed:
             event()
         set_vectors()
@@ -419,7 +430,7 @@
 
     def weights_ready(g):
         if linked:
-            owns[g].wait()
+            link.own_copy()[g].wait()
             link.weights_complete(g)
         else:
             for copy in wloads[g]:
@@ -428,8 +439,7 @@
     def norm_one(i):
         xhat, r = normed(x[rows_of(i), :].astype(F32))
         value = xhat * vec(0) + vec(1)
-        na[rows_of(i), :] = value.astype(BF)
-        n1t[:, rows_of(i)] = jnp.transpose(value).astype(BF)
+        n1[rows_of(i), :] = value.astype(BF)
 
     looped(steps, norm_one)
     weights_ready(0)
@@ -439,7 +449,7 @@
     def make_qkv(i):
         k, c = i // 3, i % 3
         span = pl.ds(pl.multiple_of(c * half, half), half)
-        qkv[k, :, span] = dot(na[...], w[0, k, :, span]).astype(BF)
+        qkv[k, :, span] = dot(n1[...], w[0, k, :, span]).astype(BF)
 
     looped(6, make_qkv, events[:lot])
 
@@ -494,28 +504,32 @@
         mid[rows_of(i), :] = middle
         xhat, r = normed(middle)
         value = xhat * vec(2) + vec(3)
-        na[rows_of(i), :] = value.astype(BF)
-        n2t[:, rows_of(i)] = jnp.transpose(value).astype(BF)
+        n2[rows_of(i), :] = value.astype(BF)
         acc[rows_of(i), :] = middle + vec(5)
 
     looped(steps, norm_two)
     for copy in cloads:
         copy.wait()
 
-    def turn_cot(i):
-        cott[:, rows_of(i)] = jnp.transpose(cot[rows_of(i), :].astype(F32)).astype(BF)
-
-    looped(steps, turn_cot)
     weights_ready(1)
     events = weight_events[2]
     lot = len(events) * 2 // 3
 
+    def grad_events(n, lo, hi):
+        if not linked:
+            return []
+        return [functools.partial(link.grad_step, n, code) for code in FALLING[lo:hi]]
+
+    def woven(*lists):
+        keyed = [((n + 0.5) / len(events), at, event) for at, events in enumerate(lists) for n, event in enumerate(events)]
+        return [event for _, _, event in sorted(keyed, key=lambda one: one[:2])]
+
     def tile_of(i):
-        return i // per, pl.ds(pl.multiple_of((i % per) * 256, 256), 256)
+        return i // per, pl.ds(pl.multiple_of((i % per) * tile, tile), tile)
 
     def up(i):
         k, span = tile_of(i)
-        pre = dot(na[...], w[1, k, :, span]) + bias[k, 6:7, span]
+        pre = dot(n2[...], w[1, k, :, span]) + bias[k, 6:7, span]
         cdf = 0.5 * (1.0 + lax.erf(pre * 0.7071067811865476))
         act[i] = (pre * cdf).astype(BF)
         slope[i] = (cdf + pre * jnp.exp(-0.5 * pre * pre) * 0.3989422804014327).astype(BF)
@@ -524,57 +538,58 @@
 
     def grad_down(i):
         k, span = tile_of(i)
-        gd[k, :, span] = dot(cott[...], act[i]).astype(BF)
+        gd[k, :, span] = dot_tn(cot[...], act[i]).astype(BF)
 
     looped(tiles, grad_down, events[lot:])
     if linked:
-        link.grads_to_core(2)
+        link.grads_to_core(DOWN)
     weights_ready(2)
 
     def down(i):
         k, span = tile_of(i)
         acc[...] += dot_nt(act[i], w[2, k, :, span])
 
-    looped(tiles, down)
-    na[...] = acc[...].astype(BF)
-
-    def row_moves(kind, start, count, n):
-        target = (out_ref if kind == 0 else back_ref).at[t, pl.ds(start, count)] if linked else (
-            out_ref if kind == 0 else back_ref
-        ).at[pl.ds(start, count)]
-        source = (na if kind == 0 else cot).at[pl.ds(start, count)]
+    looped(tiles, down, grad_events(DOWN, 0, 3))
+    out_rows[...] = acc[...].astype(BF)
+
+    def row_moves(kind, n):
+        rows = pl.ds(n * 64, 64)
+        source = (out_rows if kind == 0 else n2).at[rows]
+        target = out_ref if kind == 0 else back_ref
+        target = target.at[t, rows] if linked else target.at[rows]
         near = pltpu.make_async_copy(source, target, o_sem.at[0, kind, n])
         if not linked:
-            return [near], None
+            return [near]
         far = pltpu.make_async_remote_copy(
-            source, target, o_sem.at[1, kind, n], o_sem.at[2, kind, n], device_id=place(Y), device_id_type=MESH
-        )
-        return [near, far], far
-
-    for move in row_moves(0, 0, tokens, 0)[0]:
-        move.start()
+            source, target, o_sem.at[1, kind, n], o_sem.at[2, kind, n], device_id=link.place(Y), device_id_type=MESH
+        )
+        return [near, far]
+
+    def row_event(kind, n):
+        def go():
+            for move in row_moves(kind, n):
+                move.start()
+
+        return go
+
+    outs = [row_event(0, n) for n in range(tokens // 64)]
 
     acc[...] = jnp.zeros_like(acc)
     if linked:
         for g in range(3):
             link.weights_sent(g)
-
-    def grad_events(g, codes):
-        if not linked:
-            return []
-        return [functools.partial(link.grad_step, g, code) for code in codes]
 
     def back_up(i):
         k, span = tile_of(i)
         back = (slope[i].astype(F32) * dot(cot[...], w[2, k, :, span])).astype(BF)
         bgrad[k, 6:7, span] = jnp.sum(back.astype(F32), axis=0, keepdims=True)
         acc[...] += dot_nt(back, w[1, k, :, span])
-        w[1, k, :, span] = dot(n2t[...], back).astype(BF)
+        w[1, k, :, span] = dot_tn(n2[...], back).astype(BF)
 
     bgrad[...] = jnp.zeros_like(bgrad)
-    looped(tiles, back_up, grad_events(2, FALLING[:8]))
+    looped(tiles, back_up, woven(grad_events(DOWN, 3, 9), outs[:5]))
     if linked:
-        link.grads_to_core(1)
+        link.grads_to_core(UP)
 
     vgrad[...] = jnp.zeros_like(vgrad)
 
@@ -585,50 +600,59 @@
         back_middle = back_out + norm_back(e, xhat, r, vec(2))
         acc[rows_of(i), :] = back_middle
         cot[rows_of(i), :] = back_middle.astype(BF)
-        n2t[:, rows_of(i)] = jnp.transpose(back_middle).astype(BF)
         vgrad[2:3, :] += jnp.sum(e * xhat, axis=0, keepdims=True)
         vgrad[3:4, :] += jnp.sum(e, axis=0, keepdims=True)
         vgrad[4:5, :] += jnp.sum(back_middle, axis=0, keepdims=True)
         vgrad[5:6, :] += jnp.sum(back_out, axis=0, keepdims=True)
 
-    looped(steps, norm_two_back, grad_events(2, FALLING[8:12]))
+    looped(steps, norm_two_back, woven(grad_events(DOWN, 9, 12), outs[5:7]))
 
     dheads = heads
     for k in range(2):
         here = pl.ds(k * half, half)
-        grad = dot(n2t[...], heads[:, here]).astype(BF)
+        grad = dot_tn(cot[...], heads[:, here]).astype(BF)
         dheads[:, here] = dot(cot[...], w[0, k, :, out_span]).astype(BF)
         w[0, k, :, out_span] = grad
 
-    def attention_back(i, rows, pair):
-        k, lanes = pair_spans(pair)
-        q, key, value = (qkv[k, rows, lanes[c]] for c in range(3))
-        dh = dheads[rows, pl.ds(pl.multiple_of(pair * 128, 128), 128)]
-        dh_t = jnp.transpose(dh.astype(F32)).astype(BF)
-        q_t = jnp.transpose(q.astype(F32)).astype(BF)
-        dq, dk_t, dv_t = [], [], []
-        for h in range(2):
-            p = prob_small[pair, h] if i == nb else prob[pair, i, h]
-            dh_head = jnp.where(first if h == 0 else ~first, dh, zero)
-            dp = dot_nt(dh_head, value)
-            pf = p.astype(F32)
-            ds = (pf * (dp - jnp.sum(pf * dp, axis=-1, keepdims=True))).astype(BF)
-            dq.append(dot(ds, key))
-            dk_t.append(dot(q_t[h * HD : (h + 1) * HD], ds))
-            dv_t.append(dot(dh_t[h * HD : (h + 1) * HD], p))
+    if linked:
+        link.grads_to_core(OUT)
+
+    def attention_back(i, rows, some):
+        stage = []
+        for pair in some:
+            k, lanes = pair_spans(pair)
+            q, key, value = (qkv[k, rows, lanes[c]] for c in range(3))
+            dh = dheads[rows, pl.ds(pl.multiple_of(pair * 128, 128), 128)]
+            p = [prob_small[pair, h] if i == nb else prob[pair, i, h] for h in range(2)]
+            dp = [dot_nt(jnp.where(first if h == 0 else ~first, dh, zero), value) for h in range(2)]
+            ds = []
+            for h in range(2):
+                pf = p[h].astype(F32)
+                ds.append((pf * (dp[h] - jnp.sum(pf * dp[h], axis=-1, keepdims=True))).astype(BF))
+            stage.append((k, lanes, q, key, dh, p, ds))
+        done = []
         scale = HD ** (-0.5)
-        qkv[k, rows, lanes[0]] = (jnp.where(first, dq[0], dq[1]) * scale).astype(BF)
-        qkv[k, rows, lanes[1]] = jnp.transpose(jnp.concatenate(dk_t, axis=0) * scale).astype(BF)
-        qkv[k, rows, lanes[2]] = jnp.transpose(jnp.concatenate(dv_t, axis=0)).astype(BF)
+        for k, lanes, q, key, dh, p, ds in stage:
+            dq, dk, dv = [dot(one, key) for one in ds], [dot_tn(one, q) for one in ds], [dot_tn(one, dh) for one in p]
+            done.append((k, lanes[0], jnp.where(first, dq[0], dq[1]) * scale))
+            done.append((k, lanes[1], jnp.where(first, dk[0], dk[1]) * scale))
+            done.append((k, lanes[2], jnp.where(first, dv[0], dv[1])))
+        for k, here, value in done:
+            qkv[k, rows, here] = value.astype(BF)
 
     during = [
-        grad_events(2, FALLING[12:]) + grad_events(1, FALLING[:2]),
-        grad_events(1, FALLING[2:8]),
-        grad_events(1, FALLING[8:11]),
+        woven(grad_events(DOWN, 12, 16), outs[7:9]),
+        woven(grad_events(UP, 0, 3), outs[9:]),
+        grad_events(UP, 3, 5),
     ]
+    backs = []
     for at, (i, start, count) in enumerate(spans):
         rows = pl.ds(start, count)
-        looped(2 * pairs, lambda pair: attention_back(i, rows, pair), during[min(at, 2)] if at < 3 else [])
+        looped(
+            2,
+            lambda n: attention_back(i, rows, [n * pairs + j for j in range(pairs)]),
+            during[at] if at < 3 else [],
+        )
 
         def back_first(n):
             span = pl.ds(pl.multiple_of(n * 256, 256), 256)
@@ -644,20 +668,21 @@
             e = mid[here, :]
             xhat, r = normed(x[here, :].astype(F32))
             back_in = acc[here, :] + norm_back(e, xhat, r, vec(0))
-            cot[here, :] = back_in.astype(BF)
+            n2[here, :] = back_in.astype(BF)
             vgrad[0:1, :] += jnp.sum(e * xhat, axis=0, keepdims=True)
             vgrad[1:2, :] += jnp.sum(e, axis=0, keepdims=True)
 
         looped(count // block, norm_one_back)
-        for move in row_moves(1, start, count, at)[0]:
-            move.start()
+        mine = [row_event(1, n) for n in range(start // 64, (start + count) // 64)]
+        mine[0]()
+        backs += mine[1:]
 
     def grad_qkv(i):
         k, c = i // 3, i % 3
         span = pl.ds(pl.multiple_of(c * half, half), half)
-        w[0, k, :, span] = dot(n1t[...], qkv[k, :, span]).astype(BF)
-
-    looped(6, grad_qkv, grad_events(1, FALLING[11:]))
+        w[0, k, :, span] = dot_tn(n1[...], qkv[k, :, span]).astype(BF)
+
+    looped(6, grad_qkv, woven(grad_events(UP, 5, 8), backs[:2]))
 
     def cut_small():
         low = lax.broadcasted_iota(jnp.int32, (8, 128), 1)
@@ -701,20 +726,19 @@
         return go
 
     if linked:
-        link.grads_to_core(0)
+        link.grads_to_core(QKV)
         cut_small()
-        last_events = grad_events(0, FALLING)
         sums = [sum_step(k) for k in range(4, -2, -1)]
-        while last_events or sums:
-            if sums:
-                sums.pop(0)()
-            for event in last_events[:2]:
-                event()
-            last_events = last_events[2:]
+        first_half = woven(grad_events(UP, 8, 16), grad_events(OUT, 0, 12), grad_events(QKV, 0, 5), sums[:3], backs[2:5])
+        second = woven(grad_events(OUT, 12, 16) + grad_events(QKV, 5, 16), sums[3:], backs[5:])
+        for event in first_half + second:
+            event()
         vshare[...] = small_sum[0]
-        for g in range(3):
-            link.grads_sent(g)
+        for n in range(4):
+            link.grads_sent(n)
     else:
+        for event in backs:
+            event()
         saves = []
         for g in range(3):
             for k in range(2):
@@ -727,16 +751,12 @@
         vshare[pl.ds(0, 8), pl.ds(0, feat)] = vgrad[...]
         for k in range(2):
             vshare[pl.ds(8 + 8 * k, 8), :] = bgrad[k]
-    for move in row_moves(0, 0, tokens, 0)[0]:
-        move.wait()
-    for at, (i, start, count) in enumerate(spans):
-        near, far = row_moves(1, start, count, at)[0][0], row_moves(1, start, count, at)[1]
-        near.wait()
-        if linked:
-            far.wait()
-
-
-AHEAD = 3
+    for kind in range(2):
+        for n in range(tokens // 64):
+            for move in row_moves(kind, n):
+                move.wait()
+
+
 VLIM = 60
 
 
@@ -745,7 +765,8 @@
     ns, sl = svis.shape[0] // parts, svis.shape[2]
     tokens = nb * bl + ns * sl
     feat = big.shape[2]
-    tiles = 2 * (wide // 256)
+    tile = wide // 3
+    tiles = 6
     pairs = feat // 128
     rows = w.shape[1] if linked else 48
     vm, hbm = pl.BlockSpec(memory_space=pltpu.VMEM), pl.BlockSpec(memory_space=pl.ANY)
@@ -770,18 +791,17 @@
             link(3, 15, rows, wide),
             pltpu.VMEM((tokens, feat), BF),
             pltpu.VMEM((tokens, feat), BF),
-            pltpu.VMEM((feat, tokens), BF),
-            pltpu.VMEM((feat, tokens), BF),
+            pltpu.VMEM((tokens, feat), BF),
             pltpu.VMEM((2, tokens, 3 * feat // 2), BF),
             pltpu.VMEM((pairs, nb, 2, bl, bl), BF),
             pltpu.VMEM((pairs, 2, ns * sl, ns * sl), BF),
             pltpu.VMEM((tokens, feat), BF),
             pltpu.VMEM((tokens, feat), F32),
             pltpu.VMEM((tokens, feat), F32),
-            pltpu.VMEM((tiles, tokens, 256), BF),
-            pltpu.VMEM((tiles, tokens, 256), BF),
+            pltpu.VMEM((tiles, tokens, tile), BF),
+            pltpu.VMEM((tiles, tokens, tile), BF),
             pltpu.VMEM((tokens, feat), BF),
-            pltpu.VMEM((feat, tokens), BF),
+            pltpu.VMEM((tokens, feat), BF),
             pltpu.VMEM((8, feat), F32),
             pltpu.VMEM((2, 8, wide), F32),
             pltpu.VMEM((8, feat), F32),
@@ -794,14 +814,14 @@
             dma((3, 2, 16)),
             dma((3, 16)),
             dma((3, 16)),
-            dma((3, 2, 15)),
-            dma((3, 2, 15)),
-            dma((3, 16)),
-            dma((3, 16)),
+            dma((4, 2, 15)),
+            dma((4, 2, 15)),
+            dma((4, 16)),
+            dma((4, 16)),
             dma((3,)),
-            dma((loads, feat // 256)),
+            dma((loads, 2)),
             dma((nb + ns,)),
-            dma((3, 2, nb + 1)),
+            dma((3, 2, tokens // 64)),
             dma((4, 5)),
         ],
         compiler_params=pltpu.CompilerParams(

time: 250 us -> 199 us (0.80)
  Pallas kernels: 232 us -> 181 us
    pallas_call x1, Pallas kernels: 226 us -> 174 us  [run_layer(): pl.pallas_call(functools.partial(layer_kernel, (nb, bl, ns, sl), linked),...]
where the time goes in v3:
time: 199 us
  Pallas kernels  181 us (91%)
  other arithmetic  10.7 us (5%)
  local copies, waits for them, and re-layouts  6.22 us (3%)
    pallas_call x1, Pallas kernels, run_layer(): pl.pallas_call(functools.partial(layer_kernel, (nb, bl, ns, sl), linked),...  174 us
    pallas_call x1, Pallas kernels, scatter_rows(): pl.pallas_call(scatter_kernel, grid=(nb,), out_shape=(jax.ShapeDtypeStruc...  6.43 us
    sub x5, other arithmetic, adam_step(): return (weight - step_rate * update, moment_one, moment_two)  6.33 us

profile of v3, /device:TPU:0, one launch (start us, length us, event | category | flops | bytes accessed | tf_op | source)
XLA Modules:
  0.0 198.7 jit_solution(17384087468904044131)
XLA Ops:
  0.7 1.3 broadcast_in_dim.6.bvis_ref
  2.0 1.1 convert_bitcast_fusion
  3.1 0.9 convert_bitcast_fusion.2
  4.0 0.9 convert.18
  4.9 0.1 copy.58
  5.0 0.1 concatenate.19
  5.1 0.8 pad_maximum_fusion.w_ref
  5.9 0.6 fusion.10.vec_ref.bias_ref
  6.5 174.5 %layer.1 = (bf16[2,640,768]{2,1,0:T(8,128)(2,1)}, bf16[2,640,768]{2,1,0:T(8,128)(2,1)}, f32[3,48,1536]{2,1,0:T(8,128)}, f32[8,128]{1,0:T(8,128)}) custom-call(bf16[4,1024,768]{2,1,0:T(8,128)(2,1)} %big_ref.1, bf16[4,256,768]{2,1,0:T(8,128)(2,1)} %small_ref.1, s32[4,1,256]{2,1,0:T(1,128)} %broadcast_in_dim.6.bvis_ref, s32[4,1,64]{2,1,0:T(1,128)} %bitcast.30, ...), custom_call_target="tpu_custom_call" | custom-call | tf_op jit(solution)/shard_map/layer/pallas_call | solution.py:777
  181.0 0.0 copy-start.1
  181.0 0.0 copy-start.2
  181.0 2.8 %slice.24 = bf16[2,512,768]{2,1,0:T(8,128)(2,1)} slice(bf16[2,640,768]{2,1,0:T(8,128)(2,1)} %get-tuple-element.28), slice={[0:2], [0:512], [0:768]} | slice | bytes 3145728 | tf_op jit(solution)/shard_map/slice | solution.py:929
  183.8 1.8 slice.25
  185.6 0.0 copy-start.5
  185.6 6.4 %scatter_rows.1 = (f32[4,1024,768]{2,1,0:T(8,128)}, f32[4,256,768]{2,1,0:T(8,128)}) custom-call(s32[4,1,256]{2,1,0:T(1,128)S(1)} %copy-done.1, s32[4,1,64]{2,1,0:T(1,128)S(1)} %bitcast.31, bf16[2,640,768]{2,1,0:T(8,128)(2,1)S(1)} %copy-done, bf16[2,640,768]{2,1,0:T(8,128)(2,1)S(1)} %copy-done), custom_call_target="tpu_custom_call" | custom-call | tf_op jit(solution)/shard_map/scatter_rows/pallas_call | solution.py:850
  192.0 0.0 copy-start.7
  192.1 0.0 copy-start.8
  192.1 0.1 reshape_squeeze.3
  192.2 2.1 %multiply_subtract_fusion.2 = (f32[48,3,384]{2,0,1:T(8,128)}, f32[48,3,384]{2,0,1:T(8,128)}, f32[48,3,384]{2,0,1:T(8,128)}) fusion(f32[48,3,384]{2,0,1:T(8,128)S(1)} %copy-done.5, f32[48,3,384]{2,1,0:T(4,128)S(1)} %reshape_squeeze.3, f32[48,3,384]{2,0,1:T(8,128)} %param.31, f32[48,3,384]{2,0,1:T(8,128)} %param.32), kind=kLoop, calls=%fused_computation.13 | loop fusion | flops 829440 | bytes 1548288 | tf_op jit(solution)/shard_map/sub | solution.py:878
  194.3 1.6 multiply_subtract_fusion.3
  196.0 0.0 copy-start.18
  196.0 1.5 multiply_subtract_fusion
  197.5 0.5 multiply_subtract_fusion.5
  198.1 0.6 multiply_subtract_fusion.4
  (37 shorter events, 0.1 us)
Async XLA Ops:
  0.7 5.2 %copy-start.17 = (f32[1,96]{1,0:T(1,128)S(1)}, f32[1,96]{1,0:T(1,128)}, u32[]{:S(2)}) copy-start(f32[1,96]{1,0:T(1,128)} %param.42) | copy-start | bytes 1156
  0.7 5.2 %copy-start.13 = (f32[6,48]{1,0:T(8,128)S(1)}, f32[6,48]{1,0:T(8,128)}, u32[]{:S(2)}) copy-start(f32[6,48]{1,0:T(8,128)} %param.45) | copy-start | bytes 3460
  181.0 4.6 %copy-start = (bf16[2,640,768]{2,1,0:T(8,128)(2,1)S(1)}, bf16[2,640,768]{2,1,0:T(8,128)(2,1)}, u32[]{:S(2)}) copy-start(bf16[2,640,768]{2,1,0:T(8,128)(2,1)} %get-tuple-element.29.brow_ref.srow_ref) | copy-start | bytes 5898244
  181.0 4.6 %copy-start.1 = (s32[4,1,256]{2,1,0:T(1,128)S(1)}, s32[4,1,256]{2,1,0:T(1,128)}, u32[]{:S(2)}) copy-start(s32[4,1,256]{2,1,0:T(1,128)} %broadcast_in_dim.6.bvis_ref) | copy-start | bytes 12292
  181.0 4.6 %copy-start.2 = (s32[4,64]{1,0:T(4,128)S(1)}, s32[4,64]{1,0:T(4,128)}, u32[]{:S(2)}) copy-start(s32[4,64]{1,0:T(4,128)} %param.27) | copy-start | bytes 3076
  185.6 6.5 %copy-start.6 = (f32[3,48,1536]{2,1,0:T(8,128)S(1)}, f32[3,48,1536]{2,1,0:T(8,128)}, u32[]{:S(2)}) copy-start(f32[3,48,1536]{2,1,0:T(8,128)} %get-tuple-element.32) | copy-start | bytes 2654212
  185.6 6.6 %copy-start.5 = (f32[48,3,384]{2,0,1:T(8,128)S(1)}, f32[48,3,384]{2,0,1:T(8,128)}, u32[]{:S(2)}) copy-start(f32[48,3,384]{2,0,1:T(8,128)} %param.30) | copy-start | bytes 663556
  192.0 2.3 %copy-start.11 = (f32[48,384]{1,0:T(8,128)S(1)}, f32[48,384]{1,0:T(8,128)}, u32[]{:S(2)}) copy-start(f32[48,384]{1,0:T(8,128)} %param.33) | copy-start | bytes 221188
  192.0 2.3 %copy-start.12 = (f32[48,384]{1,0:T(8,128)S(1)}, f32[48,384]{1,0:T(8,128)}, u32[]{:S(2)}) copy-start(f32[48,384]{1,0:T(8,128)} %param.34) | copy-start | bytes 221188
  192.0 3.9 %copy-start.3 = (f32[48,1536]{1,0:T(8,128)S(1)}, f32[48,1536]{1,0:T(8,128)}, u32[]{:S(2)}) copy-start(f32[48,1536]{1,0:T(8,128)} %param.39) | copy-start | bytes 884740
  192.0 3.9 %copy-start.4 = (f32[48,1536]{1,0:T(8,128)S(1)}, f32[48,1536]{1,0:T(8,128)}, u32[]{:S(2)}) copy-start(f32[48,1536]{1,0:T(8,128)} %param.36) | copy-start | bytes 884740
  192.0 3.9 %copy-start.7 = (f32[48,1536]{1,0:T(8,128)S(1)}, f32[48,1536]{1,0:T(8,128)}, u32[]{:S(2)}) copy-start(f32[48,1536]{1,0:T(8,128)} %param.40) | copy-start | bytes 884740
  192.1 3.9 %copy-start.8 = (f32[48,1536]{1,0:T(8,128)S(1)}, f32[48,1536]{1,0:T(8,128)}, u32[]{:S(2)}) copy-start(f32[48,1536]{1,0:T(8,128)} %param.41) | copy-start | bytes 884740
  192.1 3.9 %copy-start.9 = (f32[48,1536]{1,0:T(8,128)S(1)}, f32[48,1536]{1,0:T(8,128)}, u32[]{:S(2)}) copy-start(f32[48,1536]{1,0:T(8,128)} %param.38) | copy-start | bytes 884740
  192.1 3.9 %copy-start.10 = (f32[48,1536]{1,0:T(8,128)S(1)}, f32[48,1536]{1,0:T(8,128)}, u32[]{:S(2)}) copy-start(f32[48,1536]{1,0:T(8,128)} %param.37) | copy-start | bytes 884740
  196.0 1.5 copy-start.14
  196.0 1.5 copy-start.18
  196.0 1.5 copy-start.19
  196.0 2.1 %copy-start.15 = (f32[6,48]{1,0:T(8,128)S(1)}, f32[6,48]{1,0:T(8,128)}, u32[]{:S(2)}) copy-start(f32[6,48]{1,0:T(8,128)} %param.46) | copy-start | bytes 3460
  196.0 2.1 %copy-start.16 = (f32[6,48]{1,0:T(8,128)S(1)}, f32[6,48]{1,0:T(8,128)}, u32[]{:S(2)}) copy-start(f32[6,48]{1,0:T(8,128)} %param.47) | copy-start | bytes 3460

commit v4 on v3

--- a/solution.py
+++ b/solution.py
@@ -80,7 +80,7 @@
 
 T, PP, Q, R = (Z2, Z1, X, Y), (Z2, Z1, Y, X), (Z2, Y, X, Z1), (Y, Z2, X, Z1)
 GATHER_ORDERS = ((T, PP), (T, PP), (T, PP))
-AHEAD = 3
+AHEAD = 2
 DOWN, UP, OUT, QKV = range(4)
 SUMS = (
     (2, ((PP, 0, 768), (R, 768, 768))),
@@ -105,15 +105,14 @@
 
 
 class Links:
-    def __init__(self, piece, w, gd, from_core, from_chip, share, sems):
-        self.piece, self.w, self.gd = piece, w, gd
+    def __init__(self, rows, w, gd, from_core, from_chip, share, sems):
+        self.w, self.gd = w, gd
         self.from_core, self.from_chip, self.share = from_core, from_chip, share
         (
             self.asend, self.arecv, self.acsend, self.acrecv,
-            self.rsend, self.rrecv, self.rcsend, self.rcrecv, self.own,
+            self.rsend, self.rrecv, self.rcsend, self.rcrecv,
         ) = sems
-        _, self.rows, self.cols = piece.shape
-        self.groups = piece.shape[0]
+        self.rows, self.cols = rows, w.shape[3]
 
         self.places = {(code, core): place(code, core) for code in range(16) for core in (False, True)}
         self.spans = {at: pl.ds(pl.multiple_of(d * self.rows, self.rows), self.rows) for at, (d, _) in self.places.items()}
@@ -123,21 +122,15 @@
 
     def at(self, code, core=False):
         return self.places[code, core][1], self.spans[code, core]
-
-    def own_copy(self):
-        return [
-            pltpu.make_async_copy(self.piece.at[g], self.w.at[(g,) + self.at(0)], self.own.at[g])
-            for g in range(self.groups)
-        ]
 
     def weight_move(self, g, part, code, dim):
         span = cut_columns(GATHER_ORDERS[g], self.cols)[part][1]
         target = self.w.at[(g,) + self.at(code) + (span,)]
         return pltpu.make_async_remote_copy(
-            self.piece.at[g, :, span] if code == 0 else target,
             target,
-            self.asend.at[g, part, code ^ dim],
-            self.arecv.at[g, part, code ^ dim],
+            target,
+            self.asend.at[g],
+            self.arecv.at[g, code ^ dim],
             device_id=self.place(dim),
             device_id_type=MESH,
         )
@@ -145,42 +138,39 @@
     def weight_core_move(self, g, code, mine=True):
         target = self.w.at[(g,) + self.at(code, not mine)]
         return pltpu.make_async_remote_copy(
-            self.piece.at[g] if code == 0 and mine else target,
             target,
-            self.acsend.at[g, code],
-            self.acrecv.at[g, code],
+            target,
+            self.acsend.at[g],
+            self.acrecv.at[g],
             device_id=self.place(0, True),
             device_id_type=MESH,
         )
 
     def weight_forward(self, g, code):
+        if code:
+            target = self.w.at[(g,) + self.at(code)]
+            pltpu.make_async_remote_copy(
+                target, target, self.asend.at[g], self.arecv.at[g, code], device_id=self.place(Z1), device_id_type=MESH
+            ).wait_recv()
         for part, order in enumerate(GATHER_ORDERS[g]):
-            at = top_of(order, code)
-            if code:
-                self.weight_arrival(g, part, code, order[at]).wait_recv()
-            for dim in order[at + 1 :]:
+            for dim in order[top_of(order, code) + 1 :]:
                 self.weight_move(g, part, code, dim).start()
         self.weight_core_move(g, code).start()
 
-    def weight_arrival(self, g, part, code, dim):
-        span = cut_columns(GATHER_ORDERS[g], self.cols)[part][1]
-        target = self.w.at[(g,) + self.at(code) + (span,)]
-        return pltpu.make_async_remote_copy(
-            target, target, self.asend.at[g, part, code], self.arecv.at[g, part, code],
-            device_id=self.place(dim), device_id_type=MESH,
-        )
-
     def weights_complete(self, g):
-        for code in range(16):
-            self.weight_core_move(g, code, False).wait_recv()
+        target = self.w.at[g, 0]
+        pltpu.make_async_remote_copy(
+            target, target, self.acsend.at[g], self.acrecv.at[g], device_id=self.place(0, True), device_id_type=MESH
+        ).wait_recv()
 
     def weights_sent(self, g):
-        for part, order in enumerate(GATHER_ORDERS[g]):
-            for code in range(16):
-                for dim in order[top_of(order, code) + 1 :]:
-                    self.weight_move(g, part, code, dim).wait_send()
-        for code in range(16):
-            self.weight_core_move(g, code).wait_send()
+        for ref, send, recv in (
+            (self.from_chip.at[g], self.asend.at[g], self.arecv.at[g, 1]),
+            (self.from_core.at[g], self.acsend.at[g], self.acrecv.at[g]),
+        ):
+            pltpu.make_async_remote_copy(
+                ref, ref, send, recv, device_id=self.place(0, True), device_id_type=MESH
+            ).wait_send()
 
     def grad(self, n, code, core, start, width):
         g = SUMS[n][0]
@@ -194,7 +184,7 @@
         return pltpu.make_async_remote_copy(
             ref.at[where],
             self.from_core.at[g, code, :, pl.ds(start, width)],
-            self.rcsend.at[n, code],
+            self.rcsend.at[n],
             self.rcrecv.at[n, code],
             device_id=self.place(0, True),
             device_id_type=MESH,
@@ -208,7 +198,7 @@
         return pltpu.make_async_remote_copy(
             ref.at[where],
             self.from_chip.at[g, slot, :, pl.ds(start, width)],
-            self.rsend.at[n, part, slot],
+            self.rsend.at[n],
             self.rrecv.at[n, part, slot],
             device_id=self.place(dim),
             device_id_type=MESH,
@@ -236,11 +226,15 @@
                 self.grad_move(n, part, code, order[at], True).start()
 
     def grads_sent(self, n):
-        for code in range(16):
-            self.grad_core_move(n, code).wait_send()
-            for part, (order, _, _) in enumerate(SUMS[n][1]):
-                if code:
-                    self.grad_move(n, part, code, order[top_of(order, code)], True).wait_send()
+        g, parts = SUMS[n]
+        span = pl.ds(parts[0][1], sum(part[2] for part in parts))
+        for ref, send, recv in (
+            (self.from_chip.at[g, :, :, span], self.rsend.at[n], self.rrecv.at[n, 0, 0]),
+            (self.from_core.at[g, :, :, span], self.rcsend.at[n], self.rcrecv.at[n, 0]),
+        ):
+            pltpu.make_async_remote_copy(
+                ref, ref, send, recv, device_id=self.place(0, True), device_id_type=MESH
+            ).wait_send()
 
 
 def looped(count, body, events=()):
@@ -262,9 +256,24 @@
 def layer_kernel(
     shape,
     linked,
-    big_ref, small_ref, bvis_ref, svis_ref, bcot_ref, scot_ref, w_ref, vec_ref, bias_ref,
+    big_ref, small_ref, bvis_ref, svis_ref, bcot_ref, scot_ref, *refs,
+):
+    if linked:
+        attn_ref, up_ref, down_ref, norm_ref, up_bias_ref, *refs = refs
+    else:
+        w_ref, vec_ref, bias_ref, *refs = refs
+    run_kernel(
+        shape, linked, big_ref, small_ref, bvis_ref, svis_ref, bcot_ref, scot_ref,
+        (attn_ref, up_ref, down_ref, norm_ref, up_bias_ref) if linked else (w_ref, vec_ref, bias_ref), *refs,
+    )
+
+
+def run_kernel(
+    shape,
+    linked,
+    big_ref, small_ref, bvis_ref, svis_ref, bcot_ref, scot_ref, weight_refs,
     out_ref, back_ref, share, vshare,
-    w, gd, from_core, from_chip, x, n1, n2, qkv, prob, prob_small, heads, mid, acc, act, slope, cot, out_rows,
+    few, w, gd, from_core, from_chip, x, n1, n2, qkv, prob, prob_small, heads, mid, acc, act, slope, cot, out_rows,
     vecs, bias, vgrad, bgrad, small, small_abs, small_sum, small_in,
     asend, arecv, acsend, acrecv, rsend, rrecv, rcsend, rcrecv, own, p_sem, c_sem, o_sem, s_sem,
 ):
@@ -286,10 +295,10 @@
     strips = [(at, min(tile, feat - at)) for at in range(0, feat, tile)]
 
     cloads = [
-        pltpu.make_async_copy(bcot_ref.at[t * nb + i], cot.at[pl.ds(i * bl, bl)], c_sem.at[i]) for i in range(nb)
+        pltpu.make_async_copy(bcot_ref.at[t * nb + i], cot.at[pl.ds(i * bl, bl)], c_sem) for i in range(nb)
     ]
     cloads += [
-        pltpu.make_async_copy(scot_ref.at[t * ns + i], cot.at[pl.ds(cut + i * sl, sl)], c_sem.at[nb + i])
+        pltpu.make_async_copy(scot_ref.at[t * ns + i], cot.at[pl.ds(cut + i * sl, sl)], c_sem)
         for i in range(ns)
     ]
     big_len, small_len = big_ref.shape[1], small_ref.shape[1]
@@ -318,21 +327,33 @@
         copy.start()
 
     if linked:
+        attn_ref, up_ref, down_ref, norm_ref, up_bias_ref = weight_refs
+        stage = [
+            pltpu.make_async_copy(ref, share.at[g], own.at[g, 0]) for g, ref in ((1, up_ref), (2, down_ref))
+        ]
+        for copy in stage:
+            copy.start()
+        few[...] = jnp.zeros_like(few)
+        few[: norm_ref.shape[0], : norm_ref.shape[1]] = norm_ref[...]
+        few[6:7, : up_bias_ref.shape[1]] = up_bias_ref[...]
         link = Links(
-            w_ref, w, gd, from_core, from_chip, share, (asend, arecv, acsend, acrecv, rsend, rrecv, rcsend, rcrecv, own)
-        )
-        owns = link.own_copy()
-        for copy in owns:
-            copy.start()
+            attn_ref.shape[0], w, gd, from_core, from_chip, share,
+            (asend, arecv, acsend, acrecv, rsend, rrecv, rcsend, rcrecv),
+        )
+        w[(0,) + link.at(0)] = attn_ref[...]
+        for g in (1, 2):
+            stage[g - 1].wait()
+            w[(g,) + link.at(0)] = share[g].astype(BF)
 
         def small_place(code):
             return link.place(code >> 1, bool(code & 1))
 
-        small[0] = vec_ref[...]
+        small[0] = few[...].astype(BF)
         greet(link.place)
     else:
+        w_ref, vec_ref, bias_ref = weight_refs
         wloads = [
-            [pltpu.make_async_copy(w_ref.at[g, k], w.at[g, k], acsend.at[g, k]) for k in range(2)] for g in range(3)
+            [pltpu.make_async_copy(w_ref.at[g, k], w.at[g, k], own.at[g, k]) for k in range(2)] for g in range(3)
         ]
         for copy in sum(wloads, []):
             copy.start()
@@ -388,7 +409,7 @@
             if at + 1 < len(ploads):
                 for copy in pload(at + 1):
                     copy.start()
-            column = column_of(vis_ref[row]) - part * length
+            column = column_of(vis_ref[pl.ds(row, 1), :]) - part * length
             lane = lax.broadcasted_iota(jnp.int32, column.shape, 1)
             hot = jnp.concatenate([(column == lane + k * 128).astype(BF) for k in range(length // 128)], axis=1)
             rows = pl.ds(first_row, count)
@@ -430,7 +451,6 @@
 
     def weights_ready(g):
         if linked:
-            link.own_copy()[g].wait()
             link.weights_complete(g)
         else:
             for copy in wloads[g]:
@@ -508,8 +528,7 @@
         acc[rows_of(i), :] = middle + vec(5)
 
     looped(steps, norm_two)
-    for copy in cloads:
-        copy.wait()
+    pltpu.make_async_copy(cot, cot, c_sem).wait()
 
     weights_ready(1)
     events = weight_events[2]
@@ -528,13 +547,14 @@
         return i // per, pl.ds(pl.multiple_of((i % per) * tile, tile), tile)
 
     def up(i):
-        k, span = tile_of(i)
+        at, here = i // 2, pl.ds(pl.multiple_of(i % 2 * 256, 256), 256)
+        k, span = at // per, pl.ds(pl.multiple_of(at % per * tile + i % 2 * 256, 256), 256)
         pre = dot(n2[...], w[1, k, :, span]) + bias[k, 6:7, span]
         cdf = 0.5 * (1.0 + lax.erf(pre * 0.7071067811865476))
-        act[i] = (pre * cdf).astype(BF)
-        slope[i] = (cdf + pre * jnp.exp(-0.5 * pre * pre) * 0.3989422804014327).astype(BF)
-
-    looped(tiles, up, events[:lot])
+        act[at, :, here] = (pre * cdf).astype(BF)
+        slope[at, :, here] = (cdf + pre * jnp.exp(-0.5 * pre * pre) * 0.3989422804014327).astype(BF)
+
+    looped(tiles * 2, up, events[:lot])
 
     def grad_down(i):
         k, span = tile_of(i)
@@ -557,11 +577,11 @@
         source = (out_rows if kind == 0 else n2).at[rows]
         target = out_ref if kind == 0 else back_ref
         target = target.at[t, rows] if linked else target.at[rows]
-        near = pltpu.make_async_copy(source, target, o_sem.at[0, kind, n])
+        near = pltpu.make_async_copy(source, target, o_sem.at[0, kind])
         if not linked:
             return [near]
         far = pltpu.make_async_remote_copy(
-            source, target, o_sem.at[1, kind, n], o_sem.at[2, kind, n], device_id=link.place(Y), device_id_type=MESH
+            source, target, o_sem.at[1, kind], o_sem.at[2, kind], device_id=link.place(Y), device_id_type=MESH
         )
         return [near, far]
 
@@ -743,7 +763,7 @@
         for g in range(3):
             for k in range(2):
                 source = gd.at[k] if g == 2 else w.at[g, k]
-                saves.append(pltpu.make_async_copy(source, share.at[g, k], acsend.at[g, k]))
+                saves.append(pltpu.make_async_copy(source, share.at[g, k], own.at[g, k]))
         for copy in saves:
             copy.start()
         for copy in saves:
@@ -751,24 +771,26 @@
         vshare[pl.ds(0, 8), pl.ds(0, feat)] = vgrad[...]
         for k in range(2):
             vshare[pl.ds(8 + 8 * k, 8), :] = bgrad[k]
-    for kind in range(2):
-        for n in range(tokens // 64):
-            for move in row_moves(kind, n):
-                move.wait()
+    for kind, ref in enumerate((out_rows, n2)):
+        pltpu.make_async_copy(ref, ref, o_sem.at[0, kind]).wait()
+        if linked:
+            pltpu.make_async_remote_copy(
+                ref, ref, o_sem.at[1, kind], o_sem.at[2, kind], device_id=link.place(Y), device_id_type=MESH
+            ).wait()
 
 
 VLIM = 60
 
 
-def run_layer(linked, big, small, bvis, svis, bcot, scot, w, vectors, bias, parts, wide):
-    nb, bl = bvis.shape[0] // parts, bvis.shape[2]
-    ns, sl = svis.shape[0] // parts, svis.shape[2]
+def run_layer(linked, big, small, bvis, svis, bcot, scot, weights, parts, wide):
+    nb, bl = bvis.shape[0] // parts, bvis.shape[1]
+    ns, sl = svis.shape[0] // parts, svis.shape[1]
     tokens = nb * bl + ns * sl
     feat = big.shape[2]
     tile = wide // 3
     tiles = 6
     pairs = feat // 128
-    rows = w.shape[1] if linked else 48
+    rows = weights[0].shape[0] if linked else 48
     vm, hbm = pl.BlockSpec(memory_space=pltpu.VMEM), pl.BlockSpec(memory_space=pl.ANY)
     pair = (2, tokens, feat) if linked else (tokens, feat)
     dma = pltpu.SemaphoreType.DMA
@@ -779,12 +801,13 @@
         out_shape=(
             jax.ShapeDtypeStruct(pair, BF),
             jax.ShapeDtypeStruct(pair, BF),
-            jax.ShapeDtypeStruct((3, rows, wide) if linked else w.shape, F32 if linked else BF),
+            jax.ShapeDtypeStruct((3, rows, wide) if linked else weights[0].shape, F32 if linked else BF),
             jax.ShapeDtypeStruct((8, 128) if linked else (24, wide), F32),
         ),
-        in_specs=[hbm, hbm, vm, vm, hbm, hbm, hbm, vm, vm],
+        in_specs=[hbm, hbm, vm, vm, hbm, hbm] + ([vm, hbm, hbm, vm, vm] if linked else [hbm, vm, vm]),
         out_specs=(hbm, hbm, vm if linked else hbm, vm),
         scratch_shapes=[
+            pltpu.VMEM((16, 128), F32),
             pltpu.VMEM((3, 2, feat, wide), BF),
             pltpu.VMEM((2, feat, wide), BF),
             link(3, 16, rows, wide),
@@ -810,63 +833,25 @@
             pltpu.VMEM((2, 16, 16, 128), BF),
             pltpu.VMEM((32, 8, 128), F32),
             [pltpu.VMEM((32, 8, 128), F32), pltpu.VMEM((2, 16, 8, 128), F32)],
-            dma((3, 2, 16)),
-            dma((3, 2, 16)),
+            dma((3,)),
             dma((3, 16)),
-            dma((3, 16)),
+            dma((3,)),
+            dma((3,)),
+            dma((4,)),
             dma((4, 2, 15)),
-            dma((4, 2, 15)),
+            dma((4,)),
             dma((4, 16)),
-            dma((4, 16)),
-            dma((3,)),
+            dma((3, 2)),
             dma((loads, 2)),
-            dma((nb + ns,)),
-            dma((3, 2, tokens // 64)),
+            dma,
+            dma((3, 2)),
             dma((4, 5)),
         ],
         compiler_params=pltpu.CompilerParams(
             collective_id=0 if linked else None, has_side_effects=linked, vmem_limit_bytes=VLIM * MIB
         ),
         name="layer",
-    )(big, small, bvis, svis, bcot, scot, w, vectors, bias)
-
-
-def scatter_kernel(bvis_ref, svis_ref, brow_ref, srow_ref, big_ref, small_ref):
-    def spread(vis, rows, length):
-        hot = lax.broadcasted_iota(jnp.int32, (length, vis.shape[1]), 0) == vis
-        return dot(hot.astype(BF), rows)
-
-    big_ref[...] = spread(bvis_ref[...], brow_ref[...], big_ref.shape[0])
-    small_ref[...] = spread(svis_ref[...], srow_ref[...], small_ref.shape[0])
-
-
-def scatter_rows(bvis, svis, rows, big_len, small_len):
-    parts = rows.shape[0]
-    nb, _, bl = bvis.shape
-    ns, _, sl = svis.shape
-    feat = rows.shape[2]
-    share = nb // parts
-    first_small = share * bl // sl
-    return pl.pallas_call(
-        scatter_kernel,
-        grid=(nb,),
-        out_shape=(
-            jax.ShapeDtypeStruct((nb, big_len, feat), F32),
-            jax.ShapeDtypeStruct((ns, small_len, feat), F32),
-        ),
-        in_specs=[
-            pl.BlockSpec((None, 1, bl), lambda i: (i, 0, 0)),
-            pl.BlockSpec((None, 1, sl), lambda i: (i, 0, 0)),
-            pl.BlockSpec((None, bl, feat), lambda i: (i // share, i % share, 0)),
-            pl.BlockSpec((None, sl, feat), lambda i: (i // share, first_small + i % share, 0)),
-        ],
-        out_specs=(
-            pl.BlockSpec((None, big_len, feat), lambda i: (i, 0, 0)),
-            pl.BlockSpec((None, small_len, feat), lambda i: (i, 0, 0)),
-        ),
-        compiler_params=pltpu.CompilerParams(vmem_limit_bytes=40 * MIB),
-        name="scatter_rows",
-    )(bvis, svis, rows, rows)
+    )(big, small, bvis, svis, bcot, scot, *weights)
 
 
 def adam_step(weight, moment_one, moment_two, gradient, step_rate, decay_rate):
@@ -876,6 +861,79 @@
     fixed_two = moment_two / (1.0 - 0.999**STEP_NUMBER)
     update = fixed_one / (jnp.sqrt(fixed_two) + 1e-08) + decay_rate * weight
     return (weight - step_rate * update, moment_one, moment_two)
+
+
+def finish_kernel(bvis_ref, svis_ref, orow_ref, osmall_ref, brow_ref, bsmall_ref, share_ref, few_ref, *refs):
+    states, (bout_ref, sout_ref, big_ref, small_ref), new = refs[:18], refs[18:22], refs[22:]
+    i = pl.program_id(0)
+
+    def spread(vis, rows, length):
+        hot = lax.broadcasted_iota(jnp.int32, (length, vis.shape[1]), 0) == vis
+        return dot(hot.astype(BF), rows)
+
+    bout_ref[...] = orow_ref[...]
+    sout_ref[...] = osmall_ref[...]
+    big_ref[...] = spread(bvis_ref[pl.ds(i, 1), :], brow_ref[...], big_ref.shape[0])
+    small_ref[...] = spread(svis_ref[pl.ds(i, 1), :], bsmall_ref[...], small_ref.shape[0])
+
+    def update(at, gradient, where=...):
+        old = [ref[where] for ref in states[3 * at : 3 * at + 3]]
+        for ref, value in zip(new[3 * at :], adam_step(*old, gradient, LEARN_RATES[at], DECAYS[at])):
+            ref[where] = value
+
+    half = states[3].shape[1]
+
+    @pl.when(i == 0)
+    def _():
+        update(2, share_ref[1])
+
+    @pl.when(i == 1)
+    def _():
+        update(3, share_ref[2])
+
+    @pl.when(i == 2)
+    def _():
+        for c in range(3):
+            update(0, share_ref[0, :, c * half : (c + 1) * half], (slice(None), c, slice(None)))
+
+    @pl.when(i == 3)
+    def _():
+        update(1, share_ref[0, :, 3 * half :])
+        update(4, few_ref[6:7, : states[12].shape[1]])
+        update(5, few_ref[:6, : states[15].shape[1]])
+
+
+def finish(bvis, svis, outs, backs, share, few, states, big_len, small_len):
+    parts, _, feat = outs.shape
+    nb, bl = bvis.shape
+    ns, sl = svis.shape
+    each = nb // parts
+    first_small = each * bl // sl
+    vm = pl.BlockSpec(memory_space=pltpu.VMEM)
+    rows = [
+        pl.BlockSpec((None, bl, feat), lambda i: (lax.div(i, each), lax.rem(i, each), 0)),
+        pl.BlockSpec((None, sl, feat), lambda i: (lax.div(i, each), first_small + lax.rem(i, each), 0)),
+    ]
+    whole = [pl.BlockSpec(one.shape, lambda i, n=one.ndim: (0,) * n) for one in (share, few, *states)]
+
+    def chip(length):
+        return pl.BlockSpec((None, length, feat), lambda i: (i, 0, 0))
+
+    return pl.pallas_call(
+        finish_kernel,
+        grid=(nb,),
+        out_shape=(
+            jax.ShapeDtypeStruct((nb, bl, feat), BF),
+            jax.ShapeDtypeStruct((ns, sl, feat), BF),
+            jax.ShapeDtypeStruct((nb, big_len, feat), F32),
+            jax.ShapeDtypeStruct((ns, small_len, feat), F32),
+            *(jax.ShapeDtypeStruct(one.shape, F32) for one in states),
+        ),
+        in_specs=[vm, vm] + rows + rows + whole,
+        out_specs=(chip(bl), chip(sl), chip(big_len), chip(small_len), *whole[2:]),
+        compiler_params=pltpu.CompilerParams(vmem_limit_bytes=48 * MIB),
+        name="finish",
+    )(bvis, svis, outs, outs, backs, backs, share, few, *states)
 
 
 def on_device(
@@ -889,61 +947,40 @@
     wide = up_weight.shape[1]
     feat = big_patches.shape[2]
     parts = feat // half
-    piece = jnp.stack(
-        [
-            jnp.concatenate([qkv_weight.reshape(rows, 3 * half), out_weight], axis=1).astype(BF),
-            up_weight.astype(BF),
-            down_weight.astype(BF),
-        ]
-    )
-    bvis, svis = big_visible[:, None, :], small_visible[:, None, :]
-    chips = (big_patches, small_patches, bvis, svis, big_cot, small_cot)
+    chips = (big_patches, small_patches, big_visible, small_visible, big_cot, small_cot)
+    attn = jnp.concatenate([qkv_weight.reshape(rows, 3 * half), out_weight], axis=1).astype(BF)
     if special:
-        few = jnp.concatenate(
-            [
-                jnp.pad(norm_vectors, ((0, 0), (0, 128 - norm_vectors.shape[1]))),
-                jnp.pad(up_bias, ((0, 9), (0, 128 - up_bias.shape[1]))),
-            ]
-        ).astype(BF)
-        out_both, back_both, share, vshare = run_layer(True, *chips, piece, few, few, parts, wide)
-        norm_share = vshare[:6, : norm_vectors.shape[1]]
-        bias_share = vshare[6:7, : up_bias.shape[1]]
+        weights = (attn, up_weight, down_weight, norm_vectors, up_bias)
+        outs, backs, share, few = run_layer(True, *chips, weights, parts, wide)
     else:
+        piece = jnp.stack([attn, up_weight.astype(BF), down_weight.astype(BF)])
         w = lax.all_gather(lax.all_gather(piece, "dp", axis=1, tiled=True), "tensor", axis=1)
         vectors = lax.all_gather(norm_vectors.astype(BF), "dp", axis=1, tiled=True).astype(F32)
         bias = lax.all_gather(up_bias.astype(BF), "dp", axis=1, tiled=True)
         bias = lax.all_gather(bias, "tensor", axis=0).astype(F32)
-        out_rows, back_rows, grads, few = run_layer(
-            False, *chips, w, jnp.pad(vectors, ((0, 2), (0, 0))), jnp.pad(bias, ((0, 0), (6, 1), (0, 0))), parts, wide
-        )
+        weights = (w, jnp.pad(vectors, ((0, 2), (0, 0))), jnp.pad(bias, ((0, 0), (6, 1), (0, 0))))
+        out_rows, back_rows, grads, few = run_layer(False, *chips, weights, parts, wide)
         share = lax.psum_scatter(grads, "tensor", scatter_dimension=1)
         share = lax.psum_scatter(share, "dp", scatter_dimension=1, tiled=True).astype(F32)
         both = lax.all_gather(jnp.stack([out_rows, back_rows]), "tensor", axis=1)
-        out_both, back_both = both[0], both[1]
+        outs, backs = both[0], both[1]
         norm_share = lax.psum_scatter(lax.psum(few[:6, :feat], "tensor"), "dp", scatter_dimension=1, tiled=True)
         bias_share = lax.psum_scatter(few[14::8], "tensor", scatter_dimension=0, tiled=True)
         bias_share = lax.psum_scatter(bias_share, "dp", scatter_dimension=1, tiled=True)
-    big_count, big_len = big_visible.shape
-    small_count, small_len = small_visible.shape
-    cut = big_count // parts * big_len
-    big_out = out_both[:, :cut].reshape(big_count, big_len, feat)
-    small_out = out_both[:, cut:].reshape(small_count, small_len, feat)
-    big_grad, small_grad = scatter_rows(bvis, svis, back_both, big_patches.shape[1], small_patches.shape[1])
-
-    qkv_share = share[0, :, : 3 * half].reshape(rows, 3, half)
-    new = []
-    for at, (weight, one, two, gradient) in enumerate(
-        (
-            (qkv_weight, qkv_first, qkv_second, qkv_share),
-            (out_weight, out_first, out_second, share[0, :, 3 * half :]),
-            (up_weight, up_first, up_second, share[1]),
-            (down_weight, down_first, down_second, share[2]),
-            (up_bias, up_bias_first, up_bias_second, bias_share),
-            (norm_vectors, norm_first, norm_second, norm_share),
-        )
-    ):
-        new.extend(adam_step(weight, one, two, gradient, LEARN_RATES[at], DECAYS[at]))
-    return (big_out, small_out, big_grad, small_grad, *new)
+        few = jnp.concatenate(
+            [
+                jnp.pad(norm_share, ((0, 0), (0, 128 - norm_share.shape[1]))),
+                jnp.pad(bias_share, ((0, 1), (0, 128 - bias_share.shape[1]))),
+            ]
+        )
+    states = (
+        qkv_weight, qkv_first, qkv_second, out_weight, out_first, out_second,
+        up_weight, up_first, up_second, down_weight, down_first, down_second,
+        up_bias, up_bias_first, up_bias_second, norm_vectors, norm_first, norm_second,
+    )
+    return finish(
+        big_visible, small_visible, outs, backs, share, few, states, big_patches.shape[1], small_patches.shape[1]
+    )
 
 
 def solution(mesh):

time: 199 us -> 188 us (0.945)
  other arithmetic: 10.7 us -> 2.56 us
  Pallas kernels: 181 us -> 178 us
    sub x5 -> x0, other arithmetic: 6.33 us -> none  [adam_step(): return (weight - step_rate * update, moment_one, moment_two)]
    pallas_call x1, Pallas kernels: 174 us -> 168 us  [run_layer(): pl.pallas_call(functools.partial(layer_kernel, (nb, bl, ns, sl), linked),...]
    slice x3 -> x0, local copies, waits for them, and re-layouts: 4.57 us -> none  [the longest x1 2.79 us: on_device(): big_out = out_both[:, :cut].reshape(big_count, big_len, feat)]
    unnamed x40 -> x43, local copies, waits for them, and re-layouts: 0.11 us -> 4.17 us
    pallas_call x1, Pallas kernels: 6.43 us -> 9.54 us  [finish(): pl.pallas_call(finish_kernel, grid=(nb,), out_shape=(jax.ShapeDtypeStruct...]
    pallas_call x0 -> x3, local copies, waits for them, and re-layouts: none -> 2.1 us  [finish(): pl.pallas_call(finish_kernel, grid=(nb,), out_shape=(jax.ShapeDtypeStruct...]
where the time goes in v4:
time: 188 us
  Pallas kernels  178 us (95%)
  local copies, waits for them, and re-layouts  6.28 us (3%)
  other arithmetic  2.56 us (1%)
    pallas_call x1, Pallas kernels, run_layer(): pl.pallas_call(functools.partial(layer_kernel, (nb, bl, ns, sl), linked),...  168 us
    pallas_call x1, Pallas kernels, finish(): pl.pallas_call(finish_kernel, grid=(nb,), out_shape=(jax.ShapeDtypeStruct...  9.54 us
    unnamed x43, local copies, waits for them, and re-layouts  4.17 us

profile of v4, /device:TPU:0, one launch (start us, length us, event | category | flops | bytes accessed | tf_op | source)
XLA Modules:
  0.0 187.6 jit_solution(12684672143773921707)
XLA Ops:
  0.7 0.0 copy-start.19
  0.7 0.9 convert.8
  1.6 0.9 convert_bitcast_fusion
  2.6 0.7 pad_maximum_fusion.refs_0_
  3.2 1.1 copy.55.refs_1_
  4.3 1.1 copy.56.refs_2_
  5.4 0.1 copy.54.refs_0_
  5.5 0.0 copy-start
  5.5 0.0 copy-start.1
  5.5 0.0 copy-start.4
  5.5 0.0 copy-start.5
  5.6 0.0 copy-start.8
  5.6 0.0 copy-start.9
  5.6 0.0 copy-start.10
  5.6 0.0 copy-start.11
  5.7 0.0 copy-start.14
  5.7 0.0 copy-start.16
  5.7 168.2 %layer.1 = (bf16[2,640,768]{2,1,0:T(8,128)(2,1)}, bf16[2,640,768]{2,1,0:T(8,128)(2,1)}, f32[3,48,1536]{2,1,0:T(8,128)}, f32[8,128]{1,0:T(8,128)}) custom-call(bf16[4,1024,768]{2,1,0:T(8,128)(2,1)} %big_ref.1, bf16[4,256,768]{2,1,0:T(8,128)(2,1)} %small_ref.1, s32[4,256]{1,0:T(4,128)} %bvis_ref.3, s32[4,64]{1,0:T(4,128)} %svis_ref.3, ...), custom_call_target="tpu_custom_call" | custom-call | tf_op jit(solution)/shard_map/layer/pallas_call | solution.py:799
  174.1 1.2 copy-done.2
  175.2 0.7 copy-done.15
  175.9 9.5 %finish.1 = (bf16[4,256,768]{2,1,0:T(8,128)(2,1)}, bf16[4,64,768]{2,1,0:T(8,128)(2,1)}, f32[4,1024,768]{2,1,0:T(8,128)}, f32[4,256,768]{2,1,0:T(8,128)}, f32[48,...) custom-call(s32[4,256]{1,0:T(4,128)S(1)} %copy-done.10, ...), custom_call_target="tpu_custom_call" | custom-call | tf_op jit(solution)/shard_map/finish/pallas_call | solution.py:922
  185.5 0.7 copy.57
  186.2 0.7 copy.58
  186.9 0.7 copy.59
  (28 shorter events, 0.1 us)
Async XLA Ops:
  0.7 4.7 %copy-start.19 = (f32[48,3,384]{2,0,1:T(8,128)S(1)}, f32[48,3,384]{2,0,1:T(8,128)}, u32[]{:S(2)}) copy-start(f32[48,3,384]{2,0,1:T(8,128)} %param.30) | copy-start | bytes 663556
  5.5 168.4 %copy-start = (f32[48,1536]{1,0:T(8,128)S(1)}, f32[48,1536]{1,0:T(8,128)}, u32[]{:S(2)}) copy-start(f32[48,1536]{1,0:T(8,128)} %refs_6_.1) | copy-start | bytes 884740
  5.5 168.4 %copy-start.1 = (f32[48,1536]{1,0:T(8,128)S(1)}, f32[48,1536]{1,0:T(8,128)}, u32[]{:S(2)}) copy-start(f32[48,1536]{1,0:T(8,128)} %refs_9_.1) | copy-start | bytes 884740
  5.5 168.4 %copy-start.3 = (f32[48,1536]{1,0:T(8,128)S(1)}, f32[48,1536]{1,0:T(8,128)}, u32[]{:S(2)}) copy-start(f32[48,1536]{1,0:T(8,128)} %refs_7_.1) | copy-start | bytes 884740
  5.5 168.4 %copy-start.4 = (f32[48,1536]{1,0:T(8,128)S(1)}, f32[48,1536]{1,0:T(8,128)}, u32[]{:S(2)}) copy-start(f32[48,1536]{1,0:T(8,128)} %refs_8_.1) | copy-start | bytes 884740
  5.5 168.4 %copy-start.5 = (f32[48,1536]{1,0:T(8,128)S(1)}, f32[48,1536]{1,0:T(8,128)}, u32[]{:S(2)}) copy-start(f32[48,1536]{1,0:T(8,128)} %refs_10_.1) | copy-start | bytes 884740
  5.6 168.4 %copy-start.6 = (f32[48,1536]{1,0:T(8,128)S(1)}, f32[48,1536]{1,0:T(8,128)}, u32[]{:S(2)}) copy-start(f32[48,1536]{1,0:T(8,128)} %refs_11_.1) | copy-start | bytes 884740
  5.6 168.4 %copy-start.7 = (f32[48,384]{1,0:T(8,128)S(1)}, f32[48,384]{1,0:T(8,128)}, u32[]{:S(2)}) copy-start(f32[48,384]{1,0:T(8,128)} %refs_3_.3) | copy-start | bytes 221188
  5.6 168.4 %copy-start.8 = (f32[48,384]{1,0:T(8,128)S(1)}, f32[48,384]{1,0:T(8,128)}, u32[]{:S(2)}) copy-start(f32[48,384]{1,0:T(8,128)} %refs_4_.3) | copy-start | bytes 221188
  5.6 168.4 %copy-start.9 = (f32[48,384]{1,0:T(8,128)S(1)}, f32[48,384]{1,0:T(8,128)}, u32[]{:S(2)}) copy-start(f32[48,384]{1,0:T(8,128)} %refs_5_.1) | copy-start | bytes 221188
  5.6 168.4 %copy-start.10 = (s32[4,256]{1,0:T(4,128)S(1)}, s32[4,256]{1,0:T(4,128)}, u32[]{:S(2)}) copy-start(s32[4,256]{1,0:T(4,128)} %bvis_ref.3) | copy-start | bytes 12292
  5.6 168.4 %copy-start.11 = (f32[6,48]{1,0:T(8,128)S(1)}, f32[6,48]{1,0:T(8,128)}, u32[]{:S(2)}) copy-start(f32[6,48]{1,0:T(8,128)} %refs_15_.1) | copy-start | bytes 3460
  5.6 168.4 %copy-start.12 = (s32[4,64]{1,0:T(4,128)S(1)}, s32[4,64]{1,0:T(4,128)}, u32[]{:S(2)}) copy-start(s32[4,64]{1,0:T(4,128)} %svis_ref.3) | copy-start | bytes 3076
  5.6 168.4 %copy-start.13 = (f32[6,48]{1,0:T(8,128)S(1)}, f32[6,48]{1,0:T(8,128)}, u32[]{:S(2)}) copy-start(f32[6,48]{1,0:T(8,128)} %refs_16_.1) | copy-start | bytes 3460
  5.7 168.4 %copy-start.14 = (f32[6,48]{1,0:T(8,128)S(1)}, f32[6,48]{1,0:T(8,128)}, u32[]{:S(2)}) copy-start(f32[6,48]{1,0:T(8,128)} %refs_17_.1) | copy-start | bytes 3460
  5.7 168.4 %copy-start.16 = (f32[1,96]{1,0:T(1,128)S(1)}, f32[1,96]{1,0:T(1,128)}, u32[]{:S(2)}) copy-start(f32[1,96]{1,0:T(1,128)} %refs_12_.1) | copy-start | bytes 1156
  5.7 168.4 %copy-start.17 = (f32[1,96]{1,0:T(1,128)S(1)}, f32[1,96]{1,0:T(1,128)}, u32[]{:S(2)}) copy-start(f32[1,96]{1,0:T(1,128)} %refs_13_.1) | copy-start | bytes 1156
  5.7 168.4 %copy-start.18 = (f32[1,96]{1,0:T(1,128)S(1)}, f32[1,96]{1,0:T(1,128)}, u32[]{:S(2)}) copy-start(f32[1,96]{1,0:T(1,128)} %refs_14_.1) | copy-start | bytes 1156
  174.1 1.2 copy-start.2
  175.2 0.7 copy-start.15

commit v5 on v4

--- a/solution.py
+++ b/solution.py
@@ -39,7 +39,10 @@
     for dim in DIMS:
         pl.semaphore_signal(barrier, inc=1, device_id=place(dim), device_id_type=MESH)
     pl.semaphore_signal(barrier, inc=1, device_id=place(0, True), device_id_type=MESH)
-    pl.semaphore_wait(barrier, 5)
+
+
+def await_greetings():
+    pl.semaphore_wait(pltpu.get_barrier_semaphore(), 5)
 
 
 def bits(code):
@@ -259,12 +262,12 @@
     big_ref, small_ref, bvis_ref, svis_ref, bcot_ref, scot_ref, *refs,
 ):
     if linked:
-        attn_ref, up_ref, down_ref, norm_ref, up_bias_ref, *refs = refs
+        qkv_ref, mix_ref, up_ref, down_ref, norm_ref, up_bias_ref, *refs = refs
     else:
         w_ref, vec_ref, bias_ref, *refs = refs
     run_kernel(
         shape, linked, big_ref, small_ref, bvis_ref, svis_ref, bcot_ref, scot_ref,
-        (attn_ref, up_ref, down_ref, norm_ref, up_bias_ref) if linked else (w_ref, vec_ref, bias_ref), *refs,
+        (qkv_ref, mix_ref, up_ref, down_ref, norm_ref, up_bias_ref) if linked else (w_ref, vec_ref, bias_ref), *refs,
     )
 
 
@@ -327,20 +330,28 @@
         copy.start()
 
     if linked:
-        attn_ref, up_ref, down_ref, norm_ref, up_bias_ref = weight_refs
+        qkv_ref, mix_ref, up_ref, down_ref, norm_ref, up_bias_ref = weight_refs
+        greet(place)
         stage = [
             pltpu.make_async_copy(ref, share.at[g], own.at[g, 0]) for g, ref in ((1, up_ref), (2, down_ref))
         ]
-        for copy in stage:
+        heads_in = [
+            pltpu.make_async_copy(qkv_ref.at[c], share.at[0, :, pl.ds(c * half, half)], own.at[0, c % 2]) for c in range(3)
+        ]
+        heads_in.append(pltpu.make_async_copy(mix_ref, share.at[0, :, pl.ds(3 * half, half)], own.at[0, 1]))
+        for copy in heads_in + stage:
             copy.start()
         few[...] = jnp.zeros_like(few)
         few[: norm_ref.shape[0], : norm_ref.shape[1]] = norm_ref[...]
         few[6:7, : up_bias_ref.shape[1]] = up_bias_ref[...]
         link = Links(
-            attn_ref.shape[0], w, gd, from_core, from_chip, share,
+            mix_ref.shape[0], w, gd, from_core, from_chip, share,
             (asend, arecv, acsend, acrecv, rsend, rrecv, rcsend, rcrecv),
         )
-        w[(0,) + link.at(0)] = attn_ref[...]
+        for k in range(2):
+            both = share.at[0, :, pl.ds(0, 2 * half)]
+            pltpu.make_async_copy(both, both, own.at[0, k]).wait()
+        w[(0,) + link.at(0)] = share[0].astype(BF)
         for g in (1, 2):
             stage[g - 1].wait()
             w[(g,) + link.at(0)] = share[g].astype(BF)
@@ -349,7 +360,7 @@
             return link.place(code >> 1, bool(code & 1))
 
         small[0] = few[...].astype(BF)
-        greet(link.place)
+        await_greetings()
     else:
         w_ref, vec_ref, bias_ref = weight_refs
         wloads = [
@@ -790,7 +801,7 @@
     tile = wide // 3
     tiles = 6
     pairs = feat // 128
-    rows = weights[0].shape[0] if linked else 48
+    rows = weights[1].shape[0] if linked else 48
     vm, hbm = pl.BlockSpec(memory_space=pltpu.VMEM), pl.BlockSpec(memory_space=pl.ANY)
     pair = (2, tokens, feat) if linked else (tokens, feat)
     dma = pltpu.SemaphoreType.DMA
@@ -804,7 +815,7 @@
             jax.ShapeDtypeStruct((3, rows, wide) if linked else weights[0].shape, F32 if linked else BF),
             jax.ShapeDtypeStruct((8, 128) if linked else (24, wide), F32),
         ),
-        in_specs=[hbm, hbm, vm, vm, hbm, hbm] + ([vm, hbm, hbm, vm, vm] if linked else [hbm, vm, vm]),
+        in_specs=[hbm, hbm, vm, vm, hbm, hbm] + ([hbm] * 4 + [vm, vm] if linked else [hbm, vm, vm]),
         out_specs=(hbm, hbm, vm if linked else hbm, vm),
         scratch_shapes=[
             pltpu.VMEM((16, 128), F32),
@@ -894,7 +905,7 @@
     @pl.when(i == 2)
     def _():
         for c in range(3):
-            update(0, share_ref[0, :, c * half : (c + 1) * half], (slice(None), c, slice(None)))
+            update(0, share_ref[0, :, c * half : (c + 1) * half], c)
 
     @pl.when(i == 3)
     def _():
@@ -948,11 +959,11 @@
     feat = big_patches.shape[2]
     parts = feat // half
     chips = (big_patches, small_patches, big_visible, small_visible, big_cot, small_cot)
-    attn = jnp.concatenate([qkv_weight.reshape(rows, 3 * half), out_weight], axis=1).astype(BF)
     if special:
-        weights = (attn, up_weight, down_weight, norm_vectors, up_bias)
+        weights = (jnp.swapaxes(qkv_weight, 0, 1), out_weight, up_weight, down_weight, norm_vectors, up_bias)
         outs, backs, share, few = run_layer(True, *chips, weights, parts, wide)
     else:
+        attn = jnp.concatenate([qkv_weight.reshape(rows, 3 * half), out_weight], axis=1).astype(BF)
         piece = jnp.stack([attn, up_weight.astype(BF), down_weight.astype(BF)])
         w = lax.all_gather(lax.all_gather(piece, "dp", axis=1, tiled=True), "tensor", axis=1)
         vectors = lax.all_gather(norm_vectors.astype(BF), "dp", axis=1, tiled=True).astype(F32)
@@ -974,13 +985,14 @@
             ]
         )
     states = (
-        qkv_weight, qkv_first, qkv_second, out_weight, out_first, out_second,
+        *(jnp.swapaxes(one, 0, 1) for one in (qkv_weight, qkv_first, qkv_second)), out_weight, out_first, out_second,
         up_weight, up_first, up_second, down_weight, down_first, down_second,
         up_bias, up_bias_first, up_bias_second, norm_vectors, norm_first, norm_second,
     )
-    return finish(
+    done = finish(
         big_visible, small_visible, outs, backs, share, few, states, big_patches.shape[1], small_patches.shape[1]
     )
+    return (*done[:4], *(jnp.swapaxes(one, 0, 1) for one in done[4:7]), *done[7:])
 
 
 def solution(mesh):

time: 188 us -> 181 us (0.963)
  local copies, waits for them, and re-layouts: 6.28 us -> 3.46 us
  other arithmetic: 2.56 us -> 0 us
  Pallas kernels: 178 us -> 176 us
    pallas_call x3 -> x0, local copies, waits for them, and re-layouts: 2.1 us -> none  [finish(): pl.pallas_call(finish_kernel, grid=(nb,), out_shape=(jax.ShapeDtypeStruct...]
    unnamed x43 -> x46, local copies, waits for them, and re-layouts: 4.17 us -> 3.46 us
where the time goes in v5:
time: 181 us
  Pallas kernels  176 us (97%)
  local copies, waits for them, and re-layouts  3.46 us (2%)
    pallas_call x1, Pallas kernels, run_layer(): pl.pallas_call(functools.partial(layer_kernel, (nb, bl, ns, sl), linked),...  167 us
    pallas_call x1, Pallas kernels, finish(): pl.pallas_call(finish_kernel, grid=(nb,), out_shape=(jax.ShapeDtypeStruct...  9.11 us

profile of v5, /device:TPU:0, one launch (start us, length us, event | category | flops | bytes accessed | tf_op | source)
XLA Modules:
  0.0 180.7 jit_solution(3769765052280074080)
XLA Ops:
  0.7 0.0 copy-start.1
  0.7 0.0 copy-start.2
  0.7 0.0 copy-start.3
  0.7 0.0 copy-start.5
  0.7 0.0 copy-start.6
  0.7 0.0 copy-start.7
  0.7 0.0 copy-start.8
  0.7 0.0 copy-start.9
  0.7 0.0 copy-start.10
  0.8 0.0 copy-start.11
  0.8 0.0 copy-start.12
  0.8 0.0 copy-start.13
  0.8 0.0 copy-start.14
  0.8 0.0 copy-start.15
  0.8 0.0 copy-start.16
  0.8 0.0 copy-start.17
  0.8 0.0 copy-start.18
  0.8 0.0 copy-start.20
  0.8 0.0 copy-start.21
  0.9 166.9 %layer.1 = (bf16[2,640,768]{2,1,0:T(8,128)(2,1)}, bf16[2,640,768]{2,1,0:T(8,128)(2,1)}, f32[3,48,1536]{2,1,0:T(8,128)}, f32[8,128]{1,0:T(8,128)}) custom-call(bf16[4,1024,768]{2,1,0:T(8,128)(2,1)} %big_ref.1, bf16[4,256,768]{2,1,0:T(8,128)(2,1)} %small_ref.1, s32[4,256]{1,0:T(4,128)} %bvis_ref.3, s32[4,64]{1,0:T(4,128)} %svis_ref.3, ...), custom_call_target="tpu_custom_call" | custom-call | tf_op jit(solution)/shard_map/layer/pallas_call | solution.py:810
  168.0 1.5 copy-done
  169.6 1.2 copy-done.4
  170.7 0.7 copy-done.19
  171.4 9.1 %finish.1 = (bf16[4,256,768]{2,1,0:T(8,128)(2,1)}, bf16[4,64,768]{2,1,0:T(8,128)(2,1)}, f32[4,1024,768]{2,1,0:T(8,128)}, f32[4,256,768]{2,1,0:T(8,128)}, f32[3,4...) custom-call(s32[4,256]{1,0:T(4,128)S(1)} %copy-done.14, ...), custom_call_target="tpu_custom_call" | custom-call | tf_op jit(solution)/shard_map/finish/pallas_call | solution.py:933
  (24 shorter events, 0.0 us)
Async XLA Ops:
  0.7 167.1 %copy-start.1 = (f32[48,1536]{1,0:T(8,128)S(1)}, f32[48,1536]{1,0:T(8,128)}, u32[]{:S(2)}) copy-start(f32[48,1536]{1,0:T(8,128)} %refs_6_.1) | copy-start | bytes 884740
  0.7 167.1 %copy-start.2 = (f32[48,1536]{1,0:T(8,128)S(1)}, f32[48,1536]{1,0:T(8,128)}, u32[]{:S(2)}) copy-start(f32[48,1536]{1,0:T(8,128)} %refs_9_.1) | copy-start | bytes 884740
  0.7 167.1 %copy-start.3 = (f32[48,3,384]{2,0,1:T(8,128)S(1)}, f32[48,3,384]{2,0,1:T(8,128)}, u32[]{:S(2)}) copy-start(f32[48,3,384]{2,0,1:T(8,128)} %param.30) | copy-start | bytes 663556
  0.7 167.1 %copy-start.5 = (f32[48,1536]{1,0:T(8,128)S(1)}, f32[48,1536]{1,0:T(8,128)}, u32[]{:S(2)}) copy-start(f32[48,1536]{1,0:T(8,128)} %refs_7_.1) | copy-start | bytes 884740
  0.7 167.1 %copy-start.6 = (f32[48,1536]{1,0:T(8,128)S(1)}, f32[48,1536]{1,0:T(8,128)}, u32[]{:S(2)}) copy-start(f32[48,1536]{1,0:T(8,128)} %refs_8_.1) | copy-start | bytes 884740
  0.7 167.1 %copy-start.7 = (f32[48,1536]{1,0:T(8,128)S(1)}, f32[48,1536]{1,0:T(8,128)}, u32[]{:S(2)}) copy-start(f32[48,1536]{1,0:T(8,128)} %refs_10_.1) | copy-start | bytes 884740
  0.7 167.1 %copy-start.8 = (f32[48,1536]{1,0:T(8,128)S(1)}, f32[48,1536]{1,0:T(8,128)}, u32[]{:S(2)}) copy-start(f32[48,1536]{1,0:T(8,128)} %refs_11_.1) | copy-start | bytes 884740
  0.7 167.1 %copy-start.9 = (f32[48,384]{1,0:T(8,128)S(1)}, f32[48,384]{1,0:T(8,128)}, u32[]{:S(2)}) copy-start(f32[48,384]{1,0:T(8,128)} %refs_3_.3) | copy-start | bytes 221188
  0.7 167.1 %copy-start.10 = (f32[48,3,384]{2,0,1:T(8,128)S(1)}, f32[48,3,384]{2,0,1:T(8,128)}, u32[]{:S(2)}) copy-start(f32[48,3,384]{2,0,1:T(8,128)} %param.31) | copy-start | bytes 663556
  0.8 167.1 %copy-start.11 = (f32[48,3,384]{2,0,1:T(8,128)S(1)}, f32[48,3,384]{2,0,1:T(8,128)}, u32[]{:S(2)}) copy-start(f32[48,3,384]{2,0,1:T(8,128)} %param.32) | copy-start | bytes 663556
  0.8 167.1 %copy-start.12 = (f32[48,384]{1,0:T(8,128)S(1)}, f32[48,384]{1,0:T(8,128)}, u32[]{:S(2)}) copy-start(f32[48,384]{1,0:T(8,128)} %refs_4_.3) | copy-start | bytes 221188
  0.8 167.1 %copy-start.13 = (f32[48,384]{1,0:T(8,128)S(1)}, f32[48,384]{1,0:T(8,128)}, u32[]{:S(2)}) copy-start(f32[48,384]{1,0:T(8,128)} %refs_5_.3) | copy-start | bytes 221188
  0.8 167.1 %copy-start.14 = (s32[4,256]{1,0:T(4,128)S(1)}, s32[4,256]{1,0:T(4,128)}, u32[]{:S(2)}) copy-start(s32[4,256]{1,0:T(4,128)} %bvis_ref.3) | copy-start | bytes 12292
  0.8 167.1 %copy-start.15 = (f32[6,48]{1,0:T(8,128)S(1)}, f32[6,48]{1,0:T(8,128)}, u32[]{:S(2)}) copy-start(f32[6,48]{1,0:T(8,128)} %refs_15_.1) | copy-start | bytes 3460
  0.8 167.1 %copy-start.16 = (s32[4,64]{1,0:T(4,128)S(1)}, s32[4,64]{1,0:T(4,128)}, u32[]{:S(2)}) copy-start(s32[4,64]{1,0:T(4,128)} %svis_ref.3) | copy-start | bytes 3076
  0.8 167.1 %copy-start.17 = (f32[6,48]{1,0:T(8,128)S(1)}, f32[6,48]{1,0:T(8,128)}, u32[]{:S(2)}) copy-start(f32[6,48]{1,0:T(8,128)} %refs_16_.1) | copy-start | bytes 3460
  0.8 167.1 %copy-start.18 = (f32[6,48]{1,0:T(8,128)S(1)}, f32[6,48]{1,0:T(8,128)}, u32[]{:S(2)}) copy-start(f32[6,48]{1,0:T(8,128)} %refs_17_.1) | copy-start | bytes 3460
  0.8 167.1 %copy-start.20 = (f32[1,96]{1,0:T(1,128)S(1)}, f32[1,96]{1,0:T(1,128)}, u32[]{:S(2)}) copy-start(f32[1,96]{1,0:T(1,128)} %refs_12_.1) | copy-start | bytes 1156
  0.8 167.1 %copy-start.21 = (f32[1,96]{1,0:T(1,128)S(1)}, f32[1,96]{1,0:T(1,128)}, u32[]{:S(2)}) copy-start(f32[1,96]{1,0:T(1,128)} %refs_13_.1) | copy-start | bytes 1156
  0.9 167.1 %copy-start.22 = (f32[1,96]{1,0:T(1,128)S(1)}, f32[1,96]{1,0:T(1,128)}, u32[]{:S(2)}) copy-start(f32[1,96]{1,0:T(1,128)} %refs_14_.1) | copy-start | bytes 1156
  168.0 1.5 copy-start
  169.6 1.2 copy-start.4
  170.7 0.7 copy-start.19

commit v6 on v5

--- a/solution.py
+++ b/solution.py
@@ -503,22 +503,27 @@
 
     def attention(pair):
         k, lanes = pair_spans(pair)
+        stage = []
         for i, start, count in spans:
             rows = pl.ds(start, count)
             q, key, value = (qkv[k, rows, lanes[c]] for c in range(3))
-            mixed = []
+            scores = [dot_nt(jnp.where(first if h == 0 else ~first, q, zero), key) * HD ** (-0.5) for h in range(2)]
+            stage.append((i, rows, value, scores))
+        chances = []
+        for i, rows, value, scores in stage:
+            if i == nb:
+                scores = [jnp.where(same, one, -jnp.inf) for one in scores]
+            chances.append([softmax(one).astype(BF) for one in scores])
+        here = pl.ds(pl.multiple_of(pair * 128, 128), 128)
+        for (i, rows, value, _), p in zip(stage, chances):
+            mixed = [dot(one, value) for one in p]
+            heads[rows, here] = jnp.where(first, mixed[0], mixed[1]).astype(BF)
+        for (i, _, _, _), p in zip(stage, chances):
             for h in range(2):
-                q_head = jnp.where(first if h == 0 else ~first, q, zero)
-                scores = dot_nt(q_head, key) * HD ** (-0.5)
                 if i == nb:
-                    scores = jnp.where(same, scores, -jnp.inf)
-                p = softmax(scores).astype(BF)
-                if i == nb:
-                    prob_small[pair, h] = p
+                    prob_small[pair, h] = p[h]
                 else:
-                    prob[pair, i, h] = p
-                mixed.append(dot(p, value))
-            heads[rows, pl.ds(pl.multiple_of(pair * 128, 128), 128)] = jnp.where(first, mixed[0], mixed[1]).astype(BF)
+                    prob[pair, i, h] = p[h]
 
     looped(2 * pairs, attention, events[lot:])
 
@@ -636,7 +641,7 @@
         vgrad[4:5, :] += jnp.sum(back_middle, axis=0, keepdims=True)
         vgrad[5:6, :] += jnp.sum(back_out, axis=0, keepdims=True)
 
-    looped(steps, norm_two_back, woven(grad_events(DOWN, 9, 12), outs[5:7]))
+    looped(steps, norm_two_back, woven(grad_events(DOWN, 9, 12), grad_events(UP, 0, 3), outs[5:7]))
 
     dheads = heads
     for k in range(2):
@@ -672,9 +677,9 @@
             qkv[k, rows, here] = value.astype(BF)
 
     during = [
-        woven(grad_events(DOWN, 12, 16), outs[7:9]),
-        woven(grad_events(UP, 0, 3), outs[9:]),
-        grad_events(UP, 3, 5),
+        woven(grad_events(DOWN, 12, 16), grad_events(UP, 3, 6), outs[7:9]),
+        woven(grad_events(UP, 6, 9), grad_events(OUT, 0, 3), outs[9:]),
+        woven(grad_events(UP, 9, 11), grad_events(OUT, 3, 5)),
     ]
     backs = []
     for at, (i, start, count) in enumerate(spans):
@@ -682,7 +687,7 @@
         looped(
             2,
             lambda n: attention_back(i, rows, [n * pairs + j for j in range(pairs)]),
-            during[at] if at < 3 else [],
+            during[at][: len(during[at]) // 2] if at < 3 else [],
         )
 
         def back_first(n):
@@ -692,7 +697,7 @@
                 qkv[1, rows, both], w[0, 1, span, both]
             )
 
-        looped(feat // 256, back_first)
+        looped(feat // 256, back_first, during[at][len(during[at]) // 2 :] if at < 3 else [])
 
         def norm_one_back(n):
             here = pl.ds(pl.multiple_of(start + n * block, block), block)
@@ -713,7 +718,7 @@
         span = pl.ds(pl.multiple_of(c * half, half), half)
         w[0, k, :, span] = dot_tn(n1[...], qkv[k, :, span]).astype(BF)
 
-    looped(6, grad_qkv, woven(grad_events(UP, 5, 8), backs[:2]))
+    looped(6, grad_qkv, woven(grad_events(UP, 11, 13), grad_events(OUT, 5, 8), backs[:3]))
 
     def cut_small():
         low = lax.broadcasted_iota(jnp.int32, (8, 128), 1)
@@ -760,8 +765,8 @@
         link.grads_to_core(QKV)
         cut_small()
         sums = [sum_step(k) for k in range(4, -2, -1)]
-        first_half = woven(grad_events(UP, 8, 16), grad_events(OUT, 0, 12), grad_events(QKV, 0, 5), sums[:3], backs[2:5])
-        second = woven(grad_events(OUT, 12, 16) + grad_events(QKV, 5, 16), sums[3:], backs[5:])
+        first_half = grad_events(QKV, 0, 1) + woven(grad_events(UP, 13, 16), grad_events(OUT, 8, 12), grad_events(QKV, 1, 9), sums[:3], backs[3:5])
+        second = woven(grad_events(OUT, 12, 16), grad_events(QKV, 9, 16), sums[3:], backs[5:])
         for event in first_half + second:
             event()
         vshare[...] = small_sum[0]

time: 181 us -> 171 us (0.945)
  Pallas kernels: 176 us -> 166 us
    pallas_call x1, Pallas kernels: 167 us -> 157 us  [run_layer(): pl.pallas_call(functools.partial(layer_kernel, (nb, bl, ns, sl), linked),...]
where the time goes in v6:
time: 171 us; the launch traced here: 170 us
  Pallas kernels  166 us (97%)
  local copies, waits for them, and re-layouts  3.46 us (2%)
    pallas_call x1, Pallas kernels, run_layer(): pl.pallas_call(functools.partial(layer_kernel, (nb, bl, ns, sl), linked),...  157 us
    pallas_call x1, Pallas kernels, finish(): pl.pallas_call(finish_kernel, grid=(nb,), out_shape=(jax.ShapeDtypeStruct...  9.12 us
    unnamed x46, local copies, waits for them, and re-layouts  3.46 us

profile of v6, /device:TPU:0, one launch (start us, length us, event | category | flops | bytes accessed | tf_op | source)
XLA Modules:
  0.0 170.4 jit_solution(15084528690960530780)
XLA Ops:
  0.7 0.0 copy-start.1
  0.7 0.0 copy-start.2
  0.7 0.0 copy-start.3
  0.7 0.0 copy-start.5
  0.7 0.0 copy-start.6
  0.7 0.0 copy-start.7
  0.7 0.0 copy-start.8
  0.7 0.0 copy-start.9
  0.7 0.0 copy-start.10
  0.8 0.0 copy-start.11
  0.8 0.0 copy-start.12
  0.8 0.0 copy-start.13
  0.8 0.0 copy-start.14
  0.8 0.0 copy-start.15
  0.8 0.0 copy-start.16
  0.8 0.0 copy-start.17
  0.8 0.0 copy-start.18
  0.8 0.0 copy-start.20
  0.8 0.0 copy-start.21
  0.9 156.6 %layer.1 = (bf16[2,640,768]{2,1,0:T(8,128)(2,1)}, bf16[2,640,768]{2,1,0:T(8,128)(2,1)}, f32[3,48,1536]{2,1,0:T(8,128)}, f32[8,128]{1,0:T(8,128)}) custom-call(bf16[4,1024,768]{2,1,0:T(8,128)(2,1)} %big_ref.1, bf16[4,256,768]{2,1,0:T(8,128)(2,1)} %small_ref.1, s32[4,256]{1,0:T(4,128)} %bvis_ref.3, s32[4,64]{1,0:T(4,128)} %svis_ref.3, ...), custom_call_target="tpu_custom_call" | custom-call | tf_op jit(solution)/shard_map/layer/pallas_call | solution.py:815
  157.7 1.5 copy-done
  159.2 1.2 copy-done.4
  160.4 0.7 copy-done.19
  161.1 9.1 %finish.1 = (bf16[4,256,768]{2,1,0:T(8,128)(2,1)}, bf16[4,64,768]{2,1,0:T(8,128)(2,1)}, f32[4,1024,768]{2,1,0:T(8,128)}, f32[4,256,768]{2,1,0:T(8,128)}, f32[3,4...) custom-call(s32[4,256]{1,0:T(4,128)S(1)} %copy-done.14, ...), custom_call_target="tpu_custom_call" | custom-call | tf_op jit(solution)/shard_map/finish/pallas_call | solution.py:938
  (24 shorter events, 0.0 us)
Async XLA Ops:
  0.7 156.8 %copy-start.1 = (f32[48,1536]{1,0:T(8,128)S(1)}, f32[48,1536]{1,0:T(8,128)}, u32[]{:S(2)}) copy-start(f32[48,1536]{1,0:T(8,128)} %refs_6_.1) | copy-start | bytes 884740
  0.7 156.8 %copy-start.2 = (f32[48,1536]{1,0:T(8,128)S(1)}, f32[48,1536]{1,0:T(8,128)}, u32[]{:S(2)}) copy-start(f32[48,1536]{1,0:T(8,128)} %refs_9_.1) | copy-start | bytes 884740
  0.7 156.8 %copy-start.3 = (f32[48,3,384]{2,0,1:T(8,128)S(1)}, f32[48,3,384]{2,0,1:T(8,128)}, u32[]{:S(2)}) copy-start(f32[48,3,384]{2,0,1:T(8,128)} %param.30) | copy-start | bytes 663556
  0.7 156.8 %copy-start.5 = (f32[48,1536]{1,0:T(8,128)S(1)}, f32[48,1536]{1,0:T(8,128)}, u32[]{:S(2)}) copy-start(f32[48,1536]{1,0:T(8,128)} %refs_7_.1) | copy-start | bytes 884740
  0.7 156.8 %copy-start.6 = (f32[48,1536]{1,0:T(8,128)S(1)}, f32[48,1536]{1,0:T(8,128)}, u32[]{:S(2)}) copy-start(f32[48,1536]{1,0:T(8,128)} %refs_8_.1) | copy-start | bytes 884740
  0.7 156.8 %copy-start.7 = (f32[48,1536]{1,0:T(8,128)S(1)}, f32[48,1536]{1,0:T(8,128)}, u32[]{:S(2)}) copy-start(f32[48,1536]{1,0:T(8,128)} %refs_10_.1) | copy-start | bytes 884740
  0.7 156.8 %copy-start.8 = (f32[48,1536]{1,0:T(8,128)S(1)}, f32[48,1536]{1,0:T(8,128)}, u32[]{:S(2)}) copy-start(f32[48,1536]{1,0:T(8,128)} %refs_11_.1) | copy-start | bytes 884740
  0.7 156.8 %copy-start.9 = (f32[48,384]{1,0:T(8,128)S(1)}, f32[48,384]{1,0:T(8,128)}, u32[]{:S(2)}) copy-start(f32[48,384]{1,0:T(8,128)} %refs_3_.3) | copy-start | bytes 221188
  0.7 156.8 %copy-start.10 = (f32[48,3,384]{2,0,1:T(8,128)S(1)}, f32[48,3,384]{2,0,1:T(8,128)}, u32[]{:S(2)}) copy-start(f32[48,3,384]{2,0,1:T(8,128)} %param.31) | copy-start | bytes 663556
  0.8 156.8 %copy-start.11 = (f32[48,3,384]{2,0,1:T(8,128)S(1)}, f32[48,3,384]{2,0,1:T(8,128)}, u32[]{:S(2)}) copy-start(f32[48,3,384]{2,0,1:T(8,128)} %param.32) | copy-start | bytes 663556
  0.8 156.8 %copy-start.12 = (f32[48,384]{1,0:T(8,128)S(1)}, f32[48,384]{1,0:T(8,128)}, u32[]{:S(2)}) copy-start(f32[48,384]{1,0:T(8,128)} %refs_4_.3) | copy-start | bytes 221188
  0.8 156.8 %copy-start.13 = (f32[48,384]{1,0:T(8,128)S(1)}, f32[48,384]{1,0:T(8,128)}, u32[]{:S(2)}) copy-start(f32[48,384]{1,0:T(8,128)} %refs_5_.3) | copy-start | bytes 221188
  0.8 156.8 %copy-start.14 = (s32[4,256]{1,0:T(4,128)S(1)}, s32[4,256]{1,0:T(4,128)}, u32[]{:S(2)}) copy-start(s32[4,256]{1,0:T(4,128)} %bvis_ref.3) | copy-start | bytes 12292
  0.8 156.8 %copy-start.15 = (f32[6,48]{1,0:T(8,128)S(1)}, f32[6,48]{1,0:T(8,128)}, u32[]{:S(2)}) copy-start(f32[6,48]{1,0:T(8,128)} %refs_15_.1) | copy-start | bytes 3460
  0.8 156.8 %copy-start.16 = (s32[4,64]{1,0:T(4,128)S(1)}, s32[4,64]{1,0:T(4,128)}, u32[]{:S(2)}) copy-start(s32[4,64]{1,0:T(4,128)} %svis_ref.3) | copy-start | bytes 3076
  0.8 156.8 %copy-start.17 = (f32[6,48]{1,0:T(8,128)S(1)}, f32[6,48]{1,0:T(8,128)}, u32[]{:S(2)}) copy-start(f32[6,48]{1,0:T(8,128)} %refs_16_.1) | copy-start | bytes 3460
  0.8 156.8 %copy-start.18 = (f32[6,48]{1,0:T(8,128)S(1)}, f32[6,48]{1,0:T(8,128)}, u32[]{:S(2)}) copy-start(f32[6,48]{1,0:T(8,128)} %refs_17_.1) | copy-start | bytes 3460
  0.8 156.8 %copy-start.20 = (f32[1,96]{1,0:T(1,128)S(1)}, f32[1,96]{1,0:T(1,128)}, u32[]{:S(2)}) copy-start(f32[1,96]{1,0:T(1,128)} %refs_12_.1) | copy-start | bytes 1156
  0.8 156.8 %copy-start.21 = (f32[1,96]{1,0:T(1,128)S(1)}, f32[1,96]{1,0:T(1,128)}, u32[]{:S(2)}) copy-start(f32[1,96]{1,0:T(1,128)} %refs_13_.1) | copy-start | bytes 1156
  0.9 156.8 %copy-start.22 = (f32[1,96]{1,0:T(1,128)S(1)}, f32[1,96]{1,0:T(1,128)}, u32[]{:S(2)}) copy-start(f32[1,96]{1,0:T(1,128)} %refs_14_.1) | copy-start | bytes 1156
  157.7 1.5 copy-start
  159.2 1.2 copy-start.4
  160.4 0.7 copy-start.19

commit v7 on v6

--- a/solution.py
+++ b/solution.py
@@ -86,8 +86,8 @@
 AHEAD = 2
 DOWN, UP, OUT, QKV = range(4)
 SUMS = (
-    (2, ((PP, 0, 768), (R, 768, 768))),
-    (1, ((PP, 0, 768), (R, 768, 768))),
+    (2, ((PP, 0, 640), (R, 640, 896))),
+    (1, ((PP, 0, 640), (R, 640, 896))),
     (0, ((PP, 1152, 256), (R, 1408, 128))),
     (0, ((PP, 0, 512), (R, 512, 640))),
 )

time: 171 us -> 170 us (level)
  no operation moved by 1% of the time
where the time goes in v7:
time: 170 us
  Pallas kernels  165 us (97%)
  local copies, waits for them, and re-layouts  3.46 us (2%)
    pallas_call x1, Pallas kernels, run_layer(): pl.pallas_call(functools.partial(layer_kernel, (nb, bl, ns, sl), linked),...  156 us
    pallas_call x1, Pallas kernels, finish(): pl.pallas_call(finish_kernel, grid=(nb,), out_shape=(jax.ShapeDtypeStruct...  9.1 us
    unnamed x46, local copies, waits for them, and re-layouts  3.46 us

profile of v7, /device:TPU:0, one launch (start us, length us, event | category | flops | bytes accessed | tf_op | source)
XLA Modules:
  0.0 169.9 jit_solution(2144857093167051138)
XLA Ops:
  0.7 0.0 copy-start.1
  0.7 0.0 copy-start.2
  0.7 0.0 copy-start.3
  0.7 0.0 copy-start.5
  0.7 0.0 copy-start.6
  0.7 0.0 copy-start.7
  0.7 0.0 copy-start.8
  0.7 0.0 copy-start.9
  0.7 0.0 copy-start.10
  0.8 0.0 copy-start.11
  0.8 0.0 copy-start.12
  0.8 0.0 copy-start.13
  0.8 0.0 copy-start.14
  0.8 0.0 copy-start.15
  0.8 0.0 copy-start.16
  0.8 0.0 copy-start.17
  0.8 0.0 copy-start.18
  0.8 0.0 copy-start.20
  0.8 0.0 copy-start.21
  0.9 156.1 %layer.1 = (bf16[2,640,768]{2,1,0:T(8,128)(2,1)}, bf16[2,640,768]{2,1,0:T(8,128)(2,1)}, f32[3,48,1536]{2,1,0:T(8,128)}, f32[8,128]{1,0:T(8,128)}) custom-call(bf16[4,1024,768]{2,1,0:T(8,128)(2,1)} %big_ref.1, bf16[4,256,768]{2,1,0:T(8,128)(2,1)} %small_ref.1, s32[4,256]{1,0:T(4,128)} %bvis_ref.3, s32[4,64]{1,0:T(4,128)} %svis_ref.3, ...), custom_call_target="tpu_custom_call" | custom-call | tf_op jit(solution)/shard_map/layer/pallas_call | solution.py:815
  157.2 1.5 copy-done
  158.8 1.2 copy-done.4
  159.9 0.7 copy-done.19
  160.6 9.1 %finish.1 = (bf16[4,256,768]{2,1,0:T(8,128)(2,1)}, bf16[4,64,768]{2,1,0:T(8,128)(2,1)}, f32[4,1024,768]{2,1,0:T(8,128)}, f32[4,256,768]{2,1,0:T(8,128)}, f32[3,4...) custom-call(s32[4,256]{1,0:T(4,128)S(1)} %copy-done.14, ...), custom_call_target="tpu_custom_call" | custom-call | tf_op jit(solution)/shard_map/finish/pallas_call | solution.py:938
  (24 shorter events, 0.0 us)
Async XLA Ops:
  0.7 156.4 %copy-start.1 = (f32[48,1536]{1,0:T(8,128)S(1)}, f32[48,1536]{1,0:T(8,128)}, u32[]{:S(2)}) copy-start(f32[48,1536]{1,0:T(8,128)} %refs_6_.1) | copy-start | bytes 884740
  0.7 156.4 %copy-start.2 = (f32[48,1536]{1,0:T(8,128)S(1)}, f32[48,1536]{1,0:T(8,128)}, u32[]{:S(2)}) copy-start(f32[48,1536]{1,0:T(8,128)} %refs_9_.1) | copy-start | bytes 884740
  0.7 156.4 %copy-start.3 = (f32[48,3,384]{2,0,1:T(8,128)S(1)}, f32[48,3,384]{2,0,1:T(8,128)}, u32[]{:S(2)}) copy-start(f32[48,3,384]{2,0,1:T(8,128)} %param.30) | copy-start | bytes 663556
  0.7 156.4 %copy-start.5 = (f32[48,1536]{1,0:T(8,128)S(1)}, f32[48,1536]{1,0:T(8,128)}, u32[]{:S(2)}) copy-start(f32[48,1536]{1,0:T(8,128)} %refs_7_.1) | copy-start | bytes 884740
  0.7 156.4 %copy-start.6 = (f32[48,1536]{1,0:T(8,128)S(1)}, f32[48,1536]{1,0:T(8,128)}, u32[]{:S(2)}) copy-start(f32[48,1536]{1,0:T(8,128)} %refs_8_.1) | copy-start | bytes 884740
  0.7 156.4 %copy-start.7 = (f32[48,1536]{1,0:T(8,128)S(1)}, f32[48,1536]{1,0:T(8,128)}, u32[]{:S(2)}) copy-start(f32[48,1536]{1,0:T(8,128)} %refs_10_.1) | copy-start | bytes 884740
  0.7 156.4 %copy-start.8 = (f32[48,1536]{1,0:T(8,128)S(1)}, f32[48,1536]{1,0:T(8,128)}, u32[]{:S(2)}) copy-start(f32[48,1536]{1,0:T(8,128)} %refs_11_.1) | copy-start | bytes 884740
  0.7 156.4 %copy-start.9 = (f32[48,384]{1,0:T(8,128)S(1)}, f32[48,384]{1,0:T(8,128)}, u32[]{:S(2)}) copy-start(f32[48,384]{1,0:T(8,128)} %refs_3_.3) | copy-start | bytes 221188
  0.7 156.4 %copy-start.10 = (f32[48,3,384]{2,0,1:T(8,128)S(1)}, f32[48,3,384]{2,0,1:T(8,128)}, u32[]{:S(2)}) copy-start(f32[48,3,384]{2,0,1:T(8,128)} %param.31) | copy-start | bytes 663556
  0.8 156.4 %copy-start.11 = (f32[48,3,384]{2,0,1:T(8,128)S(1)}, f32[48,3,384]{2,0,1:T(8,128)}, u32[]{:S(2)}) copy-start(f32[48,3,384]{2,0,1:T(8,128)} %param.32) | copy-start | bytes 663556
  0.8 156.4 %copy-start.12 = (f32[48,384]{1,0:T(8,128)S(1)}, f32[48,384]{1,0:T(8,128)}, u32[]{:S(2)}) copy-start(f32[48,384]{1,0:T(8,128)} %refs_4_.3) | copy-start | bytes 221188
  0.8 156.4 %copy-start.13 = (f32[48,384]{1,0:T(8,128)S(1)}, f32[48,384]{1,0:T(8,128)}, u32[]{:S(2)}) copy-start(f32[48,384]{1,0:T(8,128)} %refs_5_.3) | copy-start | bytes 221188
  0.8 156.4 %copy-start.14 = (s32[4,256]{1,0:T(4,128)S(1)}, s32[4,256]{1,0:T(4,128)}, u32[]{:S(2)}) copy-start(s32[4,256]{1,0:T(4,128)} %bvis_ref.3) | copy-start | bytes 12292
  0.8 156.4 %copy-start.15 = (f32[6,48]{1,0:T(8,128)S(1)}, f32[6,48]{1,0:T(8,128)}, u32[]{:S(2)}) copy-start(f32[6,48]{1,0:T(8,128)} %refs_15_.1) | copy-start | bytes 3460
  0.8 156.4 %copy-start.16 = (s32[4,64]{1,0:T(4,128)S(1)}, s32[4,64]{1,0:T(4,128)}, u32[]{:S(2)}) copy-start(s32[4,64]{1,0:T(4,128)} %svis_ref.3) | copy-start | bytes 3076
  0.8 156.4 %copy-start.17 = (f32[6,48]{1,0:T(8,128)S(1)}, f32[6,48]{1,0:T(8,128)}, u32[]{:S(2)}) copy-start(f32[6,48]{1,0:T(8,128)} %refs_16_.1) | copy-start | bytes 3460
  0.8 156.4 %copy-start.18 = (f32[6,48]{1,0:T(8,128)S(1)}, f32[6,48]{1,0:T(8,128)}, u32[]{:S(2)}) copy-start(f32[6,48]{1,0:T(8,128)} %refs_17_.1) | copy-start | bytes 3460
  0.8 156.4 %copy-start.20 = (f32[1,96]{1,0:T(1,128)S(1)}, f32[1,96]{1,0:T(1,128)}, u32[]{:S(2)}) copy-start(f32[1,96]{1,0:T(1,128)} %refs_12_.1) | copy-start | bytes 1156
  0.8 156.4 %copy-start.21 = (f32[1,96]{1,0:T(1,128)S(1)}, f32[1,96]{1,0:T(1,128)}, u32[]{:S(2)}) copy-start(f32[1,96]{1,0:T(1,128)} %refs_13_.1) | copy-start | bytes 1156
  0.9 156.4 %copy-start.22 = (f32[1,96]{1,0:T(1,128)S(1)}, f32[1,96]{1,0:T(1,128)}, u32[]{:S(2)}) copy-start(f32[1,96]{1,0:T(1,128)} %refs_14_.1) | copy-start | bytes 1156
  157.2 1.5 copy-start
  158.8 1.2 copy-start.4
  159.9 0.7 copy-start.19
